TPU v7x, 32 devices: a whole 2x2x4 slice. The times are simulated.
32 devices in a mesh: groups: 2 (over x), seq: 8 (over z, y), head: 2 (over core).
Axes of the slice: x: 2, y: 2, z: 4, core: 2. Of those that a mesh axis runs over, the one named last changes fastest.
Arguments:
- tokens: bfloat16 [4096, 1024], P(('groups', 'seq')), parts along dimension 0, may hold values from -6 to 6
- norm_gain: float32 [1024], replicated, may hold values from 1 to 5
- w_qkv: bfloat16 [3, 1024, 1024], P(None, None, 'head'), may hold values from -0.1875 to 0.1875
- w_out: bfloat16 [1024, 1024], P('head'), may hold values from -0.1875 to 0.1875
- readout_weight: bfloat16 [1024, 128], replicated, may hold values from -0.1875 to 0.1875
- targets: float32 [512, 128], P('groups'), parts along dimension 0, may hold values from -6 to 6
- key_blocks: int32 [32, 4], P('groups'), parts along dimension 0, may hold values from 0 to 15, as said below
- list_len: int32 [32], P('groups'), parts along dimension 0, may hold values from 1 to 4
- voxel_panel: int32 [4096, 1], P('groups'), parts along dimension 0, may hold values from 0 to 255
Outputs:
- grad_tokens: float32 [4096, 1024], P(('groups', 'seq'), 'head'), parts along dimension 0
- loss_mean: float32 [2], P('groups'), parts along dimension 0
There are 2 independent parts, one for each index of `groups`. A program takes and returns all parts, laid end to end along the dimension named above; an argument that names none is the same for every part. Nothing has to cross between parts.
Inputs may be any that keep to these rules, and one draw needn't show every extreme that they name: `key_blocks`: each row holds distinct block numbers; every number k in row b has k div (2) within one of b div (2). `voxel_panel`: every panel 0 to 255 holds at least one token of its district.
All inputs are finite; a program needn't handle non-finite values.
Results may differ from a plain program's by a relative error of at most 0.035.
The roundings to bfloat16 on the way count: a program that leaves them out, or rounds other values in their place, can miss the bound.
Values may be sent and summed in bfloat16 or wider, within the bound.
No kernel may reach another device: no remote copies, remote signals or barrier semaphores. Data moves between devices by JAX's collectives and lax.ppermute only.
A program may use at most 128 MiB of HBM per device.

v0:
```python
import math

import jax
import jax.numpy as jnp
from jax import lax
from jax.sharding import PartitionSpec as P

HD = 64
BLK = 128
LIST = 4


def softmax_parts(queries, key_rows, live_keys, score_scale):
    scores = (
        jnp.einsum("...qd,...kd->...qk", queries, key_rows, preferred_element_type=jnp.float32)
        * score_scale
    )
    scores = jnp.where(live_keys, scores, -1e30)
    top_score = jnp.max(scores, axis=-1, keepdims=True)
    expo = jnp.where(live_keys, jnp.exp(scores - top_score), jnp.float32(0.0))
    row_total = jnp.sum(expo, axis=-1, keepdims=True)
    return (expo / row_total, top_score, row_total)


def attend_back(
    queries, key_rows, value_matrix, weight, attended_rows, output_gradient, score_scale
):
    grad_weight = jnp.einsum(
        "...qd,...kd->...qk", output_gradient, value_matrix, preferred_element_type=jnp.float32
    )
    row_delta = jnp.sum(
        output_gradient.astype(jnp.float32) * attended_rows.astype(jnp.float32),
        axis=-1,
        keepdims=True,
    )
    grad_score = (weight * (grad_weight - row_delta) * score_scale).astype(jnp.bfloat16)
    grad_query = jnp.einsum(
        "...qk,...kd->...qd", grad_score, key_rows, preferred_element_type=jnp.float32
    ).astype(jnp.bfloat16)
    grad_key = jnp.einsum(
        "...qk,...qd->...kd", grad_score, queries, preferred_element_type=jnp.float32
    )
    second_weight = weight.astype(jnp.bfloat16)
    grad_value = jnp.einsum(
        "...qk,...qd->...kd", second_weight, output_gradient, preferred_element_type=jnp.float32
    )
    return (grad_query, grad_key, grad_value)


def pool_panels(read_rows, row_ids, counts, targets, all_tokens):
    partial_sums = jax.ops.segment_sum(read_rows, row_ids, num_segments=targets.shape[0])
    panel_sums = lax.psum(partial_sums, ("seq", "head"))
    residual = panel_sums / counts[:, None] - targets
    loss_mean = (
        0.5 * jnp.sum(counts[:, None] * residual * residual) / (all_tokens * targets.shape[1])
    )
    return (residual, loss_mean)


def local(
    tokens, norm_gain, w_qkv, w_out, readout_weight, targets, key_blocks, list_len, voxel_panel
):
    score_scale = 1.0 / math.sqrt(HD)
    tok_rows = tokens.shape[0]
    core_heads = w_qkv.shape[2] // HD
    seq_count = lax.axis_size("seq")
    inputs = tokens.astype(jnp.float32)
    root_mean = jnp.sqrt(jnp.mean(inputs * inputs, axis=-1, keepdims=True) + 1e-05)
    normed = (inputs * norm_gain / root_mean).astype(jnp.bfloat16)
    projected_rows = jnp.einsum(
        "td,cdf->ctf", normed, w_qkv, preferred_element_type=jnp.float32
    ).astype(jnp.bfloat16)
    parts_heads = projected_rows.reshape(3, tok_rows, core_heads, HD)
    readout_mix = jnp.dot(w_out, readout_weight, preferred_element_type=jnp.float32).astype(
        jnp.bfloat16
    )
    panel_ids = voxel_panel[:, 0]
    all_tokens = panel_ids.shape[0]
    counts = jax.ops.segment_sum(
        jnp.ones((all_tokens,), jnp.float32), panel_ids, num_segments=targets.shape[0]
    )
    live_slots = jnp.arange(LIST)[None, :] < list_len[:, None]
    key_values = jnp.concatenate([parts_heads[1], parts_heads[2]], axis=-1)
    seq_index = lax.axis_index("seq")
    copies = seq_count // core_heads
    sub_rows = tok_rows // copies
    my_head = seq_index % core_heads
    my_part = seq_index // core_heads
    query_send = (
        parts_heads[0]
        .reshape(copies, sub_rows, core_heads, HD)
        .transpose(0, 2, 1, 3)
        .reshape(seq_count, sub_rows, HD)
    )
    head_major = key_values.transpose(1, 0, 2)
    pair_send = jnp.broadcast_to(head_major[None], (copies, core_heads, tok_rows, 2 * HD)).reshape(
        seq_count, tok_rows, 2 * HD
    )
    query_recv, pair_recv = (
        lax.all_to_all(query_send, "seq", split_axis=0, concat_axis=0, tiled=True),
        lax.all_to_all(pair_send, "seq", split_axis=0, concat_axis=0, tiled=True),
    )
    block_count = all_tokens // BLK
    pair_blocks = pair_recv.reshape(block_count, BLK, 2 * HD)
    group_rows = min(sub_rows, BLK)
    per_sub = sub_rows // group_rows
    group_count = seq_count * per_sub
    group_index = jnp.arange(group_count, dtype=jnp.int32)
    row_start = (
        group_index // per_sub * tok_rows + my_part * sub_rows + group_index % per_sub * group_rows
    )
    group_block = row_start // BLK
    key_lists = key_blocks[group_block]
    live_keys = jnp.repeat(live_slots[group_block], BLK, axis=1)[:, None, :]
    gathered = pair_blocks[key_lists].reshape(group_count, LIST * BLK, 2 * HD)
    key_rows = gathered[..., :HD]
    value_matrix = gathered[..., HD:]
    queries = query_recv.reshape(group_count, group_rows, HD)
    weight, top_score, row_total = softmax_parts(queries, key_rows, live_keys, score_scale)
    second_weight = weight.astype(jnp.bfloat16)
    attended_rows = jnp.einsum(
        "gqk,gkd->gqd", second_weight, value_matrix, preferred_element_type=jnp.float32
    ).astype(jnp.bfloat16)
    head_mix = lax.dynamic_slice_in_dim(readout_mix, my_head * HD, HD, 0)
    positions = (row_start[:, None] + jnp.arange(group_rows, dtype=jnp.int32)[None, :]).reshape(-1)
    row_ids = panel_ids[positions]
    read_rows = jnp.dot(
        attended_rows.reshape(group_count * group_rows, HD),
        head_mix,
        preferred_element_type=jnp.float32,
    )
    residual, loss_mean = pool_panels(read_rows, row_ids, counts, targets, all_tokens)
    grad_read = residual[row_ids]
    output_gradient = jnp.dot(
        grad_read, head_mix.astype(jnp.float32).T, precision=lax.Precision.HIGHEST
    ).astype(jnp.bfloat16)
    output_gradient = output_gradient.reshape(group_count, group_rows, HD)
    grad_query, grad_key, grad_value = attend_back(
        queries, key_rows, value_matrix, weight, attended_rows, output_gradient, score_scale
    )
    pair_grads = jnp.concatenate([grad_key, grad_value], axis=-1).reshape(
        group_count * LIST, BLK, 2 * HD
    )
    pair_total = (
        jnp.zeros((block_count, BLK, 2 * HD), jnp.float32).at[key_lists.reshape(-1)].add(pair_grads)
    )
    query_back, pair_back = (
        lax.all_to_all(
            grad_query.astype(jnp.float32).reshape(seq_count, sub_rows, HD).astype(jnp.bfloat16),
            "seq",
            split_axis=0,
            concat_axis=0,
            tiled=True,
        ).astype(jnp.float32),
        lax.all_to_all(
            pair_total.reshape(seq_count, tok_rows, 2 * HD).astype(jnp.bfloat16),
            "seq",
            split_axis=0,
            concat_axis=0,
            tiled=True,
        ).astype(jnp.float32),
    )
    grad_query_tok = (
        query_back.reshape(copies, core_heads, sub_rows, HD)
        .transpose(0, 2, 1, 3)
        .reshape(tok_rows, core_heads * HD)
        .astype(jnp.bfloat16)
    )
    owned_gradients = (
        jnp.sum(pair_back.reshape(copies, core_heads, tok_rows, 2 * HD), axis=0)
        .transpose(1, 0, 2)
        .astype(jnp.bfloat16)
    )
    grad_key_tok = owned_gradients[..., :HD].reshape(tok_rows, core_heads * HD)
    grad_value_tok = owned_gradients[..., HD:].reshape(tok_rows, core_heads * HD)
    grad_proj = jnp.stack([grad_query_tok, grad_key_tok, grad_value_tok])
    normed_part = jnp.einsum("ctf,cdf->td", grad_proj, w_qkv, preferred_element_type=jnp.float32)
    grad_normed = lax.psum(normed_part.astype(jnp.bfloat16), "head").astype(jnp.float32)
    scaled = norm_gain * grad_normed
    gradient = scaled / root_mean - inputs * jnp.sum(inputs * scaled, axis=-1, keepdims=True) / (
        inputs.shape[1] * root_mean**3
    )
    half_width = gradient.shape[1] // lax.axis_size("head")
    gradient_local = lax.dynamic_slice_in_dim(
        gradient, lax.axis_index("head") * half_width, half_width, 1
    )
    return (gradient_local, loss_mean.reshape(1))


def solution(mesh):
    return jax.shard_map(
        local,
        mesh=mesh,
        in_specs=(
            P(("groups", "seq"), None),
            P(),
            P(None, None, "head"),
            P("head", None),
            P(),
            P("groups", None),
            P("groups", None),
            P("groups"),
            P("groups", None),
        ),
        out_specs=(P(("groups", "seq"), "head"), P("groups")),
        check_vma=False,
    )
```

profile of v0, /device:TPU:0, one launch (start us, length us, event | category | flops | bytes accessed | tf_op | source)
XLA Modules:
  0.0 292.8 jit_solution(5665452328187599604)
XLA Ops:
  9.6 2.1 fusion.14
  13.4 7.3 %all-to-all-start = ((bf16[8,256,64]{1,2,0:T(8,128)(2,1)}), bf16[8,256,64]{1,2,0:T(8,128)(2,1)S(1)}, u32[]{:S(2)}, u32[]{:S(2)}) async-start(bf16[8,256,64]{1,2,0:T(8,128)(2,1)} %bitcast.87), calls=%async_computation | async-start | bytes 524288 | tf_op jit(solution)/shard_map/all_to_all | solution.py:100
  27.3 11.8 %gather_fusion.3 = s32[2048]{0:T(1024)S(1)} fusion(s32[2048]{0:T(1024)S(1)} %bitcast.76, s32[2048]{0:T(1024)S(1)} %broadcast_clamp_fusion.1), kind=kCustom, calls=%fused_computation.3 | custom fusion | bytes 24576 | tf_op jit(solution)/shard_map/gather | solution.py:126
  39.1 1.9 maximum_bitcast_fusion
  41.0 6.0 %all-to-all-start.1 = ((bf16[8,256,128]{1,2,0:T(8,128)(2,1)}), bf16[8,256,128]{1,2,0:T(8,128)(2,1)}, u32[]{:S(2)}, u32[]{:S(2)}) async-start(bf16[8,256,128]{1,2,0:T(8,128)(2,1)} %maximum_bitcast_fusion), calls=%async_computation.1 | async-start | bytes 1048576 | tf_op jit(solution)/shard_map/all_to_all | solution.py:101
  47.7 2.3 fusion.68
  51.9 9.2 %all-to-all-done.1 = bf16[8,256,128]{1,2,0:T(8,128)(2,1)} async-done(((bf16[8,256,128]{1,2,0:T(8,128)(2,1)}), bf16[8,256,128]{1,2,0:T(8,128)(2,1)}, u32[]{:S(2)}, u32[]{:S(2)}) %all-to-all-start.1) | async-done | bytes 524320 | tf_op jit(solution)/shard_map/all_to_all | solution.py:101
  61.1 2.0 copy.42
  63.1 3.2 %gather_fusion.2 = bf16[64,128,128]{2,1,0:T(8,128)(2,1)} fusion(bf16[16,128,128]{2,1,0:T(8,128)(2,1)} %bitcast.83, s32[1024]{0:T(1024)S(1)} %pad_clamp_fusion), kind=kCustom, calls=%fused_computation.2 | custom fusion | bytes 4194560 | tf_op jit(solution)/shard_map/gather | solution.py:115
  66.3 2.4 fusion.8
  68.7 3.5 %fusion.67 = (f32[16,128]{1,0:T(8,128)S(1)}, f32[16,128,512]{2,1,0:T(8,128)S(1)}) fusion(f32[16,128,512]{2,1,0:T(8,128)S(1)} %fusion.8, pred[16,512]{1,0:T(8,128)(4,1)S(1)} %bitcast.95), kind=kOutput, calls=%fused_computation.117 | output fusion | flops 7340543 | bytes 8404992 | tf_op jit(solution)/shard_map/sub | solution.py:20
  77.8 2.1 fusion.33
  80.0 12.4 %scatter_custom_fusion = f32[256,128]{1,0:T(8,128)} fusion(s32[2048]{0:T(1024)} %copy-done.11, f32[2048,128]{1,0:T(8,128)} %fusion.33, f32[]{:T(128)} %constant.105.clone.1), kind=kCustom, calls=%fused_computation.66 | custom fusion | flops 262144 | bytes 131584 | tf_op jit(solution)/shard_map/scatter-add | solution.py:51
  92.9 15.2 %scatter_custom_fusion.1 = f32[256]{0:T(256)} fusion(s32[2048]{0:T(1024)S(1)} %bitcast.77, f32[2048]{0:T(1024)S(1)} %broadcast.321, f32[]{:T(128)} %constant.105.clone.1), kind=kCustom, calls=%fused_computation.110 | custom fusion | flops 2048 | bytes 1028 | tf_op jit(solution)/shard_map/scatter-add | solution.py:79
  108.2 70.4 %all-reduce.3.cloned.1.call-done = f32[256,128]{1,0:T(8,128)} async-done(((f32[256,128]{1,0:T(8,128)}), f32[256,128]{1,0:T(8,128)}) %all-reduce.3.cloned.1.call-update) | async-done | bytes 131088 | tf_op jit(solution)/shard_map/psum | solution.py:52
  180.2 7.6 %gather_fusion.4 = f32[2048,128]{1,0:T(8,128)} fusion(f32[256,128]{1,0:T(8,128)S(1)} %get-tuple-element.3, s32[2048]{0:T(1024)S(1)} %copy-done.10), kind=kCustom, calls=%fused_computation.4 | custom fusion | bytes 2105344 | tf_op jit(solution)/shard_map/gather | solution.py:133
  187.9 2.0 fusion.21
  191.0 4.6 %multiply_convert_fusion = bf16[16,128,512]{2,1,0:T(8,128)(2,1)S(1)} fusion(f32[16,128]{1,0:T(8,128)S(1)} %multiply_reduce_fusion.2, bf16[16,512,128]{2,1,0:T(8,128)(2,1)} %bitcast.79, f32[16,128,512]{2,1,0:T(8,128)} %copy-done.6, f32[16,128]{1,0:T(8,128)S(1)} %copy-done.13, bf16[8,16,8,128]{3,2,1,0:T(8,128)(2,1)S(1)} %fusion.21), kind=kOutput, calls=%fused_computation.10 | convolution fusion | flops 139460608 | bytes 8667136 | tf_op jit(solution)/shard_map/...qd,...kd->...qk/dot_general | solution.py:28
  202.8 6.2 %all-to-all-start.2 = ((bf16[8,256,64]{1,2,0:T(8,128)(2,1)}), bf16[8,256,64]{1,2,0:T(8,128)(2,1)}, u32[]{:S(2)}, u32[]{:S(2)}) async-start(bf16[8,256,64]{1,2,0:T(8,128)(2,1)} %copy.53), calls=%async_computation.2 | async-start | bytes 524288 | tf_op jit(solution)/shard_map/all_to_all | solution.py:148
  209.0 2.2 fusion.36
  211.3 2.4 pad_maximum_fusion
  213.7 5.3 %copy.56 = f32[16,512,128]{2,1,0:T(8,128)} copy(f32[16,512,128]{1,2,0:T(8,128)} %pad_maximum_fusion) | data formatting | bytes 8388608 | tf_op jit(solution)/shard_map/concatenate | solution.py:141
  220.1 13.2 %scatter_fusion = f32[16,128,128]{2,1,0:T(8,128)} fusion(f32[16,128,128]{2,1,0:T(8,128)} %broadcast_in_dim.70, s32[64]{0:T(128)S(1)} %copy-done.20, f32[64,128,128]{2,1,0:T(8,128)} %bitcast.82), kind=kCustom, calls=%fused_computation.7 | custom fusion | flops 1048576 | bytes 12583168 | tf_op jit(solution)/shard_map/scatter-add | solution.py:145
  233.3 2.1 convert_element_type.94
  235.4 6.0 %all-to-all-start.3 = ((bf16[8,256,128]{2,1,0:T(8,128)(2,1)}), bf16[8,256,128]{2,1,0:T(8,128)(2,1)}, u32[]{:S(2)}, u32[]{:S(2)}) async-start(bf16[8,256,128]{2,1,0:T(8,128)(2,1)} %bitcast.84), calls=%async_computation.3 | async-start | bytes 1048576 | tf_op jit(solution)/shard_map/all_to_all | solution.py:155
  241.5 1.8 copy.59
  243.3 10.7 %all-to-all-done.3 = bf16[8,256,128]{2,1,0:T(8,128)(2,1)} async-done(((bf16[8,256,128]{2,1,0:T(8,128)(2,1)}), bf16[8,256,128]{2,1,0:T(8,128)(2,1)}, u32[]{:S(2)}, u32[]{:S(2)}) %all-to-all-start.3) | async-done | bytes 524320 | tf_op jit(solution)/shard_map/all_to_all | solution.py:155
  254.0 2.3 fusion.66
  260.5 2.9 fusion.13
  263.4 2.1 convert_element_type.78
  266.1 15.2 %all-reduce.5.cloned.1.call-done = bf16[256,1024]{1,0:T(8,128)(2,1)} async-done(((bf16[256,1024]{1,0:T(8,128)(2,1)}), bf16[256,1024]{1,0:T(8,128)(2,1)}) %all-reduce.5.cloned.1.call-update) | async-done | bytes 524304 | tf_op jit(solution)/shard_map/psum | solution.py:178
  282.8 2.0 fusion.29
  (97 shorter events, 36.1 us)
Async XLA Ops:
  7.2 2.5 copy-start
  9.1 0.5 copy-start.17
  9.6 11.1 %copy-start.19 = (s32[16,4]{0,1:T(4,128)S(1)}, s32[16,4]{0,1:T(4,128)}, u32[]{:S(2)}) copy-start(s32[16,4]{0,1:T(4,128)} %param.15) | copy-start | bytes 772
  11.7 14.1 %copy-start.21 = (s32[16]{0:T(128)S(1)}, s32[16]{0:T(128)}, u32[]{:S(2)}) copy-start(s32[16]{0:T(128)} %param.16) | copy-start | bytes 196
  11.8 15.6 %copy-start.1 = (s32[2048,1]{0,1:T(1,128)S(1)}, s32[2048,1]{0,1:T(1,128)}, u32[]{:S(2)}) copy-start(s32[2048,1]{0,1:T(1,128)} %param.17) | copy-start | bytes 24580
  13.4 27.6 %all-to-all-start = ((bf16[8,256,64]{1,2,0:T(8,128)(2,1)}), bf16[8,256,64]{1,2,0:T(8,128)(2,1)S(1)}, u32[]{:S(2)}, u32[]{:S(2)}) async-start(bf16[8,256,64]{1,2,0:T(8,128)(2,1)} %bitcast.87), calls=%async_computation | async-start | bytes 524288 | tf_op jit(solution)/shard_map/all_to_all | solution.py:100
  39.1 10.9 %copy-start.11 = (s32[2048]{0:T(1024)}, s32[2048]{0:T(1024)S(1)}, u32[]{:S(2)}) copy-start(s32[2048]{0:T(1024)S(1)} %gather_fusion.3) | copy-start | bytes 24580
  41.0 20.1 %all-to-all-start.1 = ((bf16[8,256,128]{1,2,0:T(8,128)(2,1)}), bf16[8,256,128]{1,2,0:T(8,128)(2,1)}, u32[]{:S(2)}, u32[]{:S(2)}) async-start(bf16[8,256,128]{1,2,0:T(8,128)(2,1)} %maximum_bitcast_fusion), calls=%async_computation.1 | async-start | bytes 1048576 | tf_op jit(solution)/shard_map/all_to_all | solution.py:101
  47.0 131.5 %all-reduce.3.cloned.1.call-start = ((), (), s32[]{:S(2)}) async-start(), calls=%async_computation.4 | async-start | bytes 262144 | tf_op jit(solution)/shard_map/psum | solution.py:52
  66.3 2.4 copy-start.14
  72.2 2.1 copy-start.6
  72.2 2.1 copy-start.12
  72.2 3.1 %copy-start.2 = (bf16[64,128,128]{2,1,0:T(8,128)(2,1)S(1)}, bf16[64,128,128]{2,1,0:T(8,128)(2,1)}, u32[]{:S(2)}) copy-start(bf16[64,128,128]{2,1,0:T(8,128)(2,1)} %gather_fusion.2) | copy-start | bytes 6291460
  75.3 1.8 copy-start.4
  75.3 17.1 %copy-start.22 = (s32[64,1]{0,1:T(1,128)S(1)}, s32[64,1]{0,1:T(1,128)}, u32[]{:S(2)}) copy-start(s32[64,1]{0,1:T(1,128)} %reshape.289) | copy-start | bytes 772
  75.3 104.9 %copy-start.10 = (s32[2048]{0:T(1024)S(1)}, s32[2048]{0:T(1024)}, u32[]{:S(2)}) copy-start(s32[2048]{0:T(1024)} %broadcast_clamp_fusion) | copy-start | bytes 24580
  77.1 0.7 copy-start.7
  180.2 10.8 %copy-start.13 = (f32[16,128]{1,0:T(8,128)S(1)}, f32[16,128]{1,0:T(8,128)}, u32[]{:S(2)}) copy-start(f32[16,128]{1,0:T(8,128)} %copy-done.12) | copy-start | bytes 24580
  189.8 5.8 %copy-start.8 = (bf16[8,16,8,128]{3,2,1,0:T(8,128)(2,1)}, bf16[8,16,8,128]{3,2,1,0:T(8,128)(2,1)S(1)}, u32[]{:S(2)}) copy-start(bf16[8,16,8,128]{3,2,1,0:T(8,128)(2,1)S(1)} %fusion.21) | copy-start | bytes 786436
  195.6 2.0 copy-start.3
  197.6 11.4 %copy-start.9 = (bf16[8,16,8,128]{3,2,1,0:T(8,128)(2,1)S(1)}, bf16[8,16,8,128]{3,2,1,0:T(8,128)(2,1)}, u32[]{:S(2)}) copy-start(bf16[8,16,8,128]{3,2,1,0:T(8,128)(2,1)} %copy-done.8) | copy-start | bytes 786436
  202.8 32.6 %all-to-all-start.2 = ((bf16[8,256,64]{1,2,0:T(8,128)(2,1)}), bf16[8,256,64]{1,2,0:T(8,128)(2,1)}, u32[]{:S(2)}, u32[]{:S(2)}) async-start(bf16[8,256,64]{1,2,0:T(8,128)(2,1)} %copy.53), calls=%async_computation.2 | async-start | bytes 524288 | tf_op jit(solution)/shard_map/all_to_all | solution.py:148
  209.0 2.2 copy-start.5
  213.7 6.4 %copy-start.20 = (s32[64]{0:T(128)S(1)}, s32[64]{0:T(128)}, u32[]{:S(2)}) copy-start(s32[64]{0:T(128)} %fusion.59) | copy-start | bytes 772
  235.4 18.5 %all-to-all-start.3 = ((bf16[8,256,128]{2,1,0:T(8,128)(2,1)}), bf16[8,256,128]{2,1,0:T(8,128)(2,1)}, u32[]{:S(2)}, u32[]{:S(2)}) async-start(bf16[8,256,128]{2,1,0:T(8,128)(2,1)} %bitcast.84), calls=%async_computation.3 | async-start | bytes 1048576 | tf_op jit(solution)/shard_map/all_to_all | solution.py:155
  241.4 39.9 %all-reduce.5.cloned.1.call-start = ((), (), s32[]{:S(2)}) async-start(), calls=%async_computation.5 | async-start | bytes 1048576 | tf_op jit(solution)/shard_map/psum | solution.py:178
  260.5 20.9 %copy-start.15 = (f32[1024]{0:T(1024)S(1)}, f32[1024]{0:T(1024)}, u32[]{:S(2)}) copy-start(f32[1024]{0:T(1024)} %param.10) | copy-start | bytes 12292
  263.4 19.4 %copy-start.16 = (f32[256]{0:T(256)S(1)}, f32[256]{0:T(256)}, u32[]{:S(2)}) copy-start(f32[256]{0:T(256)} %get-tuple-element.11) | copy-start | bytes 3076
  263.4 19.4 %copy-start.18 = (f32[256]{0:T(256)S(1)}, f32[256]{0:T(256)}, u32[]{:S(2)}) copy-start(f32[256]{0:T(256)} %copy-done.17) | copy-start | bytes 3076
Sparse Core Ops, SparseCore 0:
  92.5 85.9 all-reduce.2
  263.5 17.7 all-reduce.4
where the time goes:
time: 294 us; the launch traced here: 293 us
  waiting for transfers between devices  106 us (36%)
  other arithmetic  62.8 us (21%)
  local copies, waits for them, and re-layouts  57.9 us (20%)
  starting transfers between devices  25.6 us (9%)
  matrix products  25 us (9%)
  between operations  16.1 us (5%)
    psum x1, waiting for transfers between devices, pool_panels(): panel_sums = lax.psum(partial_sums, ('seq', 'head'))  70.4 us
    psum x1, waiting for transfers between devices, local(): lax.psum(normed_part.astype(jnp.bfloat16), 'head').astype(jnp.float32)  15.2 us
    scatter-add x1, other arithmetic, local(): jax.ops.segment_sum(jnp.ones((all_tokens,), jnp.float32), panel_ids, num_...  15.2 us
    scatter-add x1, other arithmetic, local(): jnp.zeros((block_count, BLK, 2 * HD), jnp.float32).at[key_lists.reshape(-1)]  13.2 us
    scatter-add x1, other arithmetic, pool_panels(): jax.ops.segment_sum(read_rows, row_ids, num_segments=targets.shape[0])  12.4 us
    gather x1, local copies, waits for them, and re-layouts, local(): row_ids = panel_ids[positions]  11.8 us
    all_to_all x1, waiting for transfers between devices, local(): lax.all_to_all(pair_total.reshape(seq_count, tok_rows, 2 * HD).astype(jnp...  10.7 us
    all_to_all x1, waiting for transfers between devices, local(): lax.all_to_all(pair_send, 'seq', split_axis=0, concat_axis=0, tiled=True)  9.19 us
  transfers between devices with their start and end apart: 6, of which 4 were waited for; matrix products, arithmetic and copies ran while one was open for 24% of the time, Pallas kernels for 0%

commit v1 on v0

v1 whole, which is shorter than its diff:
```python
import functools
import math

import jax
import jax.numpy as jnp
import numpy as np
from jax import lax
from jax.experimental import pallas as pl
from jax.experimental.pallas import tpu as pltpu
from jax.sharding import PartitionSpec as P

HD = 64
BLK = 128
LIST = 4
PAIR = 2 * HD
F32 = jnp.float32
BF16 = jnp.bfloat16
DEAD = 1e30
QUERY_STEP = np.array([0, 0, 1, 1, -1, -1], np.int32)
KEY_STEP = np.array(
    [[0, 0, 1, 1, -1, -1]] * 2 + [[0, 0, 1, 1, 2, 2]] * 2 + [[0, 0, -1, -1, -2, -2]] * 2, np.int32
)
VMEM_LIMIT = 40 * 1024 * 1024

NN = (((1,), (0,)), ((), ()))
NT = (((1,), (1,)), ((), ()))
TN = (((0,), (0,)), ((), ()))


def dot(a, b, dims, precision=None):
    return lax.dot_general(a, b, dims, precision=precision, preferred_element_type=F32)


def params():
    return pltpu.CompilerParams(
        vmem_limit_bytes=VMEM_LIMIT, dimension_semantics=("arbitrary",)
    )


def project_kernel(first, x_ref, gain_ref, w_ref, out_ref, normed):
    part = pl.program_id(0)

    @pl.when(part == 0)
    def _():
        inputs = x_ref[...].astype(F32)
        root_mean = jnp.sqrt(jnp.mean(inputs * inputs, axis=-1, keepdims=True) + 1e-05)
        normed[...] = (inputs * gain_ref[...] / root_mean).astype(BF16)

    rows = dot(normed[...], w_ref[0], NN).astype(BF16)
    scale = jnp.where(part + first == 0, 1.0 / math.sqrt(HD), 1.0)
    out_ref[0] = (rows.astype(F32) * scale).astype(BF16)


def project(tokens, gain, w_qkv, first):
    rows, width = tokens.shape
    parts, cols = 3 - first, w_qkv.shape[2]
    return pl.pallas_call(
        functools.partial(project_kernel, first),
        grid=(parts,),
        in_specs=[
            pl.BlockSpec((rows, width), lambda c: (0, 0)),
            pl.BlockSpec((1, width), lambda c: (0, 0)),
            pl.BlockSpec((1, width, cols), lambda c: (c + first, 0, 0)),
        ],
        out_specs=pl.BlockSpec((1, rows, cols), lambda c: (c, 0, 0)),
        out_shape=jax.ShapeDtypeStruct((parts, rows, cols), BF16),
        scratch_shapes=[pltpu.VMEM((rows, width), BF16)],
        compiler_params=params(),
        cost_estimate=pl.CostEstimate(
            flops=2 * rows * width * cols * parts,
            bytes_accessed=parts * width * cols * 2 + rows * width * 2,
            transcendentals=rows,
        ),
        name="project",
    )(tokens, gain, w_qkv)


def two_heads(tile):
    lane = lax.broadcasted_iota(jnp.int32, tile.shape, 1)
    zero = jnp.zeros_like(tile)
    return jnp.concatenate(
        [jnp.where(lane < HD, tile, zero), jnp.where(lane >= HD, tile, zero)], axis=0
    )


def fold_heads(pair_t):
    return jnp.concatenate([pair_t[:HD, :BLK], pair_t[HD:, BLK:]], axis=0)


def attend(bias_ref, row, key_rows, values_t, query_tile):
    scores = dot(key_rows, two_heads(query_tile), NT)
    blocks = [scores[k * BLK : (k + 1) * BLK] for k in range(6)]
    tops = [
        jnp.max(blocks[k], axis=0, keepdims=True) - bias_ref[row, k] for k in range(6)
    ]
    top = functools.reduce(jnp.maximum, tops)
    expo = [jnp.exp(blocks[k] - (top + bias_ref[row, k])) for k in range(6)]
    total = functools.reduce(jnp.add, [jnp.sum(e, axis=0, keepdims=True) for e in expo])
    inverse = 1.0 / total
    weight = jnp.concatenate([(e * inverse).astype(BF16) for e in expo], axis=0)
    attended_t = fold_heads(dot(values_t, weight, NN)).astype(BF16)
    return weight, attended_t


def own_kernel(
    pairs, bias_ref, own_ref, near_ref, far_ref, mix_ref, weight_ref, att_ref, keep_ref, send_ref, read
):
    pair = pl.program_id(0)
    keys = jnp.concatenate([own_ref[1], near_ref[1], far_ref[1]], axis=0)
    values_t = jnp.concatenate([own_ref[2], near_ref[2], far_ref[2]], axis=0).T

    @pl.when(pair == 0)
    def _():
        read[...] = jnp.zeros_like(read)

    for b in range(2):
        rows = slice(b * BLK, (b + 1) * BLK)
        weight, attended_t = attend(bias_ref, b, keys, values_t, own_ref[0, rows, :])
        weight_ref[0, b] = weight
        att_ref[0, b] = attended_t
        read[rows, :] += dot(attended_t, mix_ref[...], TN)

    @pl.when(pair == pairs - 1)
    def _():
        half = read.shape[1] // 2
        keep_ref[...] = read[:, :half]
        send_ref[...] = read[:, half:]


def side_kernel(bias_ref, own_ref, a1_ref, b1_ref, a2_ref, b2_ref, weight_ref, att_ref):
    own_rows = own_ref.shape[1]
    for side, (one, two) in enumerate(((a1_ref, a2_ref), (b1_ref, b2_ref))):
        keys = jnp.concatenate([own_ref[1], one[1], two[0]], axis=0)
        values_t = jnp.concatenate([own_ref[2], one[2], two[1]], axis=0).T
        for b in range(2):
            rows = slice(b * BLK, (b + 1) * BLK)
            at = 2 * side + b
            weight, attended_t = attend(bias_ref, 2 + at, keys, values_t, one[0, rows, :])
            weight_ref[0, at] = weight[:own_rows]
            att_ref[0, at] = attended_t


def back_kernel(
    pairs,
    core_ref,
    resid_a_ref,
    resid_b_ref,
    hot_ref,
    mix_ref,
    own_ref,
    a1_ref,
    b1_ref,
    own_weight_ref,
    own_att_ref,
    side_weight_ref,
    side_att_ref,
    w_ref,
    tokens_ref,
    gain_ref,
    keep_ref,
    send_ref,
    sum_ref,
    residual,
    total,
):
    pair = pl.program_id(0)

    @pl.when(pair == 0)
    def _():
        residual[...] = jnp.concatenate([resid_a_ref[...], resid_b_ref[...]], axis=1)
        total[...] = jnp.zeros_like(total)

    panel_grad = dot(
        residual[...], mix_ref[...].astype(F32), NT, lax.Precision.HIGHEST
    ).astype(BF16)
    out_grad = dot(hot_ref[...], panel_grad, NN)
    keys = jnp.concatenate([own_ref[1], a1_ref[1], b1_ref[1]], axis=0)
    values = jnp.concatenate([own_ref[2], a1_ref[2], b1_ref[2]], axis=0)
    keys_t = keys.T
    own_rows = own_ref.shape[1]
    grad_key = jnp.zeros((own_rows, PAIR), F32)
    grad_value = jnp.zeros((own_rows, PAIR), F32)
    grad_query = []
    for i in range(6):
        source = (own_ref, a1_ref, b1_ref)[i // 2]
        rows = slice((i % 2) * BLK, (i % 2 + 1) * BLK)
        grad_tile = out_grad[i * BLK : (i + 1) * BLK]
        attended_t = own_att_ref[0, i] if i < 2 else side_att_ref[0, i - 2]
        product = grad_tile.T * attended_t.astype(F32)
        delta = jnp.concatenate(
            [
                jnp.sum(product[:HD], axis=0, keepdims=True),
                jnp.sum(product[HD:], axis=0, keepdims=True),
            ],
            axis=1,
        )
        grad_pair = two_heads(grad_tile.astype(BF16))
        query_pair = two_heads(source[0, rows, :])
        if i < 2:
            weight = own_weight_ref[0, i]
            grad_weight = dot(values, grad_pair, NT)
        else:
            weight = side_weight_ref[0, i - 2]
            grad_weight = dot(values[:own_rows], grad_pair, NT)
        grad_score = (weight.astype(F32) * (grad_weight - delta)).astype(BF16)
        if i < 2:
            grad_query_t = fold_heads(dot(keys_t, grad_score, NN)) * (1.0 / math.sqrt(HD))
            grad_query.append(grad_query_t.T.astype(BF16))
        grad_key += dot(grad_score[:own_rows], query_pair, NN)
        grad_value += dot(weight[:own_rows], grad_pair, NN)
    grad_proj = (
        jnp.concatenate(grad_query, axis=0),
        grad_key.astype(BF16),
        grad_value.astype(BF16),
    )
    half = total.shape[2]
    for h in range(2):
        part = total[h]
        for c in range(3):
            part += dot(grad_proj[c], w_ref[c, h * half : (h + 1) * half, :], NT)
        total[h] = part

    @pl.when(pair == pairs - 1)
    def _():
        row_sum = jnp.zeros((own_rows, 1), F32)
        for h in range(2):
            cols = slice(h * half, (h + 1) * half)
            row_sum += jnp.sum(
                tokens_ref[:, cols].astype(F32) * gain_ref[:, cols] * total[h],
                axis=-1,
                keepdims=True,
            )
        core = core_ref[0]
        keep_ref[...] = total[core]
        high = row_sum.astype(BF16)
        low = (row_sum - high.astype(F32)).astype(BF16)
        send_ref[:, :half] = total[1 - core].astype(BF16)
        lane = lax.broadcasted_iota(jnp.int32, (own_rows, BLK), 1)
        send_ref[:, half:] = jnp.where(lane < HD, high.astype(F32), low.astype(F32)).astype(BF16)
        sum_ref[...] = jnp.broadcast_to(row_sum, sum_ref.shape)


def pair_spec(parts, rows):
    return pl.BlockSpec((parts, rows, PAIR), lambda p: (0, 0, p))


def whole_spec(shape):
    return pl.BlockSpec(shape, lambda p: (0,) * len(shape))


def lead_spec(shape):
    return pl.BlockSpec((1,) + shape, lambda p: (p,) + (0,) * len(shape))


SMEM_SPEC = pl.BlockSpec(memory_space=pltpu.SMEM)


def local(
    tokens, norm_gain, w_qkv, w_out, readout_weight, targets, key_blocks, list_len, voxel_panel
):
    tok_rows, width = tokens.shape
    cols = w_qkv.shape[2]
    pairs = cols // PAIR
    panels, readout = targets.shape
    half_read = readout // 2
    half_width = width // 2
    seq_count = lax.axis_size("seq")
    seq_index = lax.axis_index("seq")
    core = lax.axis_index("head")
    step = 2 * core - 1
    all_tokens = voxel_panel.shape[0]
    block_count = all_tokens // BLK
    per = tok_rows // BLK
    core_swap = [(0, 1), (1, 0)]

    def shifted(far):
        return [
            (2 * s, 2 * (s + far)) for s in range(seq_count - far)
        ] + [(2 * (s + far) + 1, 2 * s + 1) for s in range(seq_count - far)]

    a1_tokens = lax.ppermute(tokens, ("seq", "head"), shifted(1))
    a2_tokens = lax.ppermute(tokens, ("seq", "head"), shifted(2))
    b1_tokens = lax.ppermute(a1_tokens, "head", core_swap)
    b2_tokens = lax.ppermute(a2_tokens, "head", core_swap)

    gain = norm_gain.reshape(1, width)
    own = project(tokens, gain, w_qkv, 0)
    mix = jnp.dot(w_out, readout_weight, preferred_element_type=F32).astype(BF16)
    mix = jnp.where(core == 0, mix, jnp.roll(mix, half_read, axis=1))
    own_targets = lax.dynamic_slice_in_dim(targets, core * half_read, half_read, 1)

    panel_ids = voxel_panel[:, 0]
    panel_range = jnp.arange(panels, dtype=jnp.int32)
    hits = panel_range[:, None] == panel_ids[None, :]
    counts = jnp.sum(hits.astype(F32), axis=1, keepdims=True)

    def stretch_rows(array, offset, rows):
        stretch = seq_index + offset
        start = jnp.clip(stretch, 0, seq_count - 1) * rows
        return lax.dynamic_slice_in_dim(array, start, rows, 0)

    def inside(offset):
        stretch = seq_index + offset
        return (stretch >= 0) & (stretch < seq_count)

    offsets = (jnp.int32(0), step, -step)
    local_ids = jnp.concatenate(
        [
            jnp.where(inside(o), stretch_rows(panel_ids, o, tok_rows), -1)
            for o in offsets
        ]
    )
    hot = (local_ids[:, None] == panel_range[None, :]).astype(BF16)
    lists = jnp.concatenate([stretch_rows(key_blocks, o, per) for o in offsets])
    lengths = jnp.concatenate([stretch_rows(list_len, o, per) for o in offsets])
    outside = jnp.concatenate(
        [jnp.broadcast_to(~inside(o), (per,)) for o in offsets]
    )
    parity = jnp.asarray(np.tile(np.arange(2, dtype=np.int32), 3))
    candidates = (seq_index + step * jnp.asarray(KEY_STEP)) * per + parity[None, :]
    slot_live = jnp.arange(LIST)[None, :] < lengths[:, None]
    live = jnp.any(
        (lists[:, None, :] == candidates[:, :, None]) & slot_live[:, None, :], axis=-1
    )
    bias = jnp.where(live | outside[:, None], 0.0, DEAD).astype(F32)

    a1 = project(a1_tokens, gain, w_qkv, 0)
    b1 = project(b1_tokens, gain, w_qkv, 0)

    own_weight, own_att, read_keep, read_send = pl.pallas_call(
        functools.partial(own_kernel, pairs),
        grid=(pairs,),
        in_specs=[SMEM_SPEC]
        + [pair_spec(3, tok_rows)] * 3
        + [pl.BlockSpec((PAIR, readout), lambda p: (p, 0))],
        out_specs=[
            lead_spec((2, 3 * tok_rows, 2 * BLK)),
            lead_spec((2, PAIR, BLK)),
            whole_spec((tok_rows, half_read)),
            whole_spec((tok_rows, half_read)),
        ],
        out_shape=[
            jax.ShapeDtypeStruct((pairs, 2, 3 * tok_rows, 2 * BLK), BF16),
            jax.ShapeDtypeStruct((pairs, 2, PAIR, BLK), BF16),
            jax.ShapeDtypeStruct((tok_rows, half_read), F32),
            jax.ShapeDtypeStruct((tok_rows, half_read), F32),
        ],
        scratch_shapes=[pltpu.VMEM((tok_rows, readout), F32)],
        compiler_params=params(),
        name="attend_own",
    )(bias, own, a1, b1, mix)

    read_half = read_keep + lax.ppermute(read_send, "head", core_swap)
    read_rows = read_half.astype(BF16)
    all_rows = lax.all_to_all(
        jnp.broadcast_to(read_rows[None], (seq_count, tok_rows, half_read)), "seq", 0, 0
    ).reshape(all_tokens, half_read)

    a2 = project(a2_tokens, gain, w_qkv, 1)
    b2 = project(b2_tokens, gain, w_qkv, 1)
    side_weight, side_att = pl.pallas_call(
        side_kernel,
        grid=(pairs,),
        in_specs=[SMEM_SPEC] + [pair_spec(3, tok_rows)] * 3 + [pair_spec(2, tok_rows)] * 2,
        out_specs=[lead_spec((4, tok_rows, 2 * BLK)), lead_spec((4, PAIR, BLK))],
        out_shape=[
            jax.ShapeDtypeStruct((pairs, 4, tok_rows, 2 * BLK), BF16),
            jax.ShapeDtypeStruct((pairs, 4, PAIR, BLK), BF16),
        ],
        compiler_params=params(),
        cost_estimate=pl.CostEstimate(
            flops=pairs * 4 * 2 * 2 * 768 * 256 * 128,
            bytes_accessed=8 * 2**20,
            transcendentals=pairs * 4 * 768 * 256,
        ),
        name="attend_sides",
    )(bias, own, a1, b1, a2, b2)

    if panels * all_tokens <= 2**22:
        sums = jnp.dot(hits.astype(BF16), all_rows, preferred_element_type=F32)
    else:
        sums = jax.ops.segment_sum(all_rows.astype(F32), panel_ids, num_segments=panels)
    resid_a = sums / counts - own_targets
    resid_b = lax.ppermute(resid_a, "head", core_swap)

    keep, send, row_sum = pl.pallas_call(
        functools.partial(back_kernel, pairs),
        grid=(pairs,),
        in_specs=[
            SMEM_SPEC,
            whole_spec((panels, half_read)),
            whole_spec((panels, half_read)),
            whole_spec((3 * tok_rows, panels)),
            pl.BlockSpec((PAIR, readout), lambda p: (p, 0)),
            pair_spec(3, tok_rows),
            pair_spec(3, tok_rows),
            pair_spec(3, tok_rows),
            lead_spec((2, 3 * tok_rows, 2 * BLK)),
            lead_spec((2, PAIR, BLK)),
            lead_spec((4, tok_rows, 2 * BLK)),
            lead_spec((4, PAIR, BLK)),
            pair_spec(3, width),
            whole_spec((tok_rows, width)),
            whole_spec((1, width)),
        ],
        out_specs=[
            whole_spec((tok_rows, half_width)),
            whole_spec((tok_rows, half_width + BLK)),
            whole_spec((tok_rows, BLK)),
        ],
        out_shape=[
            jax.ShapeDtypeStruct((tok_rows, half_width), F32),
            jax.ShapeDtypeStruct((tok_rows, half_width + BLK), BF16),
            jax.ShapeDtypeStruct((tok_rows, BLK), F32),
        ],
        scratch_shapes=[
            pltpu.VMEM((panels, readout), F32),
            pltpu.VMEM((2, tok_rows, half_width), F32),
        ],
        compiler_params=params(),
        name="back",
    )(
        core.astype(jnp.int32).reshape(1),
        resid_a,
        resid_b,
        hot,
        mix,
        own,
        a1,
        b1,
        own_weight,
        own_att,
        side_weight,
        side_att,
        w_qkv,
        tokens,
        gain,
    )
    other = lax.ppermute(send, "head", core_swap)
    loss_mean = (
        0.5
        * (jnp.sum(counts * resid_a * resid_a) + jnp.sum(counts * resid_b * resid_b))
        / (all_tokens * readout)
    )
    inputs = tokens.astype(F32)
    root_mean = jnp.sqrt(jnp.mean(inputs * inputs, axis=-1, keepdims=True) + 1e-05)
    half_inputs = lax.dynamic_slice_in_dim(tokens, core * half_width, half_width, 1).astype(F32)
    half_gain = lax.dynamic_slice_in_dim(gain, core * half_width, half_width, 1)
    grad_normed = keep + other[:, :half_width].astype(F32)
    other_sum = other[:, half_width : half_width + 1].astype(F32) + other[:, -1:].astype(F32)
    full_sum = row_sum[:, :1] + other_sum
    gradient = half_gain * grad_normed / root_mean - half_inputs * full_sum / (
        width * root_mean**3
    )
    return (gradient, loss_mean.reshape(1))


def solution(mesh):
    return jax.shard_map(
        local,
        mesh=mesh,
        in_specs=(
            P(("groups", "seq"), None),
            P(),
            P(None, None, "head"),
            P("head", None),
            P(),
            P("groups", None),
            P("groups", None),
            P("groups"),
            P("groups", None),
        ),
        out_specs=(P(("groups", "seq"), "head"), P("groups")),
        check_vma=False,
    )
```

time: 294 us -> 101 us (0.34)
  waiting for transfers between devices: 106 us -> 4.01 us
  other arithmetic: 62.8 us -> 10.7 us
  Pallas kernels: 0 us -> 43.7 us
  local copies, waits for them, and re-layouts: 57.9 us -> 19 us
  matrix products: 25 us -> 2.88 us
  between operations: 16.1 us -> 3.36 us
  starting transfers between devices: 25.6 us -> 16.2 us
    psum x2 -> x0, waiting for transfers between devices: 85.6 us -> none  [the longest x1 70.4 us: pool_panels(): panel_sums = lax.psum(partial_sums, ('seq', 'head'))]
    pallas_call x0 -> x8, Pallas kernels: none -> 43.7 us  [the longest x1 12.9 us: local(): pl.pallas_call(functools.partial(back_kernel, pairs), grid=(pairs,), in_s...]
    scatter-add x3 -> x0, other arithmetic: 40.9 us -> none  [the longest x1 15.2 us: local(): jax.ops.segment_sum(jnp.ones((all_tokens,), jnp.float32), panel_ids, num_...]
    gather x6 -> x0, local copies, waits for them, and re-layouts: 23.8 us -> none  [the longest x1 11.8 us: local(): row_ids = panel_ids[positions]]
    dot_general x11 -> x2, matrix products: 25 us -> 2.88 us  [the longest x1 1.49 us: local(): sums = jnp.dot(hits.astype(BF16), all_rows, preferred_element_type=F32)]
    all_to_all x4 -> x1, waiting for transfers between devices: 19.9 us -> 0.01 us  [local(): lax.all_to_all(jnp.broadcast_to(read_rows[None], (seq_count, tok_rows, ha...]
    all_to_all x4 -> x1, starting transfers between devices: 25.5 us -> 5.7 us  [local(): lax.all_to_all(jnp.broadcast_to(read_rows[None], (seq_count, tok_rows, ha...]
    ppermute x0 -> x7, starting transfers between devices: none -> 10.5 us  [the longest x1 5.04 us: local(): a1_tokens = lax.ppermute(tokens, ('seq', 'head'), shifted(1))]
  transfers between devices with their start and end apart: 6 -> 8, of which waited for: 4 -> 2; matrix products, arithmetic and copies ran while one was open for 24% -> 15% of each run, Pallas kernels for 0% -> 31%
where the time goes in v1:
time: 101 us; the launch traced here: 99.8 us
  Pallas kernels  43.7 us (43%)
  local copies, waits for them, and re-layouts  19 us (19%)
  starting transfers between devices  16.2 us (16%)
  other arithmetic  10.7 us (11%)
  waiting for transfers between devices  4.01 us (4%)
  between operations  3.36 us (3%)
  matrix products  2.88 us (3%)
    pallas_call x1, Pallas kernels, local(): pl.pallas_call(functools.partial(back_kernel, pairs), grid=(pairs,), in_s...  12.9 us
    unnamed x48, local copies, waits for them, and re-layouts  12.3 us
    pallas_call x1, Pallas kernels, local(): pl.pallas_call(side_kernel, grid=(pairs,), in_specs=[SMEM_SPEC] + [pair_s...  11.5 us
    pallas_call x5, Pallas kernels, project(): pl.pallas_call(functools.partial(project_kernel, first), grid=(parts,), i...  10.2 us
    pallas_call x1, Pallas kernels, local(): pl.pallas_call(functools.partial(own_kernel, pairs), grid=(pairs,), in_sp...  9.12 us
    all_to_all x1, starting transfers between devices, local(): lax.all_to_all(jnp.broadcast_to(read_rows[None], (seq_count, tok_rows, ha...  5.7 us
    ppermute x1, starting transfers between devices, local(): a1_tokens = lax.ppermute(tokens, ('seq', 'head'), shifted(1))  5.04 us
    ppermute x1, starting transfers between devices, local(): a2_tokens = lax.ppermute(tokens, ('seq', 'head'), shifted(2))  4.26 us
  transfers between devices with their start and end apart: 8, of which 2 were waited for; matrix products, arithmetic and copies ran while one was open for 15% of the time, Pallas kernels for 31%

profile of v1, /device:TPU:0, one launch (start us, length us, event | category | flops | bytes accessed | tf_op | source)
XLA Modules:
  0.0 99.8 jit_solution(296459524606740796)
XLA Ops:
  0.7 5.0 %collective-permute-start = (bf16[256,1024]{1,0:T(8,128)(2,1)}, bf16[256,1024]{1,0:T(8,128)(2,1)S(1)}, u32[]{:S(2)}, u32[]{:S(2)}) collective-permute-start(bf16[256,1024]{1,0:T(8,128)(2,1)} %tokens_ref.1), channel_id=1, source_target_pairs={{0,2},{2,4},{4,6},{6,8},{8,10},{10,12},{12,14},{3,1},{5,3},{7,5},{... | collective-permute-start | bytes 1572872 | tf_op jit(solution)/shard_map/ppermute | solution.py:281
  5.7 4.3 %collective-permute-start.4 = (bf16[256,1024]{1,0:T(8,128)(2,1)}, bf16[256,1024]{1,0:T(8,128)(2,1)}, u32[]{:S(2)}, u32[]{:S(2)}) collective-permute-start(bf16[256,1024]{1,0:T(8,128)(2,1)} %tokens_ref.1), channel_id=1, source_target_pairs={{0,4},{2,6},{4,8},{6,10},{8,12},{10,14},{5,1},{7,3},{9,5},{11,7},{... | collective-permute-start | bytes 1572872 | tf_op jit(solution)/shard_map/ppermute | solution.py:282
  10.0 0.8 fusion.9
  11.0 0.9 constant_dynamic-slice_fusion.5
  13.0 1.4 %convolution_convert_fusion = bf16[512,128]{1,0:T(8,128)(2,1)S(1)} fusion(bf16[512,1024]{1,0:T(8,128)(2,1)S(1)} %copy-done, bf16[1024,128]{1,0:T(8,128)(2,1)} %param.15), kind=kOutput, calls=%fused_computation.3 | convolution fusion | flops 134283264 | bytes 1441792 | tf_op jit(solution)/shard_map/dot_general | solution.py:288
  14.5 3.6 %collective-permute-done.x_ref = bf16[256,1024]{1,0:T(8,128)(2,1)S(1)} collective-permute-done((bf16[256,1024]{1,0:T(8,128)(2,1)}, bf16[256,1024]{1,0:T(8,128)(2,1)S(1)}, u32[]{:S(2)}, u32[]{:S(2)}) %collective-permute-start) | collective-permute-done | bytes 524320 | tf_op jit(solution)/shard_map/ppermute | solution.py:281
  18.8 1.9 %copy-done.1 = bf16[3,1024,512]{2,1,0:T(8,128)(2,1)S(1)} copy-done((bf16[3,1024,512]{2,1,0:T(8,128)(2,1)S(1)}, bf16[3,1024,512]{2,1,0:T(8,128)(2,1)}, u32[]{:S(2)}) %copy-start.1) | copy-done | bytes 3145752
  20.7 1.6 %project.5.own_ref = bf16[3,256,512]{2,1,0:T(8,128)(2,1)S(1)} custom-call(bf16[256,1024]{1,0:T(8,128)(2,1)S(1)} %copy-done.5, f32[1,1024]{1,0:T(1,128)S(1)} %bitcast.12, bf16[3,1024,512]{2,1,0:T(8,128)(2,1)S(1)} %copy-done.1), custom_call_target="tpu_custom_call" | custom-call | flops 805306368 | bytes 3670016 | tf_op jit(solution)/shard_map/project/pallas_call | solution.py:57
  22.4 1.9 %copy-done.2 = bf16[3,1024,512]{2,1,0:T(8,128)(2,1)S(1)} copy-done((bf16[3,1024,512]{2,1,0:T(8,128)(2,1)S(1)}, bf16[3,1024,512]{2,1,0:T(8,128)(2,1)}, u32[]{:S(2)}) %copy-start.2) | copy-done | bytes 3145752
  24.3 1.6 %project.6.near_ref.a1_ref = bf16[3,256,512]{2,1,0:T(8,128)(2,1)S(1)} custom-call(bf16[256,1024]{1,0:T(8,128)(2,1)S(1)} %collective-permute-done.x_ref, f32[1,1024]{1,0:T(1,128)S(1)} %bitcast.13, bf16[3,1024,512]{2,1,0:T(8,128)(2,1)S(1)} %copy-done.2), custom_call_target="tpu_custom_call" | custom-call | flops 805306368 | bytes 3670016 | tf_op jit(solution)/shard_map/project/pallas_call | solution.py:57
  25.9 2.6 %project.7.far_ref.b1_ref = bf16[3,256,512]{2,1,0:T(8,128)(2,1)S(1)} custom-call(bf16[256,1024]{1,0:T(8,128)(2,1)} %collective-permute-done.1.x_ref, f32[1,1024]{1,0:T(1,128)S(1)} %bitcast.14, bf16[3,1024,512]{2,1,0:T(8,128)(2,1)S(1)} %copy-done.2), custom_call_target="tpu_custom_call" | custom-call | flops 805306368 | bytes 3670016 | tf_op jit(solution)/shard_map/project/pallas_call | solution.py:57
  28.6 9.1 %attend_own.1 = (bf16[4,2,768,256]{3,2,1,0:T(8,128)(2,1)S(1)}, bf16[4,2,128,128]{3,2,1,0:T(8,128)(2,1)S(1)}, f32[256,64]{1,0:T(8,128)S(1)}, f32[256,64]{1,0:T(8,128)}) custom-call(f32[6,6]{1,0:T(8,128)S(1)} %or_select_fusion.bias_ref, bf16[3,256,512]{2,1,0:T(8,128)(2,1)S(1)} %project.5.own_ref, bf16[3,256,512]{2,1,0:T(8,128)(2,1)S(1)} %project.6.near_ref.a1_ref, ...), custom_call_target="tpu_custom_call" | custom-call | tf_op jit(solution)/shard_map/attend_own/pallas_call | solution.py:330
  37.7 1.6 %copy-done.7 = bf16[4,2,768,256]{3,2,1,0:T(8,128)(2,1)} copy-done((bf16[4,2,768,256]{3,2,1,0:T(8,128)(2,1)}, bf16[4,2,768,256]{3,2,1,0:T(8,128)(2,1)S(1)}, u32[]{:S(2)}) %copy-start.7) | copy-done | bytes 3145752
  41.2 0.9 convert_reduce_fusion
  42.6 1.6 %add_convert_fusion = bf16[256,64]{1,0:T(8,128)(2,1)} fusion(f32[256,64]{1,0:T(8,128)} %copy-done.18, f32[256,64]{1,0:T(8,128)} %collective-permute-done.2), kind=kLoop, calls=%fused_computation.17 | loop fusion | flops 32768 | bytes 163840 | tf_op jit(solution)/shard_map/convert_element_type | solution.py:354
  44.2 1.5 %copy.30 = bf16[256,64]{0,1:T(8,128)(2,1)} copy(bf16[256,64]{1,0:T(8,128)(2,1)} %add_convert_fusion) | data formatting | bytes 65536 | tf_op jit(solution)/shard_map/convert_element_type | solution.py:354
  45.7 1.5 %broadcast_in_dim.46 = bf16[8,256,64]{1,2,0:T(8,128)(2,1)} broadcast(bf16[256,64]{0,1:T(8,128)(2,1)} %copy.30), dimensions={1,2} | broadcast | bytes 294912 | tf_op jit(solution)/shard_map/broadcast_in_dim | solution.py:356
  47.2 5.7 %all-to-all-start = ((bf16[8,256,64]{1,2,0:T(8,128)(2,1)}), bf16[8,256,64]{1,2,0:T(8,128)(2,1)}, u32[]{:S(2)}, u32[]{:S(2)}) async-start(bf16[8,256,64]{1,2,0:T(8,128)(2,1)} %broadcast_in_dim.46), calls=%async_computation | async-start | bytes 524288 | tf_op jit(solution)/shard_map/all_to_all | solution.py:355
  54.8 0.9 fusion.4.hot_ref
  55.8 1.9 %copy-done.3 = bf16[3,1024,512]{2,1,0:T(8,128)(2,1)S(1)} copy-done((bf16[3,1024,512]{2,1,0:T(8,128)(2,1)S(1)}, bf16[3,1024,512]{2,1,0:T(8,128)(2,1)}, u32[]{:S(2)}) %copy-start.3) | copy-done | bytes 3145752
  57.7 2.2 %project.8.a2_ref = bf16[2,256,512]{2,1,0:T(8,128)(2,1)S(1)} custom-call(bf16[256,1024]{1,0:T(8,128)(2,1)} %collective-permute-done.4.x_ref, f32[1,1024]{1,0:T(1,128)S(1)} %bitcast.15, bf16[3,1024,512]{2,1,0:T(8,128)(2,1)S(1)} %copy-done.3), custom_call_target="tpu_custom_call" | custom-call | flops 536870912 | bytes 2621440 | tf_op jit(solution)/shard_map/project/pallas_call | solution.py:57
  59.9 0.8 copy-done.11
  60.6 2.2 %project.9.b2_ref = bf16[2,256,512]{2,1,0:T(8,128)(2,1)S(1)} custom-call(bf16[256,1024]{1,0:T(8,128)(2,1)} %collective-permute-done.5.x_ref, f32[1,1024]{1,0:T(1,128)S(1)} %bitcast.16, bf16[3,1024,512]{2,1,0:T(8,128)(2,1)S(1)} %copy-done.3), custom_call_target="tpu_custom_call" | custom-call | flops 536870912 | bytes 2621440 | tf_op jit(solution)/shard_map/project/pallas_call | solution.py:57
  62.8 0.8 copy-done.13
  63.6 1.0 %copy.35 = bf16[8,8,8,256]{3,2,0,1:T(8,128)(2,1)S(1)} copy(bf16[8,8,8,256]{3,2,1,0:T(8,128)(2,1)} %bitcast.7) | data formatting | bytes 524288 | tf_op jit(solution)/shard_map/reshape | solution.py:357
  64.7 1.5 %fusion.2.resid_a_ref = f32[256,64]{1,0:T(8,128)S(1)} fusion(bf16[2048,64]{0,1:T(8,128)(2,1)S(1)} %bitcast.18, s32[2048]{0:T(1024)S(1)} %bitcast.20, f32[256,128]{1,0:T(8,128)} %param.16, s32[]{:T(128)S(6)} %select_n.76, f32[256]{0:T(256)} %convert_reduce_fusion), kind=kOutput, calls=%fused_computation.5 | convolution fusion | flops 67665920 | bytes 402436 | tf_op jit(solution)/shard_map/dot_general | solution.py:380
  66.4 1.2 %copy-done.14 = bf16[2,256,512]{2,1,0:T(8,128)(2,1)S(1)} copy-done((bf16[2,256,512]{2,1,0:T(8,128)(2,1)S(1)}, bf16[2,256,512]{2,1,0:T(8,128)(2,1)}, u32[]{:S(2)}) %copy-start.14) | copy-done | bytes 524312
  67.5 11.5 %attend_sides.1 = (bf16[4,4,256,256]{3,2,1,0:T(8,128)(2,1)S(1)}, bf16[4,4,128,128]{3,2,1,0:T(8,128)(2,1)S(1)}) custom-call(f32[6,6]{1,0:T(8,128)S(1)} %or_select_fusion.bias_ref, bf16[3,256,512]{2,1,0:T(8,128)(2,1)S(1)} %project.5.own_ref, bf16[3,256,512]{2,1,0:T(8,128)(2,1)S(1)} %project.6.near_ref.a1_ref, bf16[3,256,512]{2,1,0:T(8,128)(2,1)S(1)} %project.7.far_ref.b1_ref, ...), custom_call_target="tpu_custom_call" | custom-call | flops 1610612736 | bytes 8388608 | tf_op jit(solution)/shard_map/attend_sides/pallas_call | solution.py:361
  79.1 12.9 %back.1 = (f32[256,512]{1,0:T(8,128)S(1)}, bf16[256,640]{1,0:T(8,128)(2,1)}, f32[256,128]{1,0:T(8,128)S(1)}) custom-call(s32[1]{0:T(128)} %bitcast.core_ref, f32[256,64]{1,0:T(8,128)S(1)} %fusion.2.resid_a_ref, f32[256,64]{1,0:T(8,128)S(1)} %collective-permute-done.3.resid_b_ref, bf16[768,256]{1,0:T(8,128)(2,1)S(1)} %copy-done.9, ...), custom_call_target="tpu_custom_call" | custom-call | tf_op jit(solution)/shard_map/back/pallas_call | solution.py:386
  92.1 0.8 copy-done.10
  95.4 1.1 %add_reduce_fusion = f32[256]{0:T(256)S(1)} fusion(f32[256,128]{1,0:T(8,128)} %copy-done.19, bf16[256,640]{1,0:T(8,128)(2,1)S(1)} %collective-permute-done.6), kind=kLoop, calls=%fused_computation.16 | loop fusion | flops 1024 | bytes 3072 | tf_op jit(solution)/shard_map/add | solution.py:451
  96.5 2.1 %divide_subtract_fusion = f32[256,512]{1,0:T(8,128)} fusion(f32[256,512]{1,0:T(8,128)} %copy-done.10, bf16[256,640]{1,0:T(8,128)(2,1)S(1)} %collective-permute-done.6, f32[256]{0:T(256)S(1)} %get-tuple-element.31, f32[256]{0:T(256)S(1)} %add_reduce_fusion, bf16[256,1024]{1,0:T(8,128)(2,1)} %tokens_ref.1, s32[]{:T(128)S(6)} %select_n.69, ...), kind=kLoop, calls=%fused_computation.10 | loop fusion | flops 1048576 | bytes 1577988 | tf_op jit(solution)/shard_map/sub | solution.py:452
  (71 shorter events, 8.1 us)
Async XLA Ops:
  0.6 12.4 %copy-start = (bf16[512,1024]{1,0:T(8,128)(2,1)S(1)}, bf16[512,1024]{1,0:T(8,128)(2,1)}, u32[]{:S(2)}) copy-start(bf16[512,1024]{1,0:T(8,128)(2,1)} %param.14) | copy-start | bytes 3145732
  0.6 17.4 %copy-start.5 = (bf16[256,1024]{1,0:T(8,128)(2,1)S(1)}, bf16[256,1024]{1,0:T(8,128)(2,1)}, u32[]{:S(2)}) copy-start(bf16[256,1024]{1,0:T(8,128)(2,1)} %tokens_ref.1) | copy-start | bytes 1572868
  0.7 18.2 %copy-start.17 = (f32[1024]{0:T(1024)S(1)}, f32[1024]{0:T(1024)}, u32[]{:S(2)}) copy-start(f32[1024]{0:T(1024)} %param.12) | copy-start | bytes 12292
  0.7 17.4 %collective-permute-start = (bf16[256,1024]{1,0:T(8,128)(2,1)}, bf16[256,1024]{1,0:T(8,128)(2,1)S(1)}, u32[]{:S(2)}, u32[]{:S(2)}) collective-permute-start(bf16[256,1024]{1,0:T(8,128)(2,1)} %tokens_ref.1), channel_id=1, source_target_pairs={{0,2},{2,4},{4,6},{6,8},{8,10},{10,12},{12,14},{3,1},{5,3},{7,5},{... | collective-permute-start | bytes 1572872 | tf_op jit(solution)/shard_map/ppermute | solution.py:281
  5.7 36.4 %collective-permute-start.4 = (bf16[256,1024]{1,0:T(8,128)(2,1)}, bf16[256,1024]{1,0:T(8,128)(2,1)}, u32[]{:S(2)}, u32[]{:S(2)}) collective-permute-start(bf16[256,1024]{1,0:T(8,128)(2,1)} %tokens_ref.1), channel_id=1, source_target_pairs={{0,4},{2,6},{4,8},{6,10},{8,12},{10,14},{5,1},{7,3},{9,5},{11,7},{... | collective-permute-start | bytes 1572872 | tf_op jit(solution)/shard_map/ppermute | solution.py:282
  18.1 7.9 %collective-permute-start.1 = (bf16[256,1024]{1,0:T(8,128)(2,1)S(1)}, bf16[256,1024]{1,0:T(8,128)(2,1)}, u32[]{:S(2)}, u32[]{:S(2)}) collective-permute-start(bf16[256,1024]{1,0:T(8,128)(2,1)S(1)} %collective-permute-done.x_ref), channel_id=1, source_target_pairs={{0,1},{1,0},{2,3},{3,2},{4,5},{5,4},{6,7},{7,6},{8,9},{9,8},{10,11... | collective-permute-start | bytes 1572872 | tf_op jit(solution)/shard_map/ppermute | solution.py:283
  18.8 1.9 %copy-start.1 = (bf16[3,1024,512]{2,1,0:T(8,128)(2,1)S(1)}, bf16[3,1024,512]{2,1,0:T(8,128)(2,1)}, u32[]{:S(2)}) copy-start(bf16[3,1024,512]{2,1,0:T(8,128)(2,1)} %w_ref.11) | copy-start | bytes 9437188
  22.4 1.9 %copy-start.2 = (bf16[3,1024,512]{2,1,0:T(8,128)(2,1)S(1)}, bf16[3,1024,512]{2,1,0:T(8,128)(2,1)}, u32[]{:S(2)}) copy-start(bf16[3,1024,512]{2,1,0:T(8,128)(2,1)} %w_ref.11) | copy-start | bytes 9437188
  28.6 12.6 %copy-start.20 = (s32[2048,1]{0,1:T(1,128)S(1)}, s32[2048,1]{0,1:T(1,128)}, u32[]{:S(2)}) copy-start(s32[2048,1]{0,1:T(1,128)} %param.19) | copy-start | bytes 24580
  37.7 1.6 %copy-start.7 = (bf16[4,2,768,256]{3,2,1,0:T(8,128)(2,1)}, bf16[4,2,768,256]{3,2,1,0:T(8,128)(2,1)S(1)}, u32[]{:S(2)}) copy-start(bf16[4,2,768,256]{3,2,1,0:T(8,128)(2,1)S(1)} %get-tuple-element.13.own_weight_ref) | copy-start | bytes 9437188
  39.3 0.7 copy-start.15
  40.1 0.7 copy-start.18
  40.7 1.8 %collective-permute-start.2 = (f32[256,64]{1,0:T(8,128)}, f32[256,64]{1,0:T(8,128)}, u32[]{:S(2)}, u32[]{:S(2)}) collective-permute-start(f32[256,64]{1,0:T(8,128)} %get-tuple-element.12), channel_id=1, source_target_pairs={{0,1},{1,0},{2,3},{3,2},{4,5},{5,4},{6,7},{7,6},{8,9},{9,8},{10,11... | collective-permute-start | bytes 196616 | tf_op jit(solution)/shard_map/ppermute | solution.py:353
  42.1 18.5 %collective-permute-start.5 = (bf16[256,1024]{1,0:T(8,128)(2,1)}, bf16[256,1024]{1,0:T(8,128)(2,1)}, u32[]{:S(2)}, u32[]{:S(2)}) collective-permute-start(bf16[256,1024]{1,0:T(8,128)(2,1)} %collective-permute-done.4.x_ref), channel_id=1, source_target_pairs={{0,1},{1,0},{2,3},{3,2},{4,5},{5,4},{6,7},{7,6},{8,9},{9,8},{10,11... | collective-permute-start | bytes 1572872 | tf_op jit(solution)/shard_map/ppermute | solution.py:284
  47.2 16.4 %all-to-all-start = ((bf16[8,256,64]{1,2,0:T(8,128)(2,1)}), bf16[8,256,64]{1,2,0:T(8,128)(2,1)}, u32[]{:S(2)}, u32[]{:S(2)}) async-start(bf16[8,256,64]{1,2,0:T(8,128)(2,1)} %broadcast_in_dim.46), calls=%async_computation | async-start | bytes 524288 | tf_op jit(solution)/shard_map/all_to_all | solution.py:355
  55.8 1.9 %copy-start.3 = (bf16[3,1024,512]{2,1,0:T(8,128)(2,1)S(1)}, bf16[3,1024,512]{2,1,0:T(8,128)(2,1)}, u32[]{:S(2)}) copy-start(bf16[3,1024,512]{2,1,0:T(8,128)(2,1)} %w_ref.11) | copy-start | bytes 9437188
  59.9 0.8 copy-start.11
  62.8 0.8 copy-start.13
  63.6 2.7 %copy-start.12 = (bf16[2,256,512]{2,1,0:T(8,128)(2,1)S(1)}, bf16[2,256,512]{2,1,0:T(8,128)(2,1)}, u32[]{:S(2)}) copy-start(bf16[2,256,512]{2,1,0:T(8,128)(2,1)} %copy-done.11) | copy-start | bytes 1572868
  64.7 14.4 %copy-start.8 = (bf16[4,2,768,256]{3,2,1,0:T(8,128)(2,1)S(1)}, bf16[4,2,768,256]{3,2,1,0:T(8,128)(2,1)}, u32[]{:S(2)}) copy-start(bf16[4,2,768,256]{3,2,1,0:T(8,128)(2,1)} %copy-done.7) | copy-start | bytes 9437188
  66.2 12.9 %copy-start.4 = (bf16[3,1024,512]{2,1,0:T(8,128)(2,1)S(1)}, bf16[3,1024,512]{2,1,0:T(8,128)(2,1)}, u32[]{:S(2)}) copy-start(bf16[3,1024,512]{2,1,0:T(8,128)(2,1)} %w_ref.11) | copy-start | bytes 9437188
  66.2 12.9 %copy-start.6 = (bf16[256,1024]{1,0:T(8,128)(2,1)S(1)}, bf16[256,1024]{1,0:T(8,128)(2,1)}, u32[]{:S(2)}) copy-start(bf16[256,1024]{1,0:T(8,128)(2,1)} %tokens_ref.1) | copy-start | bytes 1572868
  66.2 12.9 %copy-start.9 = (bf16[768,256]{1,0:T(8,128)(2,1)S(1)}, bf16[768,256]{1,0:T(8,128)(2,1)}, u32[]{:S(2)}) copy-start(bf16[768,256]{1,0:T(8,128)(2,1)} %fusion.4.hot_ref) | copy-start | bytes 1179652
  66.2 12.8 %collective-permute-start.3 = (f32[256,64]{1,0:T(8,128)S(1)}, f32[256,64]{1,0:T(8,128)S(1)}, u32[]{:S(2)}, u32[]{:S(2)}) collective-permute-start(f32[256,64]{1,0:T(8,128)S(1)} %fusion.2.resid_a_ref), channel_id=1, source_target_pairs={{0,1},{1,0},{2,3},{3,2},{4,5},{5,4},{6,7},{7,6},{8,9},{9,8},{10,11... | collective-permute-start | bytes 196616 | tf_op jit(solution)/shard_map/ppermute | solution.py:384
  66.4 1.2 %copy-start.14 = (bf16[2,256,512]{2,1,0:T(8,128)(2,1)S(1)}, bf16[2,256,512]{2,1,0:T(8,128)(2,1)}, u32[]{:S(2)}) copy-start(bf16[2,256,512]{2,1,0:T(8,128)(2,1)} %copy-done.13) | copy-start | bytes 1572868
  67.5 11.5 %copy-start.16 = (bf16[4,2,128,128]{3,2,1,0:T(8,128)(2,1)S(1)}, bf16[4,2,128,128]{3,2,1,0:T(8,128)(2,1)}, u32[]{:S(2)}) copy-start(bf16[4,2,128,128]{3,2,1,0:T(8,128)(2,1)} %copy-done.15) | copy-start | bytes 786436
  79.1 14.3 %copy-start.22 = (f32[256]{0:T(256)S(1)}, f32[256]{0:T(256)}, u32[]{:S(2)}) copy-start(f32[256]{0:T(256)} %multiply_reduce_fusion) | copy-start | bytes 3076
  79.1 14.3 %copy-start.23 = (f32[256]{0:T(256)S(1)}, f32[256]{0:T(256)}, u32[]{:S(2)}) copy-start(f32[256]{0:T(256)} %convert_reduce_fusion) | copy-start | bytes 3076
  79.1 17.4 %copy-start.21 = (f32[512]{0:T(512)S(1)}, f32[512]{0:T(512)}, u32[]{:S(2)}) copy-start(f32[512]{0:T(512)} %dynamic-slice.6) | copy-start | bytes 6148
  92.1 0.8 copy-start.10
  92.8 1.3 %copy-start.19 = (f32[256,128]{1,0:T(8,128)}, f32[256,128]{1,0:T(8,128)S(1)}, u32[]{:S(2)}) copy-start(f32[256,128]{1,0:T(8,128)S(1)} %get-tuple-element.19) | copy-start | bytes 393220
  92.8 2.6 %collective-permute-start.6 = (bf16[256,640]{1,0:T(8,128)(2,1)}, bf16[256,640]{1,0:T(8,128)(2,1)S(1)}, u32[]{:S(2)}, u32[]{:S(2)}) collective-permute-start(bf16[256,640]{1,0:T(8,128)(2,1)} %get-tuple-element.18), channel_id=1, source_target_pairs={{0,1},{1,0},{2,3},{3,2},{4,5},{5,4},{6,7},{7,6},{8,9},{9,8},{10,11... | collective-permute-start | bytes 983048 | tf_op jit(solution)/shard_map/ppermute | solution.py:439

commit v2 on v1

v2 whole, which is shorter than its diff:
```python
import functools
import math

import jax
import jax.numpy as jnp
import numpy as np
from jax import lax
from jax.experimental import pallas as pl
from jax.experimental.pallas import tpu as pltpu
from jax.sharding import PartitionSpec as P

HD = 64
BLK = 128
LIST = 4
PAIR = 2 * HD
GROUP = 2
F32 = jnp.float32
BF16 = jnp.bfloat16
DEAD = 1e30
SCALE = 1.0 / math.sqrt(HD)
KEY_STEP = np.array([[0, 1, -1], [0, 1, 2], [0, -1, -2]], np.int32)
MIB = 1024 * 1024

NN = (((1,), (0,)), ((), ()))
NT = (((1,), (1,)), ((), ()))
TN = (((0,), (0,)), ((), ()))


def dot(a, b, dims, precision=None):
    return lax.dot_general(a, b, dims, precision=precision, preferred_element_type=F32)


def params(mib):
    return pltpu.CompilerParams(
        vmem_limit_bytes=mib * MIB, dimension_semantics=("arbitrary",)
    )


def inverse_root(inputs):
    return 1.0 / jnp.sqrt(jnp.mean(inputs * inputs, axis=-1, keepdims=True) + 1e-05)


def project_kernel(first, x_ref, gain_ref, w_ref, out_ref, normed):
    part = pl.program_id(0)

    @pl.when(part == 0)
    def _():
        inputs = x_ref[...].astype(F32)
        normed[...] = (inputs * gain_ref[...] * inverse_root(inputs)).astype(BF16)

    rows = dot(normed[...], w_ref[0], NN).astype(BF16)
    scale = jnp.where(part + first == 0, SCALE, 1.0)
    out_ref[0] = (rows.astype(F32) * scale).astype(BF16)


def project(tokens, gain, w_qkv, first):
    rows, width = tokens.shape
    parts, cols = 3 - first, w_qkv.shape[2]
    return pl.pallas_call(
        functools.partial(project_kernel, first),
        grid=(parts,),
        in_specs=[
            pl.BlockSpec((rows, width), lambda c: (0, 0)),
            pl.BlockSpec((1, width), lambda c: (0, 0)),
            pl.BlockSpec((1, width, cols), lambda c: (c + first, 0, 0)),
        ],
        out_specs=pl.BlockSpec((1, rows, cols), lambda c: (c, 0, 0)),
        out_shape=jax.ShapeDtypeStruct((parts, rows, cols), BF16),
        scratch_shapes=[pltpu.VMEM((rows, width), BF16)],
        compiler_params=params(12),
        cost_estimate=pl.CostEstimate(
            flops=2 * rows * width * cols * parts,
            bytes_accessed=parts * width * cols * 2 + rows * width * 2,
            transcendentals=rows,
        ),
        name="project",
    )(tokens, gain, w_qkv)


def pair_cols(p):
    return slice(p * PAIR, (p + 1) * PAIR)


def two_heads(tile):
    lane = lax.broadcasted_iota(jnp.int32, tile.shape, 1)
    zero = jnp.zeros_like(tile)
    return jnp.concatenate(
        [jnp.where(lane < HD, tile, zero), jnp.where(lane >= HD, tile, zero)], axis=0
    )


def fold_heads(pair_t):
    half = pair_t.shape[1] // 2
    return jnp.concatenate([pair_t[:HD, :half], pair_t[HD:, half:]], axis=0)


def soften(bias_ref, stretch, scores):
    count = scores.shape[0] // BLK
    blocks = [scores[k * BLK : (k + 1) * BLK] for k in range(count)]
    biases = [bias_ref[stretch, k : k + 1, :] for k in range(count)]
    tops = [jnp.max(b, axis=0, keepdims=True) - d for b, d in zip(blocks, biases)]
    top = functools.reduce(jnp.maximum, tops)
    expo = [jnp.exp(b - (top + d)) for b, d in zip(blocks, biases)]
    total = functools.reduce(jnp.add, [jnp.sum(e, axis=0, keepdims=True) for e in expo])
    inverse = 1.0 / total
    return jnp.concatenate([(e * inverse).astype(BF16) for e in expo], axis=0)


def own_kernel(
    steps, bias_ref, own_ref, a1_ref, b1_ref, mix_ref, weight_ref, att_ref, keep_ref, send_ref, read
):
    step = pl.program_id(0)

    @pl.when(step == 0)
    def _():
        read[...] = jnp.zeros_like(read)

    stretches = (own_ref, a1_ref, b1_ref)
    scores = []
    for p in range(GROUP):
        keys = jnp.concatenate([r[1, :, pair_cols(p)] for r in stretches], axis=0)
        scores.append(dot(keys, two_heads(own_ref[0, :, pair_cols(p)]), NT))
    weights = []
    for p in range(GROUP):
        weights.append(soften(bias_ref, 0, scores[p]))
        weight_ref[p] = weights[p]
    attended = []
    for p in range(GROUP):
        values = jnp.concatenate([r[2, :, pair_cols(p)] for r in stretches], axis=0)
        attended.append(fold_heads(dot(values, weights[p], TN)).astype(BF16))
        att_ref[p] = attended[p]
    read[...] += dot(mix_ref[...], jnp.concatenate(attended, axis=0), NN)

    @pl.when(step == steps - 1)
    def _():
        half = read.shape[0] // 2
        keep_ref[...] = read[:half]
        send_ref[...] = read[half:]


def side_kernel(bias_ref, own_ref, a1_ref, b1_ref, a2_ref, b2_ref, weight_ref, att_ref):
    own_rows = own_ref.shape[1]
    jobs = [(p, side) for p in range(GROUP) for side in range(2)]
    near, far = (a1_ref, b1_ref), (a2_ref, b2_ref)

    def stack(p, side, part):
        cols = pair_cols(p)
        return jnp.concatenate(
            [own_ref[part, :, cols], near[side][part, :, cols], far[side][part - 1, :, cols]],
            axis=0,
        )

    scores = [
        dot(stack(p, side, 1), two_heads(near[side][0, :, pair_cols(p)]), NT) for p, side in jobs
    ]
    weights = []
    for (p, side), score in zip(jobs, scores):
        weights.append(soften(bias_ref, 1 + side, score))
        weight_ref[p, side] = weights[-1][:own_rows]
    for (p, side), weight in zip(jobs, weights):
        att_ref[p, side] = fold_heads(dot(stack(p, side, 2), weight, TN)).astype(BF16)


def spread_kernel(keep_ref, got_ref, out_ref):
    rows = (keep_ref[...] + got_ref[...]).astype(BF16)
    for s in range(out_ref.shape[0]):
        out_ref[s] = rows


def pool_kernel(steps, rows_ref, ids_ref, counts_ref, targets_ref, out_ref, sums):
    step = pl.program_id(0)
    panels = out_ref.shape[1]
    count, _, tok_rows = rows_ref.shape

    @pl.when(step == 0)
    def _():
        sums[...] = jnp.zeros_like(sums)

    panel = lax.broadcasted_iota(jnp.int32, (panels, count * tok_rows), 0)
    hits = jnp.where(panel == ids_ref[...], 1.0, 0.0).astype(BF16)
    rows = jnp.concatenate([rows_ref[s] for s in range(count)], axis=1)
    sums[...] += dot(rows, hits, NT)

    @pl.when(step == steps - 1)
    def _():
        out_ref[...] = sums[...] / counts_ref[...] - targets_ref[...]


def back_kernel(
    steps,
    core_ref,
    resid_a_ref,
    resid_b_ref,
    counts_ref,
    hot_ref,
    mix_ref,
    own_ref,
    a1_ref,
    b1_ref,
    own_weight_ref,
    own_att_ref,
    side_weight_ref,
    side_att_ref,
    w_ref,
    tokens_ref,
    gain_ref,
    keep_ref,
    send_ref,
    stat_ref,
    loss_ref,
    residual,
    total,
):
    step = pl.program_id(0)
    half_read = resid_a_ref.shape[0]
    own_rows = own_ref.shape[1]

    @pl.when(step == 0)
    def _():
        residual[:half_read] = resid_a_ref[...]
        residual[half_read:] = resid_b_ref[...]
        total[...] = jnp.zeros_like(total)
        loss_ref[...] = jnp.broadcast_to(
            jnp.sum(counts_ref[...] * residual[...] * residual[...], keepdims=True),
            loss_ref.shape,
        )

    panel_grad = dot(
        residual[...], mix_ref[...].astype(F32), TN, lax.Precision.HIGHEST
    ).astype(BF16)
    out_grad = dot(hot_ref[...], panel_grad, NN)
    stretches = (own_ref, a1_ref, b1_ref)
    grads, weights, deltas, changes = [], [], [], []
    for p in range(GROUP):
        values = jnp.concatenate([r[2, :, pair_cols(p)] for r in stretches], axis=0)
        grads.append([])
        changes.append([])
        for t in range(3):
            grad_tile = out_grad[t * own_rows : (t + 1) * own_rows, pair_cols(p)]
            grads[p].append(two_heads(grad_tile.astype(BF16)))
            seen = values if t == 0 else values[:own_rows]
            changes[p].append(dot(seen, grads[p][t], NT))
    for p in range(GROUP):
        deltas.append([])
        for t in range(3):
            grad_tile = out_grad[t * own_rows : (t + 1) * own_rows, pair_cols(p)]
            attended = own_att_ref[p] if t == 0 else side_att_ref[p, t - 1]
            product = grad_tile.T * attended.astype(F32)
            deltas[p].append(
                jnp.concatenate(
                    [
                        jnp.sum(product[:HD], axis=0, keepdims=True),
                        jnp.sum(product[HD:], axis=0, keepdims=True),
                    ],
                    axis=1,
                )
            )
    scores = []
    for p in range(GROUP):
        weights.append([own_weight_ref[p], side_weight_ref[p, 0], side_weight_ref[p, 1]])
        scores.append(
            [
                (weights[p][t].astype(F32) * (changes[p][t] - deltas[p][t])).astype(BF16)
                for t in range(3)
            ]
        )
    grad_proj = [[], [], []]
    for p in range(GROUP):
        keys = jnp.concatenate([r[1, :, pair_cols(p)] for r in stretches], axis=0)
        grad_query = fold_heads(dot(keys, scores[p][0], TN)) * SCALE
        grad_proj[0].append(grad_query.T.astype(BF16))
        queries = jnp.concatenate([two_heads(r[0, :, pair_cols(p)]) for r in stretches], axis=0)
        own_scores = jnp.concatenate([s[:own_rows] for s in scores[p]], axis=1)
        grad_proj[1].append(dot(own_scores, queries, NN).astype(BF16))
        own_weights = jnp.concatenate([w[:own_rows] for w in weights[p]], axis=1)
        grad_proj[2].append(dot(own_weights, jnp.concatenate(grads[p], axis=0), NN).astype(BF16))
    flat = jnp.concatenate([g for part in grad_proj for g in part], axis=1)
    half = total.shape[2]
    for h in range(2):
        w_part = jnp.concatenate([w_ref[c, h * half : (h + 1) * half, :] for c in range(3)], axis=1)
        total[h] += dot(flat, w_part, NT)

    @pl.when(step == steps - 1)
    def _():
        inputs = tokens_ref[...].astype(F32)
        scaled = inputs * gain_ref[...]
        row_sum = jnp.zeros((own_rows, 1), F32)
        for h in range(2):
            row_sum += jnp.sum(
                scaled[:, h * half : (h + 1) * half] * total[h], axis=-1, keepdims=True
            )
        core = core_ref[0]
        keep_ref[...] = total[core]
        high = row_sum.astype(BF16).astype(F32)
        lane = lax.broadcasted_iota(jnp.int32, (own_rows, BLK), 1)
        send_ref[:, :half] = total[1 - core].astype(BF16)
        send_ref[:, half:] = jnp.where(lane < HD, high, row_sum - high).astype(BF16)
        stat_ref[...] = jnp.where(lane < HD, row_sum, inverse_root(inputs))


def final_kernel(core_ref, keep_ref, got_ref, stat_ref, tokens_ref, gain_ref, out_ref):
    half = keep_ref.shape[1]
    cols = pl.ds(pl.multiple_of(core_ref[0] * half, half), half)
    got_sum = got_ref[:, half : half + 1].astype(F32) + got_ref[:, half + HD : half + HD + 1].astype(F32)
    row_sum = stat_ref[:, :1] + got_sum
    inverse = stat_ref[:, HD : HD + 1]
    grad_normed = keep_ref[...] + got_ref[:, :half].astype(F32)
    shrink = row_sum * (inverse * inverse * inverse) * (0.5 / half)
    out_ref[...] = (
        gain_ref[:, cols] * grad_normed * inverse - tokens_ref[:, cols].astype(F32) * shrink
    )


def pair_spec(parts, rows):
    return pl.BlockSpec((parts, rows, GROUP * PAIR), lambda p: (0, 0, p))


def whole_spec(shape):
    return pl.BlockSpec(shape, lambda p: (0,) * len(shape))


def lead_spec(shape):
    return pl.BlockSpec((GROUP,) + shape, lambda p: (p,) + (0,) * len(shape))


SMEM_SPEC = pl.BlockSpec(memory_space=pltpu.SMEM)


def local(
    tokens, norm_gain, w_qkv, w_out, readout_weight, targets, key_blocks, list_len, voxel_panel
):
    tok_rows, width = tokens.shape
    cols = w_qkv.shape[2]
    pairs = cols // PAIR
    steps = pairs // GROUP
    panels, readout = targets.shape
    half_read = readout // 2
    half_width = width // 2
    seq_count = lax.axis_size("seq")
    seq_index = lax.axis_index("seq")
    core = lax.axis_index("head")
    side_step = 2 * core - 1
    all_tokens = voxel_panel.shape[0]
    per = tok_rows // BLK
    core_swap = [(0, 1), (1, 0)]

    def shifted(far):
        return [
            (2 * s, 2 * (s + far)) for s in range(seq_count - far)
        ] + [(2 * (s + far) + 1, 2 * s + 1) for s in range(seq_count - far)]

    a1_tokens = lax.ppermute(tokens, ("seq", "head"), shifted(1))
    a2_tokens = lax.ppermute(tokens, ("seq", "head"), shifted(2))

    gain = norm_gain.reshape(1, width)
    own = project(tokens, gain, w_qkv, 0)
    mix = jnp.dot(
        readout_weight.T, w_out.T, preferred_element_type=F32
    ).astype(BF16)
    mix = jnp.where(core == 0, mix, jnp.roll(mix, half_read, axis=0))
    own_targets = lax.dynamic_slice_in_dim(targets, core * half_read, half_read, 1).T

    panel_ids = voxel_panel[:, 0]
    panel_range = jnp.arange(panels, dtype=jnp.int32)
    counts = jnp.sum(
        (panel_range[:, None] == panel_ids[None, :]).astype(F32), axis=1
    ).reshape(1, panels)

    def stretch_rows(array, offset, rows):
        stretch = seq_index + offset
        start = jnp.clip(stretch, 0, seq_count - 1) * rows
        return lax.dynamic_slice_in_dim(array, start, rows, 0)

    def inside(offset):
        stretch = seq_index + offset
        return (stretch >= 0) & (stretch < seq_count)

    offsets = (jnp.int32(0), side_step, -side_step)
    local_ids = jnp.concatenate(
        [jnp.where(inside(o), stretch_rows(panel_ids, o, tok_rows), -1) for o in offsets]
    )
    hot = (local_ids[:, None] == panel_range[None, :]).astype(BF16)
    lists = jnp.stack([stretch_rows(key_blocks, o, per) for o in offsets])
    lengths = jnp.stack([stretch_rows(list_len, o, per) for o in offsets])
    outside = jnp.stack([~inside(o) for o in offsets])
    candidates = (
        (seq_index + side_step * jnp.asarray(KEY_STEP))[:, :, None] * per
        + jnp.arange(per, dtype=jnp.int32)
    ).reshape(3, 3 * per)
    slot_live = jnp.arange(LIST) < lengths[..., None]
    live = jnp.any(
        (lists[:, None] == candidates[:, :, None, None]) & slot_live[:, None], axis=-1
    )
    bias = jnp.where(live | outside[:, None, None], 0.0, DEAD).astype(F32)
    bias = jnp.tile(jnp.repeat(bias, BLK, axis=2), (1, 1, 2))

    a2 = project(a2_tokens, gain, w_qkv, 1)
    b2_tokens = lax.ppermute(a2_tokens, "head", core_swap)
    b2 = project(b2_tokens, gain, w_qkv, 1)

    a1_tokens, own, a2, b2, mix, own_targets, counts, hot, bias = lax.optimization_barrier(
        (a1_tokens, own, a2, b2, mix, own_targets, counts, hot, bias)
    )
    b1_tokens = lax.ppermute(a1_tokens, "head", core_swap)
    a1 = project(a1_tokens, gain, w_qkv, 0)
    b1 = project(b1_tokens, gain, w_qkv, 0)

    bias_spec = whole_spec(bias.shape)
    mix_spec = pl.BlockSpec((readout, GROUP * PAIR), lambda p: (0, p))
    own_weight, own_att, read_keep, read_send = pl.pallas_call(
        functools.partial(own_kernel, steps),
        grid=(steps,),
        in_specs=[bias_spec] + [pair_spec(3, tok_rows)] * 3 + [mix_spec],
        out_specs=[
            lead_spec((3 * tok_rows, 2 * tok_rows)),
            lead_spec((PAIR, tok_rows)),
            whole_spec((half_read, tok_rows)),
            whole_spec((half_read, tok_rows)),
        ],
        out_shape=[
            jax.ShapeDtypeStruct((pairs, 3 * tok_rows, 2 * tok_rows), BF16),
            jax.ShapeDtypeStruct((pairs, PAIR, tok_rows), BF16),
            jax.ShapeDtypeStruct((half_read, tok_rows), F32),
            jax.ShapeDtypeStruct((half_read, tok_rows), F32),
        ],
        scratch_shapes=[pltpu.VMEM((readout, tok_rows), F32)],
        compiler_params=params(24),
        name="attend_own",
    )(bias, own, a1, b1, mix)

    read_got = lax.ppermute(read_send, "head", core_swap)
    spread = pl.pallas_call(
        spread_kernel,
        out_shape=jax.ShapeDtypeStruct((seq_count, half_read, tok_rows), BF16),
        compiler_params=pltpu.CompilerParams(vmem_limit_bytes=8 * MIB),
        name="spread",
    )(read_keep, read_got)
    all_rows = lax.all_to_all(spread, "seq", 0, 0)

    side_weight, side_att = pl.pallas_call(
        side_kernel,
        grid=(steps,),
        in_specs=[bias_spec] + [pair_spec(3, tok_rows)] * 3 + [pair_spec(2, tok_rows)] * 2,
        out_specs=[lead_spec((2, tok_rows, 2 * tok_rows)), lead_spec((2, PAIR, tok_rows))],
        out_shape=[
            jax.ShapeDtypeStruct((pairs, 2, tok_rows, 2 * tok_rows), BF16),
            jax.ShapeDtypeStruct((pairs, 2, PAIR, tok_rows), BF16),
        ],
        compiler_params=params(28),
        cost_estimate=pl.CostEstimate(
            flops=pairs * 4 * 2 * 2 * 768 * 256 * 128,
            bytes_accessed=8 * MIB,
            transcendentals=pairs * 4 * 768 * 256,
        ),
        name="attend_sides",
    )(bias, own, a1, b1, a2, b2)
    all_rows, side_weight, side_att = lax.optimization_barrier((all_rows, side_weight, side_att))

    batch = min(seq_count, 8)
    pool_steps = seq_count // batch
    resid_a = pl.pallas_call(
        functools.partial(pool_kernel, pool_steps),
        grid=(pool_steps,),
        in_specs=[
            pl.BlockSpec((batch, half_read, tok_rows), lambda s: (s, 0, 0)),
            pl.BlockSpec((1, batch * tok_rows), lambda s: (0, s)),
            whole_spec((1, panels)),
            whole_spec((half_read, panels)),
        ],
        out_specs=whole_spec((half_read, panels)),
        out_shape=jax.ShapeDtypeStruct((half_read, panels), F32),
        scratch_shapes=[pltpu.VMEM((half_read, panels), F32)],
        compiler_params=params(12 + panels // 64),
        name="pool",
    )(all_rows, voxel_panel.reshape(1, all_tokens), counts, own_targets)
    resid_b = lax.ppermute(resid_a, "head", core_swap)

    core_index = core.astype(jnp.int32).reshape(1)
    keep, send, stats, loss = pl.pallas_call(
        functools.partial(back_kernel, steps),
        grid=(steps,),
        in_specs=[
            SMEM_SPEC,
            whole_spec((half_read, panels)),
            whole_spec((half_read, panels)),
            whole_spec((1, panels)),
            whole_spec((3 * tok_rows, panels)),
            mix_spec,
            pair_spec(3, tok_rows),
            pair_spec(3, tok_rows),
            pair_spec(3, tok_rows),
            lead_spec((3 * tok_rows, 2 * tok_rows)),
            lead_spec((PAIR, tok_rows)),
            lead_spec((2, tok_rows, 2 * tok_rows)),
            lead_spec((2, PAIR, tok_rows)),
            pair_spec(3, width),
            whole_spec((tok_rows, width)),
            whole_spec((1, width)),
        ],
        out_specs=[
            whole_spec((tok_rows, half_width)),
            whole_spec((tok_rows, half_width + BLK)),
            whole_spec((tok_rows, BLK)),
            whole_spec((1, BLK)),
        ],
        out_shape=[
            jax.ShapeDtypeStruct((tok_rows, half_width), F32),
            jax.ShapeDtypeStruct((tok_rows, half_width + BLK), BF16),
            jax.ShapeDtypeStruct((tok_rows, BLK), F32),
            jax.ShapeDtypeStruct((1, BLK), F32),
        ],
        scratch_shapes=[
            pltpu.VMEM((readout, panels), F32),
            pltpu.VMEM((2, tok_rows, half_width), F32),
        ],
        compiler_params=params(30 + panels // 128),
        name="back",
    )(
        core_index,
        resid_a,
        resid_b,
        counts,
        hot,
        mix,
        own,
        a1,
        b1,
        own_weight,
        own_att,
        side_weight,
        side_att,
        w_qkv,
        tokens,
        gain,
    )
    got = lax.ppermute(send, "head", core_swap)
    loss_mean = 0.5 * loss[0, :1] / (all_tokens * readout)
    gradient = pl.pallas_call(
        final_kernel,
        in_specs=[SMEM_SPEC] + [pl.BlockSpec(memory_space=pltpu.VMEM)] * 5,
        out_shape=jax.ShapeDtypeStruct((tok_rows, half_width), F32),
        compiler_params=pltpu.CompilerParams(vmem_limit_bytes=8 * MIB),
        name="final",
    )(core_index, keep, got, stats, tokens, gain)
    return (gradient, loss_mean)


def solution(mesh):
    return jax.shard_map(
        local,
        mesh=mesh,
        in_specs=(
            P(("groups", "seq"), None),
            P(),
            P(None, None, "head"),
            P("head", None),
            P(),
            P("groups", None),
            P("groups", None),
            P("groups"),
            P("groups", None),
        ),
        out_specs=(P(("groups", "seq"), "head"), P("groups")),
        check_vma=False,
    )
```

time: 101 us -> 82.1 us (0.81)
  Pallas kernels: 43.7 us -> 28.3 us
  local copies, waits for them, and re-layouts: 19 us -> 26.8 us
  other arithmetic: 10.7 us -> 3.83 us
  matrix products: 2.88 us -> 1.44 us
  starting transfers between devices: 16.2 us -> 15 us
  between operations: 3.36 us -> 2.18 us
    pallas_call x3 -> x6, Pallas kernels: 33.5 us -> 19 us  [the longest x1 7.6 us: local(): pl.pallas_call(functools.partial(back_kernel, steps), grid=(steps,), in_s...]
    unnamed x48 -> x51, local copies, waits for them, and re-layouts: 12.3 us -> 22.8 us
    ppermute x1, waiting for transfers between devices: 3.56 us -> 0.01 us  [local(): a1_tokens = lax.ppermute(tokens, ('seq', 'head'), shifted(1))]
    sub x1 -> x0, other arithmetic: 2.11 us -> none  [local(): half_gain * grad_normed / root_mean]
    ppermute x2, waiting for transfers between devices: 0.44 us -> 2.33 us  [the longest x1 1.33 us: local(): got = lax.ppermute(send, 'head', core_swap)]
    add x2 -> x1, other arithmetic: 1.78 us -> 0.07 us  [local(): (seq_index + side_step * jnp.asarray(KEY_STEP))[:, :, None] * per]
    convert_element_type x1 -> x0, other arithmetic: 1.61 us -> none  [local(): read_rows = read_half.astype(BF16)]
    ppermute x1, starting transfers between devices: 4.26 us -> 5.85 us  [local(): a2_tokens = lax.ppermute(tokens, ('seq', 'head'), shifted(2))]
  transfers between devices with their start and end apart: 8 -> 8, of which waited for: 2 -> 3; matrix products, arithmetic and copies ran while one was open for 15% -> 12% of each run, Pallas kernels for 31% -> 16%
where the time goes in v2:
time: 82.1 us; the launch traced here: 81 us
  Pallas kernels  28.3 us (34%)
  local copies, waits for them, and re-layouts  26.8 us (33%)
  starting transfers between devices  15 us (18%)
  other arithmetic  3.83 us (5%)
  waiting for transfers between devices  3.34 us (4%)
  between operations  2.18 us (3%)
  matrix products  1.44 us (2%)
    unnamed x51, local copies, waits for them, and re-layouts  22.8 us
    pallas_call x5, Pallas kernels, project(): pl.pallas_call(functools.partial(project_kernel, first), grid=(parts,), i...  9.36 us
    pallas_call x1, Pallas kernels, local(): pl.pallas_call(functools.partial(back_kernel, steps), grid=(steps,), in_s...  7.6 us
    ppermute x1, starting transfers between devices, local(): a2_tokens = lax.ppermute(tokens, ('seq', 'head'), shifted(2))  5.85 us
    pallas_call x1, Pallas kernels, local(): pl.pallas_call(side_kernel, grid=(steps,), in_specs=[bias_spec] + [pair_s...  5.4 us
    all_to_all x1, starting transfers between devices, local(): all_rows = lax.all_to_all(spread, 'seq', 0, 0)  4.22 us
    pallas_call x1, Pallas kernels, local(): pl.pallas_call(functools.partial(own_kernel, steps), grid=(steps,), in_sp...  3.55 us
    ppermute x1, starting transfers between devices, local(): a1_tokens = lax.ppermute(tokens, ('seq', 'head'), shifted(1))  3.45 us
  transfers between devices with their start and end apart: 8, of which 3 were waited for; matrix products, arithmetic and copies ran while one was open for 12% of the time, Pallas kernels for 16%

profile of v2, /device:TPU:0, one launch (start us, length us, event | category | flops | bytes accessed | tf_op | source)
XLA Modules:
  0.0 81.0 jit_solution(18009842116620972342)
XLA Ops:
  0.7 5.9 %collective-permute-start.1 = (bf16[256,1024]{1,0:T(8,128)(2,1)}, bf16[256,1024]{1,0:T(8,128)(2,1)}, u32[]{:S(2)}, u32[]{:S(2)}) collective-permute-start(bf16[256,1024]{1,0:T(8,128)(2,1)} %tokens_ref.3), channel_id=1, source_target_pairs={{0,4},{2,6},{4,8},{6,10},{8,12},{10,14},{5,1},{7,3},{9,5},{11,7},{... | collective-permute-start | bytes 1572872 | tf_op jit(solution)/shard_map/ppermute | solution.py:353
  6.5 3.4 %collective-permute-start = (bf16[256,1024]{1,0:T(8,128)(2,1)}, bf16[256,1024]{1,0:T(8,128)(2,1)S(1)}, u32[]{:S(2)}, u32[]{:S(2)}) collective-permute-start(bf16[256,1024]{1,0:T(8,128)(2,1)} %tokens_ref.3), channel_id=1, source_target_pairs={{0,2},{2,4},{4,6},{6,8},{8,10},{10,12},{12,14},{3,1},{5,3},{7,5},{... | collective-permute-start | bytes 1572872 | tf_op jit(solution)/shard_map/ppermute | solution.py:352
  10.7 1.0 %convert_reduce_fusion = f32[256]{0:T(256)S(1)} fusion(s32[2048]{0:T(1024)} %bitcast.35), kind=kLoop, calls=%fused_computation | loop fusion | flops 1572608 | bytes 9216 | tf_op jit(solution)/shard_map/reduce_sum | solution.py:365
  14.3 1.0 %constant_dynamic-slice_fusion.6 = f32[256,64]{1,0:T(8,128)S(1)} fusion(f32[256,128]{1,0:T(8,128)} %param.15, s32[]{:T(128)S(6)} %select_n.67), kind=kLoop, calls=%fused_computation.24 | loop fusion | bytes 131076 | tf_op jit(solution)/shard_map/dynamic_slice | solution.py:361
  16.1 1.4 %convolution_convert_fusion = bf16[128,512]{1,0:T(8,128)(2,1)S(1)} fusion(bf16[1024,128]{1,0:T(8,128)(2,1)} %param.14, bf16[512,1024]{1,0:T(8,128)(2,1)S(1)} %copy-done), kind=kOutput, calls=%fused_computation.2 | convolution fusion | flops 134283264 | bytes 1441792 | tf_op jit(solution)/shard_map/dot_general | solution.py:357
  17.7 1.9 %copy-done.1 = bf16[3,1024,512]{2,1,0:T(8,128)(2,1)S(1)} copy-done((bf16[3,1024,512]{2,1,0:T(8,128)(2,1)S(1)}, bf16[3,1024,512]{2,1,0:T(8,128)(2,1)}, u32[]{:S(2)}) %copy-start.1) | copy-done | bytes 3145752
  19.6 1.6 %project.5.own_ref = bf16[3,256,512]{2,1,0:T(8,128)(2,1)S(1)} custom-call(bf16[256,1024]{1,0:T(8,128)(2,1)S(1)} %copy-done.4, f32[1,1024]{1,0:T(1,128)S(1)} %bitcast.28, bf16[3,1024,512]{2,1,0:T(8,128)(2,1)S(1)} %copy-done.1), custom_call_target="tpu_custom_call" | custom-call | flops 805306368 | bytes 3670016 | tf_op jit(solution)/shard_map/project/pallas_call | solution.py:59
  23.7 1.9 %copy-done.2 = bf16[3,1024,512]{2,1,0:T(8,128)(2,1)S(1)} copy-done((bf16[3,1024,512]{2,1,0:T(8,128)(2,1)S(1)}, bf16[3,1024,512]{2,1,0:T(8,128)(2,1)}, u32[]{:S(2)}) %copy-start.2) | copy-done | bytes 3145752
  25.6 2.2 %project.6.a2_ref = bf16[2,256,512]{2,1,0:T(8,128)(2,1)S(1)} custom-call(bf16[256,1024]{1,0:T(8,128)(2,1)} %collective-permute-done.1.x_ref, f32[1,1024]{1,0:T(1,128)S(1)} %bitcast.29, bf16[3,1024,512]{2,1,0:T(8,128)(2,1)S(1)} %copy-done.2), custom_call_target="tpu_custom_call" | custom-call | flops 536870912 | bytes 2621440 | tf_op jit(solution)/shard_map/project/pallas_call | solution.py:59
  27.8 2.4 %project.7.b2_ref = bf16[2,256,512]{2,1,0:T(8,128)(2,1)S(1)} custom-call(bf16[256,1024]{1,0:T(8,128)(2,1)} %collective-permute-done.2.x_ref, f32[1,1024]{1,0:T(1,128)S(1)} %bitcast.30, bf16[3,1024,512]{2,1,0:T(8,128)(2,1)S(1)} %copy-done.2), custom_call_target="tpu_custom_call" | custom-call | flops 536870912 | bytes 2621440 | tf_op jit(solution)/shard_map/project/pallas_call | solution.py:59
  30.8 1.6 %project.8.a1_ref = bf16[3,256,512]{2,1,0:T(8,128)(2,1)S(1)} custom-call(bf16[256,1024]{1,0:T(8,128)(2,1)S(1)} %collective-permute-done.x_ref, f32[1,1024]{1,0:T(1,128)S(1)} %bitcast.31, bf16[3,1024,512]{2,1,0:T(8,128)(2,1)S(1)} %copy-done.2), custom_call_target="tpu_custom_call" | custom-call | flops 805306368 | bytes 3670016 | tf_op jit(solution)/shard_map/project/pallas_call | solution.py:59
  32.4 1.6 %project.9.b1_ref = bf16[3,256,512]{2,1,0:T(8,128)(2,1)S(1)} custom-call(bf16[256,1024]{1,0:T(8,128)(2,1)S(1)} %collective-permute-done.3.x_ref, f32[1,1024]{1,0:T(1,128)S(1)} %bitcast.32, bf16[3,1024,512]{2,1,0:T(8,128)(2,1)S(1)} %copy-done.2), custom_call_target="tpu_custom_call" | custom-call | flops 805306368 | bytes 3670016 | tf_op jit(solution)/shard_map/project/pallas_call | solution.py:59
  34.1 3.6 %attend_own.1 = (bf16[4,768,512]{2,1,0:T(8,128)(2,1)S(1)}, bf16[4,128,256]{2,1,0:T(8,128)(2,1)S(1)}, f32[64,256]{1,0:T(8,128)S(1)}, f32[64,256]{1,0:T(8,128)S(1)}) custom-call(f32[3,6,512]{2,1,0:T(8,128)S(1)} %copy-done.22, bf16[3,256,512]{2,1,0:T(8,128)(2,1)S(1)} %project.5.own_ref, bf16[3,256,512]{2,1,0:T(8,128)(2,1)S(1)} %project.8.a1_ref, ...), custom_call_target="tpu_custom_call" | custom-call | tf_op jit(solution)/shard_map/attend_own/pallas_call | solution.py:410
  37.6 1.6 %copy-done.6 = bf16[4,768,512]{2,1,0:T(8,128)(2,1)} copy-done((bf16[4,768,512]{2,1,0:T(8,128)(2,1)}, bf16[4,768,512]{2,1,0:T(8,128)(2,1)S(1)}, u32[]{:S(2)}) %copy-start.6) | copy-done | bytes 3145752
  40.2 1.0 %collective-permute-done.4.got_ref = f32[64,256]{1,0:T(8,128)S(1)} collective-permute-done((f32[64,256]{1,0:T(8,128)S(1)}, f32[64,256]{1,0:T(8,128)S(1)}, u32[]{:S(2)}, u32[]{:S(2)}) %collective-permute-start.4) | collective-permute-done | bytes 65568 | tf_op jit(solution)/shard_map/ppermute | solution.py:431
  41.9 4.2 %all-to-all-start = ((bf16[8,64,256]{2,1,0:T(8,128)(2,1)}), bf16[8,64,256]{2,1,0:T(8,128)(2,1)}, u32[]{:S(2)}, u32[]{:S(2)}) async-start(bf16[8,64,256]{2,1,0:T(8,128)(2,1)} %copy-done.11), calls=%async_computation | async-start | bytes 524288 | tf_op jit(solution)/shard_map/all_to_all | solution.py:438
  46.2 1.0 %copy-done.13 = bf16[2,256,512]{2,1,0:T(8,128)(2,1)S(1)} copy-done((bf16[2,256,512]{2,1,0:T(8,128)(2,1)S(1)}, bf16[2,256,512]{2,1,0:T(8,128)(2,1)}, u32[]{:S(2)}) %copy-start.13) | copy-done | bytes 524312
  47.2 1.0 %copy-done.15 = bf16[2,256,512]{2,1,0:T(8,128)(2,1)S(1)} copy-done((bf16[2,256,512]{2,1,0:T(8,128)(2,1)S(1)}, bf16[2,256,512]{2,1,0:T(8,128)(2,1)}, u32[]{:S(2)}) %copy-start.15) | copy-done | bytes 524312
  49.0 5.4 %attend_sides.1 = (bf16[4,2,256,512]{3,2,1,0:T(8,128)(2,1)S(1)}, bf16[4,2,128,256]{3,2,1,0:T(8,128)(2,1)S(1)}) custom-call(f32[3,6,512]{2,1,0:T(8,128)S(1)} %copy-done.23, bf16[3,256,512]{2,1,0:T(8,128)(2,1)S(1)} %project.5.own_ref, bf16[3,256,512]{2,1,0:T(8,128)(2,1)S(1)} %project.8.a1_ref, bf16[3,256,512]{2,1,0:T(8,128)(2,1)S(1)} %project.9.b1_ref, ...), custom_call_target="tpu_custom_call" | custom-call | flops 1610612736 | bytes 8388608 | tf_op jit(solution)/shard_map/attend_sides/pallas_call | solution.py:440
  54.5 1.3 %copy-done.8 = bf16[4,2,256,512]{3,2,1,0:T(8,128)(2,1)} copy-done((bf16[4,2,256,512]{3,2,1,0:T(8,128)(2,1)}, bf16[4,2,256,512]{3,2,1,0:T(8,128)(2,1)S(1)}, u32[]{:S(2)}) %copy-start.8) | copy-done | bytes 2097176
  57.4 1.4 %pool.1.resid_a_ref = f32[64,256]{1,0:T(8,128)S(1)} custom-call(bf16[8,64,256]{2,1,0:T(8,128)(2,1)} %all-to-all-done.rows_ref, s32[1,2048]{1,0:T(1,128)S(1)} %bitcast.36, f32[1,256]{1,0:T(1,128)S(1)} %bitcast.37, f32[64,256]{1,0:T(8,128)S(1)} %bitcast.27), custom_call_target="tpu_custom_call" | custom-call | tf_op jit(solution)/shard_map/pool/pallas_call | solution.py:461
  59.1 1.0 %collective-permute-done.5.resid_b_ref = f32[64,256]{1,0:T(8,128)S(1)} collective-permute-done((f32[64,256]{1,0:T(8,128)S(1)}, f32[64,256]{1,0:T(8,128)S(1)}, u32[]{:S(2)}, u32[]{:S(2)}) %collective-permute-start.5) | collective-permute-done | bytes 65568 | tf_op jit(solution)/shard_map/ppermute | solution.py:476
  60.1 1.9 %copy-done.3 = bf16[3,1024,512]{2,1,0:T(8,128)(2,1)S(1)} copy-done((bf16[3,1024,512]{2,1,0:T(8,128)(2,1)S(1)}, bf16[3,1024,512]{2,1,0:T(8,128)(2,1)}, u32[]{:S(2)}) %copy-start.3) | copy-done | bytes 3145752
  62.0 1.0 %copy-done.5 = bf16[256,1024]{1,0:T(8,128)(2,1)S(1)} copy-done((bf16[256,1024]{1,0:T(8,128)(2,1)S(1)}, bf16[256,1024]{1,0:T(8,128)(2,1)}, u32[]{:S(2)}) %copy-start.5) | copy-done | bytes 524312
  63.1 1.9 %copy-done.7 = bf16[4,768,512]{2,1,0:T(8,128)(2,1)S(1)} copy-done((bf16[4,768,512]{2,1,0:T(8,128)(2,1)S(1)}, bf16[4,768,512]{2,1,0:T(8,128)(2,1)}, u32[]{:S(2)}) %copy-start.7) | copy-done | bytes 3145752
  65.0 1.6 %copy-done.9 = bf16[4,2,256,512]{3,2,1,0:T(8,128)(2,1)S(1)} copy-done((bf16[4,2,256,512]{3,2,1,0:T(8,128)(2,1)S(1)}, bf16[4,2,256,512]{3,2,1,0:T(8,128)(2,1)}, u32[]{:S(2)}) %copy-start.9) | copy-done | bytes 2097176
  66.6 1.0 %copy-done.10 = bf16[768,256]{1,0:T(8,128)(2,1)S(1)} copy-done((bf16[768,256]{1,0:T(8,128)(2,1)S(1)}, bf16[768,256]{1,0:T(8,128)(2,1)}, u32[]{:S(2)}) %copy-start.10) | copy-done | bytes 393240
  67.6 1.0 %copy-done.17 = bf16[4,2,128,256]{3,2,1,0:T(8,128)(2,1)S(1)} copy-done((bf16[4,2,128,256]{3,2,1,0:T(8,128)(2,1)S(1)}, bf16[4,2,128,256]{3,2,1,0:T(8,128)(2,1)}, u32[]{:S(2)}) %copy-start.17) | copy-done | bytes 524312
  68.6 0.9 %copy-done.19 = bf16[4,128,256]{2,1,0:T(8,128)(2,1)S(1)} copy-done((bf16[4,128,256]{2,1,0:T(8,128)(2,1)S(1)}, bf16[4,128,256]{2,1,0:T(8,128)(2,1)}, u32[]{:S(2)}) %copy-start.19) | copy-done | bytes 262168
  69.5 7.6 %back.1 = (f32[256,512]{1,0:T(8,128)S(1)}, bf16[256,640]{1,0:T(8,128)(2,1)S(1)}, f32[256,128]{1,0:T(8,128)S(1)}, f32[1,128]{1,0:T(1,128)S(1)}) custom-call(s32[1]{0:T(128)} %bitcast.core_ref, f32[64,256]{1,0:T(8,128)S(1)} %pool.1.resid_a_ref, f32[64,256]{1,0:T(8,128)S(1)} %collective-permute-done.5.resid_b_ref, f32[1,256]{1,0:T(1,128)S(1)} %bitcast.38, ...), custom_call_target="tpu_custom_call" | custom-call | tf_op jit(solution)/shard_map/back/pallas_call | solution.py:479
  77.5 1.3 %collective-permute-done.6.got_ref = bf16[256,640]{1,0:T(8,128)(2,1)S(1)} collective-permute-done((bf16[256,640]{1,0:T(8,128)(2,1)S(1)}, bf16[256,640]{1,0:T(8,128)(2,1)S(1)}, u32[]{:S(2)}, u32[]{:S(2)}) %collective-permute-start.6) | collective-permute-done | bytes 327712 | tf_op jit(solution)/shard_map/ppermute | solution.py:536
  78.9 1.0 %final.1 = f32[256,512]{1,0:T(8,128)} custom-call(s32[1]{0:T(128)} %bitcast.core_ref, f32[256,512]{1,0:T(8,128)S(1)} %get-tuple-element.42.keep_ref, bf16[256,640]{1,0:T(8,128)(2,1)S(1)} %collective-permute-done.6.got_ref, f32[256,128]{1,0:T(8,128)S(1)} %get-tuple-element.44.stat_ref, bf16[256,1024]{1,0:T(8,128)(2,1)S(1)} %copy-done.5, f32[1,1024]{1,0:T(1,128)S(1)} %bitcast.34), custom_call_target="tpu_custom_call" | custom-call | tf_op jit(solution)/shard_map/final/pallas_call | solution.py:538
  (77 shorter events, 12.1 us)
Async XLA Ops:
  0.6 15.5 %copy-start = (bf16[512,1024]{1,0:T(8,128)(2,1)S(1)}, bf16[512,1024]{1,0:T(8,128)(2,1)}, u32[]{:S(2)}) copy-start(bf16[512,1024]{1,0:T(8,128)(2,1)} %param.13) | copy-start | bytes 3145732
  0.6 17.0 %copy-start.4 = (bf16[256,1024]{1,0:T(8,128)(2,1)S(1)}, bf16[256,1024]{1,0:T(8,128)(2,1)}, u32[]{:S(2)}) copy-start(bf16[256,1024]{1,0:T(8,128)(2,1)} %tokens_ref.3) | copy-start | bytes 1572868
  0.7 17.0 %copy-start.21 = (f32[1024]{0:T(1024)S(1)}, f32[1024]{0:T(1024)}, u32[]{:S(2)}) copy-start(f32[1024]{0:T(1024)} %param.11) | copy-start | bytes 12292
  0.7 16.9 %collective-permute-start.1 = (bf16[256,1024]{1,0:T(8,128)(2,1)}, bf16[256,1024]{1,0:T(8,128)(2,1)}, u32[]{:S(2)}, u32[]{:S(2)}) collective-permute-start(bf16[256,1024]{1,0:T(8,128)(2,1)} %tokens_ref.3), channel_id=1, source_target_pairs={{0,4},{2,6},{4,8},{6,10},{8,12},{10,14},{5,1},{7,3},{9,5},{11,7},{... | collective-permute-start | bytes 1572872 | tf_op jit(solution)/shard_map/ppermute | solution.py:353
  6.5 23.7 %collective-permute-start = (bf16[256,1024]{1,0:T(8,128)(2,1)}, bf16[256,1024]{1,0:T(8,128)(2,1)S(1)}, u32[]{:S(2)}, u32[]{:S(2)}) collective-permute-start(bf16[256,1024]{1,0:T(8,128)(2,1)} %tokens_ref.3), channel_id=1, source_target_pairs={{0,2},{2,4},{4,6},{6,8},{8,10},{10,12},{12,14},{3,1},{5,3},{7,5},{... | collective-permute-start | bytes 1572872 | tf_op jit(solution)/shard_map/ppermute | solution.py:352
  17.6 10.2 %collective-permute-start.2 = (bf16[256,1024]{1,0:T(8,128)(2,1)}, bf16[256,1024]{1,0:T(8,128)(2,1)}, u32[]{:S(2)}, u32[]{:S(2)}) collective-permute-start(bf16[256,1024]{1,0:T(8,128)(2,1)} %collective-permute-done.1.x_ref), channel_id=1, source_target_pairs={{0,1},{1,0},{2,3},{3,2},{4,5},{5,4},{6,7},{7,6},{8,9},{9,8},{10,11... | collective-permute-start | bytes 1572872 | tf_op jit(solution)/shard_map/ppermute | solution.py:398
  17.7 1.9 %copy-start.1 = (bf16[3,1024,512]{2,1,0:T(8,128)(2,1)S(1)}, bf16[3,1024,512]{2,1,0:T(8,128)(2,1)}, u32[]{:S(2)}) copy-start(bf16[3,1024,512]{2,1,0:T(8,128)(2,1)} %w_ref.11) | copy-start | bytes 9437188
  23.7 1.9 %copy-start.2 = (bf16[3,1024,512]{2,1,0:T(8,128)(2,1)S(1)}, bf16[3,1024,512]{2,1,0:T(8,128)(2,1)}, u32[]{:S(2)}) copy-start(bf16[3,1024,512]{2,1,0:T(8,128)(2,1)} %w_ref.11) | copy-start | bytes 9437188
  27.8 2.4 %copy-start.12 = (bf16[2,256,512]{2,1,0:T(8,128)(2,1)}, bf16[2,256,512]{2,1,0:T(8,128)(2,1)S(1)}, u32[]{:S(2)}) copy-start(bf16[2,256,512]{2,1,0:T(8,128)(2,1)S(1)} %project.6.a2_ref) | copy-start | bytes 1572868
  30.2 2.2 %copy-start.14 = (bf16[2,256,512]{2,1,0:T(8,128)(2,1)}, bf16[2,256,512]{2,1,0:T(8,128)(2,1)S(1)}, u32[]{:S(2)}) copy-start(bf16[2,256,512]{2,1,0:T(8,128)(2,1)S(1)} %project.7.b2_ref) | copy-start | bytes 1572868
  30.2 2.2 %collective-permute-start.3 = (bf16[256,1024]{1,0:T(8,128)(2,1)S(1)}, bf16[256,1024]{1,0:T(8,128)(2,1)S(1)}, u32[]{:S(2)}, u32[]{:S(2)}) collective-permute-start(bf16[256,1024]{1,0:T(8,128)(2,1)S(1)} %collective-permute-done.x_ref), channel_id=1, source_target_pairs={{0,1},{1,0},{2,3},{3,2},{4,5},{5,4},{6,7},{7,6},{8,9},{9,8},{10,11... | collective-permute-start | bytes 1572872 | tf_op jit(solution)/shard_map/ppermute | solution.py:404
  32.4 1.6 %copy-start.22 = (f32[3,6,512]{2,1,0:T(8,128)S(1)}, f32[3,6,512]{2,1,0:T(8,128)}, u32[]{:S(2)}) copy-start(f32[3,6,512]{2,1,0:T(8,128)} %tile.12.bias_ref) | copy-start | bytes 110596
  37.6 1.6 %copy-start.6 = (bf16[4,768,512]{2,1,0:T(8,128)(2,1)}, bf16[4,768,512]{2,1,0:T(8,128)(2,1)S(1)}, u32[]{:S(2)}) copy-start(bf16[4,768,512]{2,1,0:T(8,128)(2,1)S(1)} %get-tuple-element.38.own_weight_ref) | copy-start | bytes 9437188
  39.9 1.3 %collective-permute-start.4 = (f32[64,256]{1,0:T(8,128)S(1)}, f32[64,256]{1,0:T(8,128)S(1)}, u32[]{:S(2)}, u32[]{:S(2)}) collective-permute-start(f32[64,256]{1,0:T(8,128)S(1)} %get-tuple-element.29), channel_id=1, source_target_pairs={{0,1},{1,0},{2,3},{3,2},{4,5},{5,4},{6,7},{7,6},{8,9},{9,8},{10,11... | collective-permute-start | bytes 196616 | tf_op jit(solution)/shard_map/ppermute | solution.py:431
  41.2 0.7 copy-start.11
  41.9 14.7 %all-to-all-start = ((bf16[8,64,256]{2,1,0:T(8,128)(2,1)}), bf16[8,64,256]{2,1,0:T(8,128)(2,1)}, u32[]{:S(2)}, u32[]{:S(2)}) async-start(bf16[8,64,256]{2,1,0:T(8,128)(2,1)} %copy-done.11), calls=%async_computation | async-start | bytes 524288 | tf_op jit(solution)/shard_map/all_to_all | solution.py:438
  46.1 1.0 %copy-start.13 = (bf16[2,256,512]{2,1,0:T(8,128)(2,1)S(1)}, bf16[2,256,512]{2,1,0:T(8,128)(2,1)}, u32[]{:S(2)}) copy-start(bf16[2,256,512]{2,1,0:T(8,128)(2,1)} %copy-done.12) | copy-start | bytes 1572868
  47.2 1.0 %copy-start.15 = (bf16[2,256,512]{2,1,0:T(8,128)(2,1)S(1)}, bf16[2,256,512]{2,1,0:T(8,128)(2,1)}, u32[]{:S(2)}) copy-start(bf16[2,256,512]{2,1,0:T(8,128)(2,1)} %copy-done.14) | copy-start | bytes 1572868
  48.2 0.8 copy-start.23
  49.0 7.6 %copy-start.24 = (s32[2048,1]{0,1:T(1,128)S(1)}, s32[2048,1]{0,1:T(1,128)}, u32[]{:S(2)}) copy-start(s32[2048,1]{0,1:T(1,128)} %param.18) | copy-start | bytes 24580
  54.4 1.4 %copy-start.8 = (bf16[4,2,256,512]{3,2,1,0:T(8,128)(2,1)}, bf16[4,2,256,512]{3,2,1,0:T(8,128)(2,1)S(1)}, u32[]{:S(2)}) copy-start(bf16[4,2,256,512]{3,2,1,0:T(8,128)(2,1)S(1)} %get-tuple-element.40.side_weight_ref) | copy-start | bytes 6291460
  55.8 0.8 copy-start.16
  56.6 0.8 %copy-start.20 = (f32[256,64]{0,1:T(8,128)S(1)}, f32[256,64]{0,1:T(8,128)}, u32[]{:S(2)}) copy-start(f32[256,64]{0,1:T(8,128)} %copy.28) | copy-start | bytes 196612
  58.8 1.3 %collective-permute-start.5 = (f32[64,256]{1,0:T(8,128)S(1)}, f32[64,256]{1,0:T(8,128)S(1)}, u32[]{:S(2)}, u32[]{:S(2)}) collective-permute-start(f32[64,256]{1,0:T(8,128)S(1)} %pool.1.resid_a_ref), channel_id=1, source_target_pairs={{0,1},{1,0},{2,3},{3,2},{4,5},{5,4},{6,7},{7,6},{8,9},{9,8},{10,11... | collective-permute-start | bytes 196616 | tf_op jit(solution)/shard_map/ppermute | solution.py:476
  60.1 1.9 %copy-start.3 = (bf16[3,1024,512]{2,1,0:T(8,128)(2,1)S(1)}, bf16[3,1024,512]{2,1,0:T(8,128)(2,1)}, u32[]{:S(2)}) copy-start(bf16[3,1024,512]{2,1,0:T(8,128)(2,1)} %w_ref.11) | copy-start | bytes 9437188
  62.0 1.0 %copy-start.5 = (bf16[256,1024]{1,0:T(8,128)(2,1)S(1)}, bf16[256,1024]{1,0:T(8,128)(2,1)}, u32[]{:S(2)}) copy-start(bf16[256,1024]{1,0:T(8,128)(2,1)} %tokens_ref.3) | copy-start | bytes 1572868
  63.1 1.9 %copy-start.7 = (bf16[4,768,512]{2,1,0:T(8,128)(2,1)S(1)}, bf16[4,768,512]{2,1,0:T(8,128)(2,1)}, u32[]{:S(2)}) copy-start(bf16[4,768,512]{2,1,0:T(8,128)(2,1)} %copy-done.6) | copy-start | bytes 9437188
  65.0 1.6 %copy-start.9 = (bf16[4,2,256,512]{3,2,1,0:T(8,128)(2,1)S(1)}, bf16[4,2,256,512]{3,2,1,0:T(8,128)(2,1)}, u32[]{:S(2)}) copy-start(bf16[4,2,256,512]{3,2,1,0:T(8,128)(2,1)} %copy-done.8) | copy-start | bytes 6291460
  66.6 1.0 %copy-start.10 = (bf16[768,256]{1,0:T(8,128)(2,1)S(1)}, bf16[768,256]{1,0:T(8,128)(2,1)}, u32[]{:S(2)}) copy-start(bf16[768,256]{1,0:T(8,128)(2,1)} %fusion.hot_ref) | copy-start | bytes 1179652
  67.6 1.0 %copy-start.17 = (bf16[4,2,128,256]{3,2,1,0:T(8,128)(2,1)S(1)}, bf16[4,2,128,256]{3,2,1,0:T(8,128)(2,1)}, u32[]{:S(2)}) copy-start(bf16[4,2,128,256]{3,2,1,0:T(8,128)(2,1)} %copy-done.16) | copy-start | bytes 1572868
  68.6 0.9 %copy-start.19 = (bf16[4,128,256]{2,1,0:T(8,128)(2,1)S(1)}, bf16[4,128,256]{2,1,0:T(8,128)(2,1)}, u32[]{:S(2)}) copy-start(bf16[4,128,256]{2,1,0:T(8,128)(2,1)} %copy-done.18) | copy-start | bytes 786436
  77.2 1.7 %collective-permute-start.6 = (bf16[256,640]{1,0:T(8,128)(2,1)S(1)}, bf16[256,640]{1,0:T(8,128)(2,1)S(1)}, u32[]{:S(2)}, u32[]{:S(2)}) collective-permute-start(bf16[256,640]{1,0:T(8,128)(2,1)S(1)} %get-tuple-element.43), channel_id=1, source_target_pairs={{0,1},{1,0},{2,3},{3,2},{4,5},{5,4},{6,7},{7,6},{8,9},{9,8},{10,11... | collective-permute-start | bytes 983048 | tf_op jit(solution)/shard_map/ppermute | solution.py:536
  (1 other events, 0.7 us)

commit v3 on v2

v3 whole, which is shorter than its diff:
```python
import functools
import math

import jax
import jax.numpy as jnp
import numpy as np
from jax import lax
from jax.experimental import pallas as pl
from jax.experimental.pallas import tpu as pltpu
from jax.sharding import PartitionSpec as P

HD = 64
BLK = 128
LIST = 4
PAIR = 2 * HD
GROUP = 2
F32 = jnp.float32
BF16 = jnp.bfloat16
DEAD = 1e30
SCALE = 1.0 / math.sqrt(HD)
KEY_STEP = np.array([[0, 1, -1], [0, 1, 2], [0, -1, -2]], np.int32)
MIB = 1024 * 1024

NN = (((1,), (0,)), ((), ()))
NT = (((1,), (1,)), ((), ()))
TN = (((0,), (0,)), ((), ()))


def dot(a, b, dims, precision=None):
    return lax.dot_general(a, b, dims, precision=precision, preferred_element_type=F32)


def params(*semantics, mib=52):
    return pltpu.CompilerParams(vmem_limit_bytes=mib * MIB, dimension_semantics=semantics or None)


def inverse_root(inputs):
    return 1.0 / jnp.sqrt(jnp.mean(inputs * inputs, axis=-1, keepdims=True) + 1e-05)


def normalise(x_ref, gain_ref):
    inputs = x_ref[...].astype(F32)
    return (inputs * gain_ref[...] * inverse_root(inputs)).astype(BF16)


def project_rows(normed, w_part, part):
    rows = dot(normed, w_part, NN).astype(BF16)
    scale = jnp.where(part == 0, SCALE, 1.0)
    return (rows.astype(F32) * scale).astype(BF16)


def first_kernel(
    place_ref, lists_ref, lengths_ref, ids_ref, w_out_ref, read_ref, targets_ref, x_ref, gain_ref, w_ref,
    bias_ref, hot_ref, mix_ref, own_targets_ref, own_ref, flipped, normed,
):
    part = pl.program_id(0)

    @pl.when(part == 0)
    def _():
        normed[...] = normalise(x_ref, gain_ref)

    own_ref[0] = project_rows(normed[...], w_ref[0], part)

    @pl.when(part == 0)
    def _():
        prepare(
            place_ref, lists_ref, lengths_ref, ids_ref, w_out_ref, read_ref, targets_ref,
            bias_ref, hot_ref, mix_ref, own_targets_ref, flipped,
        )


def prepare(
    place_ref, lists_ref, lengths_ref, ids_ref, w_out_ref, read_ref, targets_ref,
    bias_ref, hot_ref, mix_ref, own_targets_ref, flipped,
):
    seq_index, core, seq_count = place_ref[0], place_ref[1], place_ref[2]
    side = 2 * core - 1
    half_read = own_targets_ref.shape[0]
    panels, tok_rows = hot_ref.shape[0], hot_ref.shape[1] // 3
    per = tok_rows // BLK
    mix = dot(w_out_ref[...], read_ref[...], NN).T
    flip = jnp.concatenate([mix[half_read:], mix[:half_read]], axis=0)
    mix_ref[...] = jnp.where(core == 0, mix, flip).astype(BF16)
    flipped[...] = targets_ref[...].T
    own_targets_ref[...] = flipped[pl.ds(pl.multiple_of(core * half_read, half_read), half_read), :]
    panel = lax.broadcasted_iota(jnp.int32, (panels, tok_rows), 0)
    column = lax.broadcasted_iota(jnp.int32, (1, 2 * tok_rows), 1)
    for t, move in enumerate((0, 1, -1)):
        stretch = seq_index + side * move
        inside = (stretch >= 0) & (stretch < seq_count)
        stretch = jnp.clip(stretch, 0, seq_count - 1)
        ids = ids_ref[:, pl.ds(pl.multiple_of(stretch * tok_rows, tok_rows), tok_rows)]
        hits = (panel == ids) & inside
        hot_ref[:, t * tok_rows : (t + 1) * tok_rows] = jnp.where(hits, 1.0, 0.0).astype(BF16)
        for k in range(3 * per):
            key_block = (seq_index + side * int(KEY_STEP[t, k // per])) * per + k % per
            row = jnp.zeros((1, 2 * tok_rows), F32)
            for b in range(per):
                query_block = stretch * per + b
                live = jnp.logical_not(inside)
                for j in range(LIST):
                    live = live | (
                        (lists_ref[j, query_block] == key_block) & (j < lengths_ref[query_block])
                    )
                off = jnp.where(live, 0.0, DEAD)
                row = jnp.where((column // BLK) % per == b, off, row)
            bias_ref[t, k : k + 1, :] = row


def far_kernel(a2_ref, b2_top_ref, b2_low_ref, gain_ref, w_ref, out_a_ref, out_b_ref, normed):
    rows = a2_ref.shape[0]
    piece = b2_top_ref.shape[0]

    @pl.when(pl.program_id(0) == 0)
    def _():
        normed[:rows] = normalise(a2_ref, gain_ref)
        normed[rows : rows + piece] = normalise(b2_top_ref, gain_ref)
        normed[rows + piece :] = normalise(b2_low_ref, gain_ref)

    both = dot(normed[...], w_ref[0], NN).astype(BF16)
    out_a_ref[0] = both[:rows]
    out_b_ref[0] = both[rows:]


def pair_cols(p):
    return slice(p * PAIR, (p + 1) * PAIR)


def two_heads(tile):
    lane = lax.broadcasted_iota(jnp.int32, tile.shape, 1)
    zero = jnp.zeros_like(tile)
    return jnp.concatenate(
        [jnp.where(lane < HD, tile, zero), jnp.where(lane >= HD, tile, zero)], axis=0
    )


def fold_heads(pair_t):
    half = pair_t.shape[1] // 2
    return jnp.concatenate([pair_t[:HD, :half], pair_t[HD:, half:]], axis=0)


def soften(bias_ref, stretch, scores):
    count = scores.shape[0] // BLK
    blocks = [scores[k * BLK : (k + 1) * BLK] for k in range(count)]
    biases = [bias_ref[stretch, k : k + 1, :] for k in range(count)]
    tops = [jnp.max(b, axis=0, keepdims=True) - d for b, d in zip(blocks, biases)]
    top = functools.reduce(jnp.maximum, tops)
    expo = [jnp.exp(b - (top + d)) for b, d in zip(blocks, biases)]
    total = functools.reduce(jnp.add, [jnp.sum(e, axis=0, keepdims=True) for e in expo])
    inverse = 1.0 / total
    return jnp.concatenate([(e * inverse).astype(BF16) for e in expo], axis=0)


def near_kernel(
    steps, bias_ref, own_ref, mix_ref, a1x_ref, b1x_ref, gain_ref, w_ref,
    a1_ref, b1_ref, weight_ref, att_ref, keep_ref, send_ref, normed, read,
):
    step = pl.program_id(0)
    rows = own_ref.shape[1]

    @pl.when(step == 0)
    def _():
        read[...] = jnp.zeros_like(read)
        normed[:rows] = normalise(a1x_ref, gain_ref)
        normed[rows:] = normalise(b1x_ref, gain_ref)

    near = {}
    for c in (1, 2, 0):
        near[c] = project_rows(normed[...], w_ref[c], c)
        a1_ref[c] = near[c][:rows]
        b1_ref[c] = near[c][rows:]
    scores = []
    for p in range(GROUP):
        keys = jnp.concatenate([own_ref[1, :, pair_cols(p)], near[1][:, pair_cols(p)]], axis=0)
        scores.append(dot(keys, two_heads(own_ref[0, :, pair_cols(p)]), NT))
    weights = []
    for p in range(GROUP):
        weights.append(soften(bias_ref, 0, scores[p]))
        weight_ref[p] = weights[p]
    attended = []
    for p in range(GROUP):
        values = jnp.concatenate([own_ref[2, :, pair_cols(p)], near[2][:, pair_cols(p)]], axis=0)
        attended.append(fold_heads(dot(values, weights[p], TN)).astype(BF16))
        att_ref[p] = attended[p]
    read[...] += dot(mix_ref[...], jnp.concatenate(attended, axis=0), NN)

    @pl.when(step == steps - 1)
    def _():
        half = read.shape[0] // 2
        keep_ref[...] = read[:half]
        send_ref[...] = read[half:]


def side_kernel(bias_ref, own_ref, a1_ref, b1_ref, a2_ref, b2_ref, weight_ref, att_ref):
    own_rows = own_ref.shape[1]
    jobs = [(p, side) for p in range(GROUP) for side in range(2)]
    near, far = (a1_ref, b1_ref), (a2_ref, b2_ref)

    def stack(p, side, part):
        cols = pair_cols(p)
        return jnp.concatenate(
            [own_ref[part, :, cols], near[side][part, :, cols], far[side][part - 1, :, cols]],
            axis=0,
        )

    scores = [
        dot(stack(p, side, 1), two_heads(near[side][0, :, pair_cols(p)]), NT) for p, side in jobs
    ]
    weights = []
    for (p, side), score in zip(jobs, scores):
        weights.append(soften(bias_ref, 1 + side, score))
        weight_ref[p, side] = weights[-1][:own_rows]
    for (p, side), weight in zip(jobs, weights):
        att_ref[p, side] = fold_heads(dot(stack(p, side, 2), weight, TN)).astype(BF16)


def spread_kernel(keep_ref, got_ref, out_ref):
    rows = (keep_ref[...] + got_ref[...]).astype(BF16)
    for s in range(out_ref.shape[0]):
        out_ref[s] = rows


def pool_kernel(steps, rows_ref, ids_ref, targets_ref, out_ref, counts_ref, sums):
    step = pl.program_id(0)
    half_read, panels = out_ref.shape
    count, _, tok_rows = rows_ref.shape

    @pl.when(step == 0)
    def _():
        sums[...] = jnp.zeros_like(sums)

    panel = lax.broadcasted_iota(jnp.int32, (panels, count * tok_rows), 0)
    hits = jnp.where(panel == ids_ref[...], 1.0, 0.0).astype(BF16)
    rows = jnp.concatenate([rows_ref[s] for s in range(count)], axis=1)
    rows = jnp.concatenate([rows, jnp.ones((16, count * tok_rows), BF16)], axis=0)
    sums[...] += dot(rows, hits, NT)

    @pl.when(step == steps - 1)
    def _():
        counts = sums[half_read : half_read + 1]
        out_ref[...] = sums[:half_read] / counts - targets_ref[...]
        counts_ref[...] = counts


def back_kernel(
    core_ref, resid_a_ref, resid_b_ref, counts_ref, hot_ref, mix_ref, gain_ref, *refs
):
    sources, (keep_ref, send_ref, stat_ref, loss_ref) = refs[:9], refs[9:13]
    buffers, arrived = refs[13:22], refs[22]
    copies = [
        pltpu.make_async_copy(source, buffer, arrived.at[n])
        for n, (source, buffer) in enumerate(zip(sources, buffers))
    ]
    for copy in copies:
        copy.start()
    own_ref, a1_ref, b1_ref, own_att_ref, side_att_ref, own_w_ref, side_w_ref, w_ref, tokens_ref = buffers
    own_rows = own_ref.shape[1]
    pairs = own_ref.shape[2] // PAIR
    residual = jnp.concatenate([resid_a_ref[...], resid_b_ref[...]], axis=0)
    loss_ref[...] = jnp.broadcast_to(
        jnp.sum(counts_ref[...] * residual * residual, keepdims=True), loss_ref.shape
    )
    panel_grad = dot(mix_ref[...].astype(F32), residual, TN, lax.Precision.HIGHEST).astype(BF16)
    out_grad = dot(panel_grad, hot_ref[...], NN).astype(BF16)
    stretches = (own_ref, a1_ref, b1_ref)

    def tile_of(p, t):
        return out_grad[pair_cols(p), t * own_rows : (t + 1) * own_rows]

    def open_pair(p):
        values = jnp.concatenate([r[2, :, pair_cols(p)] for r in stretches], axis=0)
        grads, changes = [], []
        for t in range(3):
            tile = tile_of(p, t)
            none = jnp.zeros((HD, own_rows), BF16)
            grads.append(
                jnp.concatenate(
                    [
                        jnp.concatenate([tile[:HD], none], axis=0),
                        jnp.concatenate([none, tile[HD:]], axis=0),
                    ],
                    axis=1,
                )
            )
            changes.append(dot(values if t == 0 else values[:own_rows], grads[t], NN))
        return grads, changes

    def score_pair(p, changes):
        scores = []
        for t in range(3):
            attended = own_att_ref[p] if t == 0 else side_att_ref[p, t - 1]
            product = tile_of(p, t).astype(F32) * attended.astype(F32)
            delta = jnp.concatenate(
                [
                    jnp.sum(product[:HD], axis=0, keepdims=True),
                    jnp.sum(product[HD:], axis=0, keepdims=True),
                ],
                axis=1,
            )
            weight = own_w_ref[p] if t == 0 else side_w_ref[p, t - 1]
            scores.append((weight.astype(F32) * (changes[t] - delta)).astype(BF16))
        return scores

    def close_pair(p, grads, scores):
        keys = jnp.concatenate([r[1, :, pair_cols(p)] for r in stretches], axis=0)
        grad_query = fold_heads(dot(keys, scores[0], TN)) * SCALE
        queries = jnp.concatenate([two_heads(r[0, :, pair_cols(p)]) for r in stretches], axis=0)
        own_scores = jnp.concatenate([s[:own_rows] for s in scores], axis=1)
        grad_key = dot(own_scores, queries, NN)
        own_weights = jnp.concatenate(
            [own_w_ref[p, :own_rows], side_w_ref[p, 0], side_w_ref[p, 1]], axis=1
        )
        grad_value = dot(own_weights, jnp.concatenate(grads, axis=1), NT)
        return grad_query.T.astype(BF16), grad_key.astype(BF16), grad_value.astype(BF16)

    for copy in copies[:3]:
        copy.wait()
    opened = open_pair(0)
    for copy in copies[3:7]:
        copy.wait()
    grad_proj = []
    for p in range(pairs):
        grads, changes = opened
        if p + 1 < pairs:
            opened = open_pair(p + 1)
        grad_proj.append(close_pair(p, grads, score_pair(p, changes)))
    flat = jnp.concatenate([grad_proj[p][c] for c in range(3) for p in range(pairs)], axis=1)
    for copy in copies[7:]:
        copy.wait()
    half = keep_ref.shape[1]
    inputs = tokens_ref[...].astype(F32)
    scaled = inputs * gain_ref[...]
    row_sum = jnp.zeros((own_rows, 1), F32)
    parts = []
    for h in range(2):
        rows = slice(h * half, (h + 1) * half)
        w_part = jnp.concatenate([w_ref[c, rows, :] for c in range(3)], axis=1)
        parts.append(dot(flat, w_part, NT))
        row_sum += jnp.sum(scaled[:, rows] * parts[h], axis=-1, keepdims=True)
    first = core_ref[0] == 0
    keep_ref[...] = jnp.where(first, parts[0], parts[1])
    send_ref[:, :half] = jnp.where(first, parts[1], parts[0]).astype(BF16)
    high = row_sum.astype(BF16).astype(F32)
    lane = lax.broadcasted_iota(jnp.int32, (own_rows, BLK), 1)
    send_ref[:, half:] = jnp.where(lane < HD, high, row_sum - high).astype(BF16)
    stat_ref[...] = jnp.where(lane < HD, row_sum, inverse_root(inputs))


def final_kernel(core_ref, keep_ref, got_ref, stat_ref, tokens_ref, gain_ref, out_ref):
    half = keep_ref.shape[1]
    cols = pl.ds(pl.multiple_of(core_ref[0] * half, half), half)
    got_sum = got_ref[:, half : half + 1].astype(F32) + got_ref[:, half + HD : half + HD + 1].astype(F32)
    row_sum = stat_ref[:, :1] + got_sum
    inverse = stat_ref[:, HD : HD + 1]
    grad_normed = keep_ref[...] + got_ref[:, :half].astype(F32)
    shrink = row_sum * (inverse * inverse * inverse) * (0.5 / half)
    out_ref[...] = (
        gain_ref[:, cols] * grad_normed * inverse - tokens_ref[:, cols].astype(F32) * shrink
    )


def pair_spec(parts, rows):
    return pl.BlockSpec((parts, rows, GROUP * PAIR), lambda p: (0, 0, p))


def whole_spec(shape):
    return pl.BlockSpec(shape, lambda p: (0,) * len(shape))


def lead_spec(shape):
    return pl.BlockSpec((GROUP,) + shape, lambda p: (p,) + (0,) * len(shape))


SMEM_SPEC = pl.BlockSpec(memory_space=pltpu.SMEM)


def local(
    tokens, norm_gain, w_qkv, w_out, readout_weight, targets, key_blocks, list_len, voxel_panel
):
    tok_rows, width = tokens.shape
    cols = w_qkv.shape[2]
    pairs = cols // PAIR
    steps = pairs // GROUP
    panels, readout = targets.shape
    half_read = readout // 2
    half_width = width // 2
    seq_count = lax.axis_size("seq")
    seq_index = lax.axis_index("seq")
    core = lax.axis_index("head")
    side_step = 2 * core - 1
    all_tokens = voxel_panel.shape[0]
    per = tok_rows // BLK
    core_swap = [(0, 1), (1, 0)]

    def shifted(far):
        return [
            (2 * s, 2 * (s + far)) for s in range(seq_count - far)
        ] + [(2 * (s + far) + 1, 2 * s + 1) for s in range(seq_count - far)]

    a1_tokens = lax.ppermute(tokens, ("seq", "head"), shifted(1))
    a2_tokens = lax.ppermute(tokens, ("seq", "head"), shifted(2))

    gain = norm_gain.reshape(1, width)
    flat_ids = voxel_panel.reshape(1, all_tokens)
    place = jnp.stack([seq_index, core, jnp.int32(seq_count)]).astype(jnp.int32)
    vmem = pl.BlockSpec(memory_space=pltpu.VMEM)
    whole_tokens = whole_spec((tok_rows, width))
    whole_gain = whole_spec((1, width))
    bias_spec = whole_spec((3, 3 * per, 2 * tok_rows))
    bias, hot, mix, own_targets, own = pl.pallas_call(
        first_kernel,
        grid=(3,),
        in_specs=[SMEM_SPEC] * 3
        + [
            whole_spec((1, all_tokens)),
            whole_spec(w_out.shape),
            whole_spec(readout_weight.shape),
            whole_spec(targets.shape),
            whole_tokens,
            whole_gain,
            pl.BlockSpec((1, width, cols), lambda c: (c, 0, 0)),
        ],
        out_specs=[
            bias_spec,
            whole_spec((panels, 3 * tok_rows)),
            whole_spec((readout, cols)),
            whole_spec((half_read, panels)),
            pl.BlockSpec((1, tok_rows, cols), lambda c: (c, 0, 0)),
        ],
        out_shape=[
            jax.ShapeDtypeStruct((3, 3 * per, 2 * tok_rows), F32),
            jax.ShapeDtypeStruct((panels, 3 * tok_rows), BF16),
            jax.ShapeDtypeStruct((readout, cols), BF16),
            jax.ShapeDtypeStruct((half_read, panels), F32),
            jax.ShapeDtypeStruct((3, tok_rows, cols), BF16),
        ],
        scratch_shapes=[pltpu.VMEM((readout, panels), F32), pltpu.VMEM((tok_rows, width), BF16)],
        compiler_params=params("arbitrary", mib=60),
        cost_estimate=pl.CostEstimate(flops=2**31, bytes_accessed=6 * MIB, transcendentals=0),
        name="first",
    )(
        place, key_blocks.T, list_len, flat_ids, w_out, readout_weight, targets, tokens, gain, w_qkv
    )

    a2_tokens, own = lax.optimization_barrier((a2_tokens, own))
    piece = tok_rows // 2
    b2_top = lax.ppermute(a2_tokens[:piece], "head", core_swap)
    b2_low = lax.ppermute(a2_tokens[piece:], "head", core_swap)
    a2, b2 = pl.pallas_call(
        far_kernel,
        grid=(2,),
        in_specs=[
            whole_tokens,
            whole_spec((piece, width)),
            whole_spec((piece, width)),
            whole_gain,
            pl.BlockSpec((1, width, cols), lambda c: (c + 1, 0, 0)),
        ],
        out_specs=[pl.BlockSpec((1, tok_rows, cols), lambda c: (c, 0, 0))] * 2,
        out_shape=[jax.ShapeDtypeStruct((2, tok_rows, cols), BF16)] * 2,
        scratch_shapes=[pltpu.VMEM((2 * tok_rows, width), BF16)],
        compiler_params=params("arbitrary"),
        cost_estimate=pl.CostEstimate(flops=2**20, bytes_accessed=4 * MIB, transcendentals=0),
        name="far",
    )(a2_tokens, b2_top, b2_low, gain, w_qkv)

    a1_tokens, own, a2, b2, mix, own_targets, hot, bias = lax.optimization_barrier(
        (a1_tokens, own, a2, b2, mix, own_targets, hot, bias)
    )
    b1_tokens = lax.ppermute(a1_tokens, "head", core_swap)
    mix_spec = pl.BlockSpec((readout, GROUP * PAIR), lambda p: (0, p))
    a1, b1, own_weight, own_att, read_keep, read_send = pl.pallas_call(
        functools.partial(near_kernel, steps),
        grid=(steps,),
        in_specs=[
            bias_spec,
            pair_spec(3, tok_rows),
            mix_spec,
            whole_tokens,
            whole_tokens,
            whole_gain,
            pair_spec(3, width),
        ],
        out_specs=[
            pair_spec(3, tok_rows),
            pair_spec(3, tok_rows),
            lead_spec((3 * tok_rows, 2 * tok_rows)),
            lead_spec((PAIR, tok_rows)),
            whole_spec((half_read, tok_rows)),
            whole_spec((half_read, tok_rows)),
        ],
        out_shape=[
            jax.ShapeDtypeStruct((3, tok_rows, cols), BF16),
            jax.ShapeDtypeStruct((3, tok_rows, cols), BF16),
            jax.ShapeDtypeStruct((pairs, 3 * tok_rows, 2 * tok_rows), BF16),
            jax.ShapeDtypeStruct((pairs, PAIR, tok_rows), BF16),
            jax.ShapeDtypeStruct((half_read, tok_rows), F32),
            jax.ShapeDtypeStruct((half_read, tok_rows), F32),
        ],
        scratch_shapes=[
            pltpu.VMEM((2 * tok_rows, width), BF16),
            pltpu.VMEM((readout, tok_rows), F32),
        ],
        compiler_params=params("arbitrary"),
        name="near",
    )(bias, own, mix, a1_tokens, b1_tokens, gain, w_qkv)

    read_got = lax.ppermute(read_send, "head", core_swap)
    spread = pl.pallas_call(
        spread_kernel,
        out_shape=jax.ShapeDtypeStruct((seq_count, half_read, tok_rows), BF16),
        compiler_params=params(),
        name="spread",
    )(read_keep, read_got)
    all_rows = lax.all_to_all(spread, "seq", 0, 0)

    side_weight, side_att = pl.pallas_call(
        side_kernel,
        grid=(steps,),
        in_specs=[bias_spec] + [pair_spec(3, tok_rows)] * 3 + [pair_spec(2, tok_rows)] * 2,
        out_specs=[lead_spec((2, tok_rows, 2 * tok_rows)), lead_spec((2, PAIR, tok_rows))],
        out_shape=[
            jax.ShapeDtypeStruct((pairs, 2, tok_rows, 2 * tok_rows), BF16),
            jax.ShapeDtypeStruct((pairs, 2, PAIR, tok_rows), BF16),
        ],
        compiler_params=params("arbitrary"),
        cost_estimate=pl.CostEstimate(
            flops=pairs * 4 * 2 * 2 * 768 * 256 * 128,
            bytes_accessed=8 * MIB,
            transcendentals=pairs * 4 * 768 * 256,
        ),
        name="attend_sides",
    )(bias, own, a1, b1, a2, b2)
    all_rows, side_weight, side_att = lax.optimization_barrier((all_rows, side_weight, side_att))

    batch = min(seq_count, 8)
    pool_steps = seq_count // batch
    resid_a, counts = pl.pallas_call(
        functools.partial(pool_kernel, pool_steps),
        grid=(pool_steps,),
        in_specs=[
            pl.BlockSpec((batch, half_read, tok_rows), lambda s: (s, 0, 0)),
            pl.BlockSpec((1, batch * tok_rows), lambda s: (0, s)),
            whole_spec((half_read, panels)),
        ],
        out_specs=[whole_spec((half_read, panels)), whole_spec((1, panels))],
        out_shape=[
            jax.ShapeDtypeStruct((half_read, panels), F32),
            jax.ShapeDtypeStruct((1, panels), F32),
        ],
        scratch_shapes=[pltpu.VMEM((half_read + 16, panels), F32)],
        compiler_params=params("arbitrary"),
        name="pool",
    )(all_rows, flat_ids, own_targets)
    resid_b = lax.ppermute(resid_a, "head", core_swap)

    core_index = place[1:2]
    sources = (own, a1, b1, own_att, side_att, own_weight, side_weight, w_qkv, tokens)
    keep, send, stats, loss = pl.pallas_call(
        back_kernel,
        in_specs=[SMEM_SPEC] + [vmem] * 6 + [pl.BlockSpec(memory_space=pl.ANY)] * len(sources),
        out_specs=[vmem] * 4,
        out_shape=[
            jax.ShapeDtypeStruct((tok_rows, half_width), F32),
            jax.ShapeDtypeStruct((tok_rows, half_width + BLK), BF16),
            jax.ShapeDtypeStruct((tok_rows, BLK), F32),
            jax.ShapeDtypeStruct((1, BLK), F32),
        ],
        scratch_shapes=[pltpu.VMEM(a.shape, a.dtype) for a in sources]
        + [pltpu.SemaphoreType.DMA((len(sources),))],
        compiler_params=params(),
        name="back",
    )(core_index, resid_a, resid_b, counts, hot, mix, gain, *sources)
    got = lax.ppermute(send, "head", core_swap)
    loss_mean = 0.5 * loss[0, :1] / (all_tokens * readout)
    gradient = pl.pallas_call(
        final_kernel,
        in_specs=[SMEM_SPEC] + [pl.BlockSpec(memory_space=pltpu.VMEM)] * 5,
        out_shape=jax.ShapeDtypeStruct((tok_rows, half_width), F32),
        compiler_params=params(),
        name="final",
    )(core_index, keep, got, stats, tokens, gain)
    return (gradient, loss_mean)


def solution(mesh):
    return jax.shard_map(
        local,
        mesh=mesh,
        in_specs=(
            P(("groups", "seq"), None),
            P(),
            P(None, None, "head"),
            P("head", None),
            P(),
            P("groups", None),
            P("groups", None),
            P("groups"),
            P("groups", None),
        ),
        out_specs=(P(("groups", "seq"), "head"), P("groups")),
        check_vma=False,
    )
```

time: 82.1 us -> 63.5 us (0.77)
  local copies, waits for them, and re-layouts: 26.8 us -> 0.86 us
  Pallas kernels: 28.3 us -> 35.6 us
  waiting for transfers between devices: 3.34 us -> 8.9 us
  other arithmetic: 3.83 us -> 0.59 us
  matrix products: 1.44 us -> 0 us
    unnamed x51 -> x18, local copies, waits for them, and re-layouts: 22.8 us -> 0.82 us
    pallas_call x7 -> x4, Pallas kernels: 20.5 us -> 26.2 us  [the longest x1 8.64 us: local(): pl.pallas_call(back_kernel, in_specs=[SMEM_SPEC] + [vmem] * 6 + [pl.Block...]
    dynamic_slice x5 -> x0, local copies, waits for them, and re-layouts: 2.14 us -> none  [the longest x4 1.14 us: stretch_rows(): return lax.dynamic_slice_in_dim(array, start, rows, 0)]
    ppermute x1, waiting for transfers between devices: 0.01 us -> 1.91 us  [local(): b1_tokens = lax.ppermute(a1_tokens, 'head', core_swap)]
    pallas_call x1, Pallas kernels: 5.4 us -> 7.23 us  [local(): pl.pallas_call(side_kernel, grid=(steps,), in_specs=[bias_spec] + [pair_s...]
    all_to_all x1, starting transfers between devices: 4.22 us -> 5.78 us  [local(): all_rows = lax.all_to_all(spread, 'seq', 0, 0)]
    another operation x4 -> x0, local copies, waits for them, and re-layouts: 1.53 us -> none  [the longest x1 0.85 us: local(): lengths = jnp.stack([stretch_rows(list_len, o, per) for o in offsets])]
    dot_general x1 -> x0, matrix products: 1.44 us -> none  [local(): jnp.dot(readout_weight.T, w_out.T, preferred_element_type=F32).astype(BF16)]
  transfers between devices with their start and end apart: 8 -> 9, of which waited for: 3 -> 8; matrix products, arithmetic and copies ran while one was open for 12% -> 1% of each run, Pallas kernels for 16% -> 26%
where the time goes in v3:
time: 63.5 us; the launch traced here: 63.1 us
  Pallas kernels  35.6 us (56%)
  starting transfers between devices  15.2 us (24%)
  waiting for transfers between devices  8.9 us (14%)
  between operations  1.92 us (3%)
  local copies, waits for them, and re-layouts  0.86 us (1%)
    pallas_call x1, Pallas kernels, local(): pl.pallas_call(back_kernel, in_specs=[SMEM_SPEC] + [vmem] * 6 + [pl.Block...  8.64 us
    pallas_call x1, Pallas kernels, local(): pl.pallas_call(functools.partial(near_kernel, steps), grid=(steps,), in_s...  8.22 us
    pallas_call x1, Pallas kernels, local(): pl.pallas_call(side_kernel, grid=(steps,), in_specs=[bias_spec] + [pair_s...  7.23 us
    pallas_call x1, Pallas kernels, local(): pl.pallas_call(first_kernel, grid=(3,), in_specs=[SMEM_SPEC] * 3 + [whole...  6.04 us
    all_to_all x1, starting transfers between devices, local(): all_rows = lax.all_to_all(spread, 'seq', 0, 0)  5.78 us
    ppermute x1, starting transfers between devices, local(): a2_tokens = lax.ppermute(tokens, ('seq', 'head'), shifted(2))  4.96 us
    ppermute x1, starting transfers between devices, local(): a1_tokens = lax.ppermute(tokens, ('seq', 'head'), shifted(1))  3.46 us
    pallas_call x1, Pallas kernels, local(): pl.pallas_call(far_kernel, grid=(2,), in_specs=[whole_tokens, whole_spec(...  3.29 us
  transfers between devices with their start and end apart: 9, of which 8 were waited for; matrix products, arithmetic and copies ran while one was open for 1% of the time, Pallas kernels for 26%

profile of v3, /device:TPU:0, one launch (start us, length us, event | category | flops | bytes accessed | tf_op | source)
XLA Modules:
  0.0 63.1 jit_solution(3038232200990222611)
XLA Ops:
  0.6 5.0 %collective-permute-start.1 = (bf16[256,1024]{1,0:T(8,128)(2,1)}, bf16[256,1024]{1,0:T(8,128)(2,1)S(1)}, u32[]{:S(2)}, u32[]{:S(2)}) collective-permute-start(bf16[256,1024]{1,0:T(8,128)(2,1)} %tokens_ref.1), channel_id=1, source_target_pairs={{0,4},{2,6},{4,8},{6,10},{8,12},{10,14},{5,1},{7,3},{9,5},{11,7},{... | collective-permute-start | bytes 1572872 | tf_op jit(solution)/shard_map/ppermute | solution.py:401
  5.6 3.5 %collective-permute-start = (bf16[256,1024]{1,0:T(8,128)(2,1)}, bf16[256,1024]{1,0:T(8,128)(2,1)S(1)}, u32[]{:S(2)}, u32[]{:S(2)}) collective-permute-start(bf16[256,1024]{1,0:T(8,128)(2,1)} %tokens_ref.1), channel_id=1, source_target_pairs={{0,2},{2,4},{4,6},{6,8},{8,10},{10,12},{12,14},{3,1},{5,3},{7,5},{... | collective-permute-start | bytes 1572872 | tf_op jit(solution)/shard_map/ppermute | solution.py:400
  9.1 0.6 pad_add_fusion.place_ref
  9.7 6.0 %first.1 = (f32[3,6,512]{2,1,0:T(8,128)}, bf16[256,768]{1,0:T(8,128)(2,1)}, bf16[128,512]{1,0:T(8,128)(2,1)}, f32[64,256]{1,0:T(8,128)}, bf16[3,256,512]{2,1,0:T(8,128)(2,1)}) custom-call(s32[3]{0:T(128)} %pad_add_fusion.place_ref, s32[4,16]{1,0:T(4,128)} %bitcast.15, s32[16]{0:T(128)} %lengths_ref.1, s32[1,2048]{1,0:T(1,128)} %bitcast.12, ...), custom_call_target="tpu_custom_call" | custom-call | flops 2147483648 | bytes 6291456 | tf_op jit(solution)/shard_map/first/pallas_call | solution.py:410
  15.7 0.0 copy-start.6
  15.7 0.0 collective-permute-done.1.a2_ref
  15.7 0.0 copy-start.8
  15.8 0.1 collective-permute-start.2
  15.9 0.5 collective-permute-start.3
  16.4 1.0 %collective-permute-done.2.b2_top_ref = bf16[128,1024]{1,0:T(8,128)(2,1)S(1)} collective-permute-done((bf16[128,1024]{1,0:T(8,128)(2,1)S(1)}, bf16[128,1024]{1,0:T(8,128)(2,1)S(1)}, u32[]{:S(2)}, u32[]{:S(2)}) %collective-permute-start.2) | collective-permute-done | bytes 262176 | tf_op jit(solution)/shard_map/ppermute | solution.py:447
  17.4 0.4 collective-permute-done.3.b2_low_ref
  17.8 0.0 copy-done.5
  17.8 3.3 %far.1 = (bf16[2,256,512]{2,1,0:T(8,128)(2,1)S(1)}, bf16[2,256,512]{2,1,0:T(8,128)(2,1)S(1)}) custom-call(bf16[256,1024]{1,0:T(8,128)(2,1)} %copy-done.8, bf16[128,1024]{1,0:T(8,128)(2,1)S(1)} %collective-permute-done.2.b2_top_ref, bf16[128,1024]{1,0:T(8,128)(2,1)S(1)} %collective-permute-done.3.b2_low_ref, f32[1,1024]{1,0:T(1,128)S(1)} %bitcast.8, ...), custom_call_target="tpu_custom_call" | custom-call | flops 1048576 | bytes 4194304 | tf_op jit(solution)/shard_map/far/pallas_call | solution.py:449
  21.1 0.6 collective-permute-done.a1x_ref
  21.6 0.0 collective-permute-start.4
  21.7 1.9 %collective-permute-done.4.b1x_ref = bf16[256,1024]{1,0:T(8,128)(2,1)S(1)} collective-permute-done((bf16[256,1024]{1,0:T(8,128)(2,1)S(1)}, bf16[256,1024]{1,0:T(8,128)(2,1)S(1)}, u32[]{:S(2)}, u32[]{:S(2)}) %collective-permute-start.4) | collective-permute-done | bytes 524320 | tf_op jit(solution)/shard_map/ppermute | solution.py:470
  23.6 8.2 %near.1 = (bf16[3,256,512]{2,1,0:T(8,128)(2,1)}, bf16[3,256,512]{2,1,0:T(8,128)(2,1)}, bf16[4,768,512]{2,1,0:T(8,128)(2,1)}, bf16[4,128,256]{2,1,0:T(8,128)(2,1)...) custom-call(f32[3,6,512]{2,1,0:T(8,128)S(1)} %copy-done.6, bf16[3,256,512]{2,1,0:T(8,128)(2,1)} %get-tuple-element.46.own_ref.refs_0_, ...), custom_call_target="tpu_custom_call" | custom-call | tf_op jit(solution)/shard_map/near/pallas_call | solution.py:472
  31.8 0.1 collective-permute-start.5
  31.9 1.1 %collective-permute-done.5.got_ref = f32[64,256]{1,0:T(8,128)S(1)} collective-permute-done((f32[64,256]{1,0:T(8,128)S(1)}, f32[64,256]{1,0:T(8,128)S(1)}, u32[]{:S(2)}, u32[]{:S(2)}) %collective-permute-start.5) | collective-permute-done | bytes 65568 | tf_op jit(solution)/shard_map/ppermute | solution.py:508
  33.0 0.7 %spread.1 = bf16[8,64,256]{2,1,0:T(8,128)(2,1)} custom-call(f32[64,256]{1,0:T(8,128)S(1)} %get-tuple-element.49.keep_ref, f32[64,256]{1,0:T(8,128)S(1)} %collective-permute-done.5.got_ref), custom_call_target="tpu_custom_call" | custom-call | tf_op jit(solution)/shard_map/spread/pallas_call | solution.py:509
  33.8 5.8 %all-to-all-start = ((bf16[8,64,256]{2,1,0:T(8,128)(2,1)}), bf16[8,64,256]{2,1,0:T(8,128)(2,1)S(1)}, u32[]{:S(2)}, u32[]{:S(2)}) async-start(bf16[8,64,256]{2,1,0:T(8,128)(2,1)} %spread.1), calls=%async_computation | async-start | bytes 524288 | tf_op jit(solution)/shard_map/all_to_all | solution.py:515
  39.6 7.2 %attend_sides.1 = (bf16[4,2,256,512]{3,2,1,0:T(8,128)(2,1)}, bf16[4,2,128,256]{3,2,1,0:T(8,128)(2,1)S(1)}) custom-call(f32[3,6,512]{2,1,0:T(8,128)S(1)} %copy-done.6, bf16[3,256,512]{2,1,0:T(8,128)(2,1)} %get-tuple-element.46.own_ref.refs_0_, bf16[3,256,512]{2,1,0:T(8,128)(2,1)} %get-tuple-element.51.a1_ref.refs_1_, ...), custom_call_target="tpu_custom_call" | custom-call | flops 1610612736 | bytes 8388608 | tf_op jit(solution)/shard_map/attend_sides/pallas_call | solution.py:517
  46.8 0.8 %copy-done.2 = bf16[4,2,128,256]{3,2,1,0:T(8,128)(2,1)} copy-done((bf16[4,2,128,256]{3,2,1,0:T(8,128)(2,1)}, bf16[4,2,128,256]{3,2,1,0:T(8,128)(2,1)S(1)}, u32[]{:S(2)}) %copy-start.2) | copy-done | bytes 524312
  47.6 1.2 %all-to-all-done.rows_ref = bf16[8,64,256]{2,1,0:T(8,128)(2,1)S(1)} async-done(((bf16[8,64,256]{2,1,0:T(8,128)(2,1)}), bf16[8,64,256]{2,1,0:T(8,128)(2,1)S(1)}, u32[]{:S(2)}, u32[]{:S(2)}) %all-to-all-start) | async-done | bytes 262176 | tf_op jit(solution)/shard_map/all_to_all | solution.py:515
  48.8 0.5 pool.1
  49.3 0.1 collective-permute-start.6
  49.4 1.2 %collective-permute-done.6.resid_b_ref = f32[64,256]{1,0:T(8,128)S(1)} collective-permute-done((f32[64,256]{1,0:T(8,128)S(1)}, f32[64,256]{1,0:T(8,128)S(1)}, u32[]{:S(2)}, u32[]{:S(2)}) %collective-permute-start.6) | collective-permute-done | bytes 65568 | tf_op jit(solution)/shard_map/ppermute | solution.py:555
  50.6 8.6 %back.1 = (f32[256,512]{1,0:T(8,128)S(1)}, bf16[256,640]{1,0:T(8,128)(2,1)S(1)}, f32[256,128]{1,0:T(8,128)S(1)}, f32[1,128]{1,0:T(1,128)S(1)}) custom-call(s32[1]{0:T(128)} %bitcast.core_ref, f32[64,256]{1,0:T(8,128)S(1)} %get-tuple-element.59.resid_a_ref, f32[64,256]{1,0:T(8,128)S(1)} %collective-permute-done.6.resid_b_ref, ...), custom_call_target="tpu_custom_call" | custom-call | tf_op jit(solution)/shard_map/back/pallas_call | solution.py:559
  59.3 0.2 collective-permute-start.7
  59.5 1.4 %collective-permute-done.7.got_ref = bf16[256,640]{1,0:T(8,128)(2,1)S(1)} collective-permute-done((bf16[256,640]{1,0:T(8,128)(2,1)S(1)}, bf16[256,640]{1,0:T(8,128)(2,1)S(1)}, u32[]{:S(2)}, u32[]{:S(2)}) %collective-permute-start.7) | collective-permute-done | bytes 327712 | tf_op jit(solution)/shard_map/ppermute | solution.py:574
  60.9 0.0 copy-done
  60.9 1.0 %final.1 = f32[256,512]{1,0:T(8,128)} custom-call(s32[1]{0:T(128)} %bitcast.core_ref, f32[256,512]{1,0:T(8,128)S(1)} %get-tuple-element.66.keep_ref, bf16[256,640]{1,0:T(8,128)(2,1)S(1)} %collective-permute-done.7.got_ref, f32[256,128]{1,0:T(8,128)S(1)} %get-tuple-element.68.stat_ref, bf16[256,1024]{1,0:T(8,128)(2,1)S(1)} %copy-done, f32[1,1024]{1,0:T(1,128)S(1)} %bitcast.11), custom_call_target="tpu_custom_call" | custom-call | tf_op jit(solution)/shard_map/final/pallas_call | solution.py:576
  (14 shorter events, 0.1 us)
Async XLA Ops:
  0.6 15.1 %collective-permute-start.1 = (bf16[256,1024]{1,0:T(8,128)(2,1)}, bf16[256,1024]{1,0:T(8,128)(2,1)S(1)}, u32[]{:S(2)}, u32[]{:S(2)}) collective-permute-start(bf16[256,1024]{1,0:T(8,128)(2,1)} %tokens_ref.1), channel_id=1, source_target_pairs={{0,4},{2,6},{4,8},{6,10},{8,12},{10,14},{5,1},{7,3},{9,5},{11,7},{... | collective-permute-start | bytes 1572872 | tf_op jit(solution)/shard_map/ppermute | solution.py:401
  5.6 16.0 %collective-permute-start = (bf16[256,1024]{1,0:T(8,128)(2,1)}, bf16[256,1024]{1,0:T(8,128)(2,1)S(1)}, u32[]{:S(2)}, u32[]{:S(2)}) collective-permute-start(bf16[256,1024]{1,0:T(8,128)(2,1)} %tokens_ref.1), channel_id=1, source_target_pairs={{0,2},{2,4},{4,6},{6,8},{8,10},{10,12},{12,14},{3,1},{5,3},{7,5},{... | collective-permute-start | bytes 1572872 | tf_op jit(solution)/shard_map/ppermute | solution.py:400
  9.7 8.1 %copy-start.5 = (f32[1024]{0:T(1024)S(1)}, f32[1024]{0:T(1024)}, u32[]{:S(2)}) copy-start(f32[1024]{0:T(1024)} %param.10) | copy-start | bytes 12292
  15.7 7.9 %copy-start.1 = (bf16[128,512]{1,0:T(8,128)(2,1)S(1)}, bf16[128,512]{1,0:T(8,128)(2,1)}, u32[]{:S(2)}) copy-start(bf16[128,512]{1,0:T(8,128)(2,1)} %get-tuple-element.47.mix_ref) | copy-start | bytes 393220
  15.7 7.9 %copy-start.6 = (f32[3,6,512]{2,1,0:T(8,128)S(1)}, f32[3,6,512]{2,1,0:T(8,128)}, u32[]{:S(2)}) copy-start(f32[3,6,512]{2,1,0:T(8,128)} %get-tuple-element.45.bias_ref) | copy-start | bytes 110596
  15.7 2.0 %copy-start.8 = (bf16[256,1024]{1,0:T(8,128)(2,1)}, bf16[256,1024]{1,0:T(8,128)(2,1)S(1)}, u32[]{:S(2)}) copy-start(bf16[256,1024]{1,0:T(8,128)(2,1)S(1)} %collective-permute-done.1.a2_ref) | copy-start | bytes 1572868
  15.8 1.6 %collective-permute-start.2 = (bf16[128,1024]{1,0:T(8,128)(2,1)S(1)}, bf16[128,1024]{1,0:T(8,128)(2,1)S(1)}, u32[]{:S(2)}, u32[]{:S(2)}) collective-permute-start(bf16[128,1024]{1,0:T(8,128)(2,1)S(1)} %get-tuple-element.71), channel_id=1, source_target_pairs={{0,1},{1,0},{2,3},{3,2},{4,5},{5,4},{6,7},{7,6},{8,9},{9,8},{10,11... | collective-permute-start | bytes 786440 | tf_op jit(solution)/shard_map/ppermute | solution.py:447
  15.9 1.9 %collective-permute-start.3 = (bf16[128,1024]{1,0:T(8,128)(2,1)S(1)}, bf16[128,1024]{1,0:T(8,128)(2,1)S(1)}, u32[]{:S(2)}, u32[]{:S(2)}) collective-permute-start(bf16[128,1024]{1,0:T(8,128)(2,1)S(1)} %get-tuple-element.70), channel_id=1, source_target_pairs={{0,1},{1,0},{2,3},{3,2},{4,5},{5,4},{6,7},{7,6},{8,9},{9,8},{10,11... | collective-permute-start | bytes 786440 | tf_op jit(solution)/shard_map/ppermute | solution.py:448
  21.6 1.9 %collective-permute-start.4 = (bf16[256,1024]{1,0:T(8,128)(2,1)S(1)}, bf16[256,1024]{1,0:T(8,128)(2,1)S(1)}, u32[]{:S(2)}, u32[]{:S(2)}) collective-permute-start(bf16[256,1024]{1,0:T(8,128)(2,1)S(1)} %collective-permute-done.a1x_ref), channel_id=1, source_target_pairs={{0,1},{1,0},{2,3},{3,2},{4,5},{5,4},{6,7},{7,6},{8,9},{9,8},{10,11... | collective-permute-start | bytes 1572872 | tf_op jit(solution)/shard_map/ppermute | solution.py:470
  31.8 1.3 %collective-permute-start.5 = (f32[64,256]{1,0:T(8,128)S(1)}, f32[64,256]{1,0:T(8,128)S(1)}, u32[]{:S(2)}, u32[]{:S(2)}) collective-permute-start(f32[64,256]{1,0:T(8,128)S(1)} %get-tuple-element.50), channel_id=1, source_target_pairs={{0,1},{1,0},{2,3},{3,2},{4,5},{5,4},{6,7},{7,6},{8,9},{9,8},{10,11... | collective-permute-start | bytes 196616 | tf_op jit(solution)/shard_map/ppermute | solution.py:508
  33.8 15.0 %copy-start.4 = (f32[64,256]{1,0:T(8,128)S(1)}, f32[64,256]{1,0:T(8,128)}, u32[]{:S(2)}) copy-start(f32[64,256]{1,0:T(8,128)} %get-tuple-element.58.targets_ref) | copy-start | bytes 196612
  33.8 15.0 %copy-start.7 = (s32[2048,1]{0,1:T(1,128)S(1)}, s32[2048,1]{0,1:T(1,128)}, u32[]{:S(2)}) copy-start(s32[2048,1]{0,1:T(1,128)} %param.17) | copy-start | bytes 24580
  33.8 15.0 %all-to-all-start = ((bf16[8,64,256]{2,1,0:T(8,128)(2,1)}), bf16[8,64,256]{2,1,0:T(8,128)(2,1)S(1)}, u32[]{:S(2)}, u32[]{:S(2)}) async-start(bf16[8,64,256]{2,1,0:T(8,128)(2,1)} %spread.1), calls=%async_computation | async-start | bytes 524288 | tf_op jit(solution)/shard_map/all_to_all | solution.py:515
  39.6 11.0 %copy-start.3 = (bf16[256,768]{1,0:T(8,128)(2,1)S(1)}, bf16[256,768]{1,0:T(8,128)(2,1)}, u32[]{:S(2)}) copy-start(bf16[256,768]{1,0:T(8,128)(2,1)} %get-tuple-element.61.hot_ref) | copy-start | bytes 1179652
  46.8 0.8 %copy-start.2 = (bf16[4,2,128,256]{3,2,1,0:T(8,128)(2,1)}, bf16[4,2,128,256]{3,2,1,0:T(8,128)(2,1)S(1)}, u32[]{:S(2)}) copy-start(bf16[4,2,128,256]{3,2,1,0:T(8,128)(2,1)S(1)} %get-tuple-element.63.refs_4_) | copy-start | bytes 1572868
  49.3 1.3 %collective-permute-start.6 = (f32[64,256]{1,0:T(8,128)S(1)}, f32[64,256]{1,0:T(8,128)S(1)}, u32[]{:S(2)}, u32[]{:S(2)}) collective-permute-start(f32[64,256]{1,0:T(8,128)S(1)} %get-tuple-element.59.resid_a_ref), channel_id=1, source_target_pairs={{0,1},{1,0},{2,3},{3,2},{4,5},{5,4},{6,7},{7,6},{8,9},{9,8},{10,11... | collective-permute-start | bytes 196616 | tf_op jit(solution)/shard_map/ppermute | solution.py:555
  50.6 10.3 %copy-start = (bf16[256,1024]{1,0:T(8,128)(2,1)S(1)}, bf16[256,1024]{1,0:T(8,128)(2,1)}, u32[]{:S(2)}) copy-start(bf16[256,1024]{1,0:T(8,128)(2,1)} %tokens_ref.1) | copy-start | bytes 1572868
  59.3 1.7 %collective-permute-start.7 = (bf16[256,640]{1,0:T(8,128)(2,1)S(1)}, bf16[256,640]{1,0:T(8,128)(2,1)S(1)}, u32[]{:S(2)}, u32[]{:S(2)}) collective-permute-start(bf16[256,640]{1,0:T(8,128)(2,1)S(1)} %get-tuple-element.67), channel_id=1, source_target_pairs={{0,1},{1,0},{2,3},{3,2},{4,5},{5,4},{6,7},{7,6},{8,9},{9,8},{10,11... | collective-permute-start | bytes 983048 | tf_op jit(solution)/shard_map/ppermute | solution.py:574

commit v4 on v3

--- a/solution.py
+++ b/solution.py
@@ -13,7 +13,6 @@
 BLK = 128
 LIST = 4
 PAIR = 2 * HD
-GROUP = 2
 F32 = jnp.float32
 BF16 = jnp.bfloat16
 DEAD = 1e30
@@ -107,21 +106,6 @@
             bias_ref[t, k : k + 1, :] = row
 
 
-def far_kernel(a2_ref, b2_top_ref, b2_low_ref, gain_ref, w_ref, out_a_ref, out_b_ref, normed):
-    rows = a2_ref.shape[0]
-    piece = b2_top_ref.shape[0]
-
-    @pl.when(pl.program_id(0) == 0)
-    def _():
-        normed[:rows] = normalise(a2_ref, gain_ref)
-        normed[rows : rows + piece] = normalise(b2_top_ref, gain_ref)
-        normed[rows + piece :] = normalise(b2_low_ref, gain_ref)
-
-    both = dot(normed[...], w_ref[0], NN).astype(BF16)
-    out_a_ref[0] = both[:rows]
-    out_b_ref[0] = both[rows:]
-
-
 def pair_cols(p):
     return slice(p * PAIR, (p + 1) * PAIR)
 
@@ -151,67 +135,116 @@
     return jnp.concatenate([(e * inverse).astype(BF16) for e in expo], axis=0)
 
 
+def start_all(copies):
+    for copy in copies:
+        copy.start()
+    return copies
+
+
+def wait_all(copies):
+    for copy in copies:
+        copy.wait()
+
+
 def near_kernel(
-    steps, bias_ref, own_ref, mix_ref, a1x_ref, b1x_ref, gain_ref, w_ref,
-    a1_ref, b1_ref, weight_ref, att_ref, keep_ref, send_ref, normed, read,
+    bias_ref, mix_ref, a1x_ref, b1x_ref, gain_ref, own_hbm, w_hbm,
+    a1_hbm, b1_hbm, weight_hbm, att_ref, keep_ref, send_ref,
+    own_ref, w_ref, near_ref, weight_ref, arrived, sent,
 ):
-    step = pl.program_id(0)
     rows = own_ref.shape[1]
-
-    @pl.when(step == 0)
-    def _():
-        read[...] = jnp.zeros_like(read)
-        normed[:rows] = normalise(a1x_ref, gain_ref)
-        normed[rows:] = normalise(b1x_ref, gain_ref)
-
-    near = {}
-    for c in (1, 2, 0):
-        near[c] = project_rows(normed[...], w_ref[c], c)
-        a1_ref[c] = near[c][:rows]
-        b1_ref[c] = near[c][rows:]
-    scores = []
-    for p in range(GROUP):
-        keys = jnp.concatenate([own_ref[1, :, pair_cols(p)], near[1][:, pair_cols(p)]], axis=0)
-        scores.append(dot(keys, two_heads(own_ref[0, :, pair_cols(p)]), NT))
-    weights = []
-    for p in range(GROUP):
-        weights.append(soften(bias_ref, 0, scores[p]))
-        weight_ref[p] = weights[p]
+    pairs = own_ref.shape[2] // PAIR
+    order = (1, 2, 0)
+    w_in = {c: pltpu.make_async_copy(w_hbm.at[c], w_ref.at[c], arrived.at[c]) for c in order}
+    own_in = pltpu.make_async_copy(own_hbm, own_ref, arrived.at[3])
+    start_all([w_in[1], own_in, w_in[2], w_in[0]])
+    normed = jnp.concatenate([normalise(a1x_ref, gain_ref), normalise(b1x_ref, gain_ref)], axis=0)
+    out = []
+
+    def project(c):
+        w_in[c].wait()
+        near_ref[c] = project_rows(normed, w_ref[c], c)
+        for side, target in enumerate((a1_hbm, b1_hbm)):
+            source = near_ref.at[c, pl.ds(side * rows, rows)]
+            out.append(pltpu.make_async_copy(source, target.at[c], sent.at[2 * c + side]))
+            out[-1].start()
+
+    def stack(c, p):
+        return jnp.concatenate([own_ref[c, :, pair_cols(p)], near_ref[c, :, pair_cols(p)]], axis=0)
+
+    def score(p):
+        return dot(stack(1, p), two_heads(own_ref[0, :, pair_cols(p)]), NT)
+
+    project(1)
+    own_in.wait()
+    scores = {0: score(0)}
+    project(2)
     attended = []
-    for p in range(GROUP):
-        values = jnp.concatenate([own_ref[2, :, pair_cols(p)], near[2][:, pair_cols(p)]], axis=0)
-        attended.append(fold_heads(dot(values, weights[p], TN)).astype(BF16))
+    for p in range(pairs):
+        if p + 1 < pairs:
+            scores[p + 1] = score(p + 1)
+        weight = soften(bias_ref, 0, scores[p])
+        weight_ref[p] = weight
+        out.append(pltpu.make_async_copy(weight_ref.at[p], weight_hbm.at[p], sent.at[6 + p]))
+        out[-1].start()
+        if p == pairs - 1:
+            project(0)
+        attended.append(fold_heads(dot(stack(2, p), weight, TN)).astype(BF16))
         att_ref[p] = attended[p]
-    read[...] += dot(mix_ref[...], jnp.concatenate(attended, axis=0), NN)
-
-    @pl.when(step == steps - 1)
-    def _():
-        half = read.shape[0] // 2
-        keep_ref[...] = read[:half]
-        send_ref[...] = read[half:]
-
-
-def side_kernel(bias_ref, own_ref, a1_ref, b1_ref, a2_ref, b2_ref, weight_ref, att_ref):
-    own_rows = own_ref.shape[1]
-    jobs = [(p, side) for p in range(GROUP) for side in range(2)]
-    near, far = (a1_ref, b1_ref), (a2_ref, b2_ref)
-
-    def stack(p, side, part):
+    read = dot(mix_ref[...], jnp.concatenate(attended, axis=0), NN)
+    half = keep_ref.shape[0]
+    keep_ref[...] = read[:half]
+    send_ref[...] = read[half:]
+    wait_all(out)
+
+
+def side_kernel(
+    bias_ref, a2x_ref, b2x_ref, gain_ref, own_hbm, a1_hbm, b1_hbm, w_hbm, weight_hbm, att_ref,
+    own_ref, a1_ref, b1_ref, w_ref, far_ref, weight_ref, arrived, sent,
+):
+    rows = own_ref.shape[1]
+    pairs = own_ref.shape[2] // PAIR
+    w_in = [
+        pltpu.make_async_copy(w_hbm.at[c + 1], w_ref.at[c], arrived.at[c]) for c in range(2)
+    ]
+    rows_in = [
+        pltpu.make_async_copy(source, target, arrived.at[2 + n])
+        for n, (source, target) in enumerate(
+            ((own_hbm, own_ref), (a1_hbm, a1_ref), (b1_hbm, b1_ref))
+        )
+    ]
+    start_all([w_in[0]] + rows_in + [w_in[1]])
+    normed = jnp.concatenate([normalise(a2x_ref, gain_ref), normalise(b2x_ref, gain_ref)], axis=0)
+    near = (a1_ref, b1_ref)
+    out = []
+
+    def project(c):
+        w_in[c].wait()
+        far_ref[c] = dot(normed, w_ref[c], NN).astype(BF16)
+
+    def stack(c, p, side):
         cols = pair_cols(p)
-        return jnp.concatenate(
-            [own_ref[part, :, cols], near[side][part, :, cols], far[side][part - 1, :, cols]],
-            axis=0,
+        far = far_ref[c - 1, side * rows : (side + 1) * rows, cols]
+        return jnp.concatenate([own_ref[c, :, cols], near[side][c, :, cols], far], axis=0)
+
+    def score(p, side):
+        return dot(stack(1, p, side), two_heads(near[side][0, :, pair_cols(p)]), NT)
+
+    project(0)
+    wait_all(rows_in)
+    jobs = [(p, side) for p in range(pairs) for side in range(2)]
+    scores = {jobs[0]: score(*jobs[0])}
+    project(1)
+    for n, (p, side) in enumerate(jobs):
+        if n + 1 < len(jobs):
+            scores[jobs[n + 1]] = score(*jobs[n + 1])
+        weight = soften(bias_ref, 1 + side, scores[p, side])
+        weight_ref[p, side] = weight[:rows]
+        out.append(
+            pltpu.make_async_copy(weight_ref.at[p, side], weight_hbm.at[p, side], sent.at[n])
         )
-
-    scores = [
-        dot(stack(p, side, 1), two_heads(near[side][0, :, pair_cols(p)]), NT) for p, side in jobs
-    ]
-    weights = []
-    for (p, side), score in zip(jobs, scores):
-        weights.append(soften(bias_ref, 1 + side, score))
-        weight_ref[p, side] = weights[-1][:own_rows]
-    for (p, side), weight in zip(jobs, weights):
-        att_ref[p, side] = fold_heads(dot(stack(p, side, 2), weight, TN)).astype(BF16)
+        out[-1].start()
+        att_ref[p, side] = fold_heads(dot(stack(2, p, side), weight, TN)).astype(BF16)
+    wait_all(out)
 
 
 def spread_kernel(keep_ref, got_ref, out_ref):
@@ -247,15 +280,22 @@
 ):
     sources, (keep_ref, send_ref, stat_ref, loss_ref) = refs[:9], refs[9:13]
     buffers, arrived = refs[13:22], refs[22]
+    own_ref, a1_ref, b1_ref, own_att_ref, side_att_ref, own_w_ref, side_w_ref, w_ref, tokens_ref = buffers
+    pairs = own_ref.shape[2] // PAIR
     copies = [
-        pltpu.make_async_copy(source, buffer, arrived.at[n])
-        for n, (source, buffer) in enumerate(zip(sources, buffers))
+        pltpu.make_async_copy(sources[n], buffers[n], arrived.at[n]) for n in (0, 1, 2, 3, 4, 7, 8)
     ]
-    for copy in copies:
-        copy.start()
-    own_ref, a1_ref, b1_ref, own_att_ref, side_att_ref, own_w_ref, side_w_ref, w_ref, tokens_ref = buffers
+    weight_in = [
+        [
+            pltpu.make_async_copy(
+                sources[n].at[p], buffers[n].at[p], arrived.at[9 + 2 * p + n - 5]
+            )
+            for n in (5, 6)
+        ]
+        for p in range(pairs)
+    ]
+    start_all(copies[:5] + [copy for pair in weight_in for copy in pair] + copies[5:])
     own_rows = own_ref.shape[1]
-    pairs = own_ref.shape[2] // PAIR
     residual = jnp.concatenate([resid_a_ref[...], resid_b_ref[...]], axis=0)
     loss_ref[...] = jnp.broadcast_to(
         jnp.sum(counts_ref[...] * residual * residual, keepdims=True), loss_ref.shape
@@ -313,20 +353,18 @@
         grad_value = dot(own_weights, jnp.concatenate(grads, axis=1), NT)
         return grad_query.T.astype(BF16), grad_key.astype(BF16), grad_value.astype(BF16)
 
-    for copy in copies[:3]:
-        copy.wait()
+    wait_all(copies[:3])
     opened = open_pair(0)
-    for copy in copies[3:7]:
-        copy.wait()
+    wait_all(copies[3:5])
     grad_proj = []
     for p in range(pairs):
         grads, changes = opened
         if p + 1 < pairs:
             opened = open_pair(p + 1)
+        wait_all(weight_in[p])
         grad_proj.append(close_pair(p, grads, score_pair(p, changes)))
     flat = jnp.concatenate([grad_proj[p][c] for c in range(3) for p in range(pairs)], axis=1)
-    for copy in copies[7:]:
-        copy.wait()
+    wait_all(copies[5:])
     half = keep_ref.shape[1]
     inputs = tokens_ref[...].astype(F32)
     scaled = inputs * gain_ref[...]
@@ -359,16 +397,8 @@
     )
 
 
-def pair_spec(parts, rows):
-    return pl.BlockSpec((parts, rows, GROUP * PAIR), lambda p: (0, 0, p))
-
-
 def whole_spec(shape):
     return pl.BlockSpec(shape, lambda p: (0,) * len(shape))
-
-
-def lead_spec(shape):
-    return pl.BlockSpec((GROUP,) + shape, lambda p: (p,) + (0,) * len(shape))
 
 
 SMEM_SPEC = pl.BlockSpec(memory_space=pltpu.SMEM)
@@ -380,7 +410,6 @@
     tok_rows, width = tokens.shape
     cols = w_qkv.shape[2]
     pairs = cols // PAIR
-    steps = pairs // GROUP
     panels, readout = targets.shape
     half_read = readout // 2
     half_width = width // 2
@@ -442,53 +471,17 @@
         place, key_blocks.T, list_len, flat_ids, w_out, readout_weight, targets, tokens, gain, w_qkv
     )
 
-    a2_tokens, own = lax.optimization_barrier((a2_tokens, own))
-    piece = tok_rows // 2
-    b2_top = lax.ppermute(a2_tokens[:piece], "head", core_swap)
-    b2_low = lax.ppermute(a2_tokens[piece:], "head", core_swap)
-    a2, b2 = pl.pallas_call(
-        far_kernel,
-        grid=(2,),
-        in_specs=[
-            whole_tokens,
-            whole_spec((piece, width)),
-            whole_spec((piece, width)),
-            whole_gain,
-            pl.BlockSpec((1, width, cols), lambda c: (c + 1, 0, 0)),
-        ],
-        out_specs=[pl.BlockSpec((1, tok_rows, cols), lambda c: (c, 0, 0))] * 2,
-        out_shape=[jax.ShapeDtypeStruct((2, tok_rows, cols), BF16)] * 2,
-        scratch_shapes=[pltpu.VMEM((2 * tok_rows, width), BF16)],
-        compiler_params=params("arbitrary"),
-        cost_estimate=pl.CostEstimate(flops=2**20, bytes_accessed=4 * MIB, transcendentals=0),
-        name="far",
-    )(a2_tokens, b2_top, b2_low, gain, w_qkv)
-
-    a1_tokens, own, a2, b2, mix, own_targets, hot, bias = lax.optimization_barrier(
-        (a1_tokens, own, a2, b2, mix, own_targets, hot, bias)
+    a1_tokens, own, mix, own_targets, hot, bias = lax.optimization_barrier(
+        (a1_tokens, own, mix, own_targets, hot, bias)
     )
     b1_tokens = lax.ppermute(a1_tokens, "head", core_swap)
-    mix_spec = pl.BlockSpec((readout, GROUP * PAIR), lambda p: (0, p))
+    a2_tokens, b1_tokens = lax.optimization_barrier((a2_tokens, b1_tokens))
+    b2_tokens = lax.ppermute(a2_tokens, "head", core_swap)
+    hbm = pl.BlockSpec(memory_space=pl.ANY)
     a1, b1, own_weight, own_att, read_keep, read_send = pl.pallas_call(
-        functools.partial(near_kernel, steps),
-        grid=(steps,),
-        in_specs=[
-            bias_spec,
-            pair_spec(3, tok_rows),
-            mix_spec,
-            whole_tokens,
-            whole_tokens,
-            whole_gain,
-            pair_spec(3, width),
-        ],
-        out_specs=[
-            pair_spec(3, tok_rows),
-            pair_spec(3, tok_rows),
-            lead_spec((3 * tok_rows, 2 * tok_rows)),
-            lead_spec((PAIR, tok_rows)),
-            whole_spec((half_read, tok_rows)),
-            whole_spec((half_read, tok_rows)),
-        ],
+        near_kernel,
+        in_specs=[vmem] * 5 + [hbm] * 2,
+        out_specs=[hbm] * 3 + [vmem] * 3,
         out_shape=[
             jax.ShapeDtypeStruct((3, tok_rows, cols), BF16),
             jax.ShapeDtypeStruct((3, tok_rows, cols), BF16),
@@ -498,13 +491,19 @@
             jax.ShapeDtypeStruct((half_read, tok_rows), F32),
         ],
         scratch_shapes=[
-            pltpu.VMEM((2 * tok_rows, width), BF16),
-            pltpu.VMEM((readout, tok_rows), F32),
-        ],
-        compiler_params=params("arbitrary"),
+            pltpu.VMEM((3, tok_rows, cols), BF16),
+            pltpu.VMEM((3, width, cols), BF16),
+            pltpu.VMEM((3, 2 * tok_rows, cols), BF16),
+            pltpu.VMEM((pairs, 3 * tok_rows, 2 * tok_rows), BF16),
+            pltpu.SemaphoreType.DMA((4,)),
+            pltpu.SemaphoreType.DMA((6 + pairs,)),
+        ],
+        compiler_params=params(),
+        cost_estimate=pl.CostEstimate(flops=2**33, bytes_accessed=8 * MIB, transcendentals=0),
         name="near",
-    )(bias, own, mix, a1_tokens, b1_tokens, gain, w_qkv)
-
+    )(bias, mix, a1_tokens, b1_tokens, gain, own, w_qkv)
+
+    read_send, b2_tokens = lax.optimization_barrier((read_send, b2_tokens))
     read_got = lax.ppermute(read_send, "head", core_swap)
     spread = pl.pallas_call(
         spread_kernel,
@@ -516,21 +515,24 @@
 
     side_weight, side_att = pl.pallas_call(
         side_kernel,
-        grid=(steps,),
-        in_specs=[bias_spec] + [pair_spec(3, tok_rows)] * 3 + [pair_spec(2, tok_rows)] * 2,
-        out_specs=[lead_spec((2, tok_rows, 2 * tok_rows)), lead_spec((2, PAIR, tok_rows))],
+        in_specs=[vmem] * 4 + [hbm] * 4,
+        out_specs=[hbm, vmem],
         out_shape=[
             jax.ShapeDtypeStruct((pairs, 2, tok_rows, 2 * tok_rows), BF16),
             jax.ShapeDtypeStruct((pairs, 2, PAIR, tok_rows), BF16),
         ],
-        compiler_params=params("arbitrary"),
-        cost_estimate=pl.CostEstimate(
-            flops=pairs * 4 * 2 * 2 * 768 * 256 * 128,
-            bytes_accessed=8 * MIB,
-            transcendentals=pairs * 4 * 768 * 256,
-        ),
+        scratch_shapes=[pltpu.VMEM((3, tok_rows, cols), BF16)] * 3
+        + [
+            pltpu.VMEM((2, width, cols), BF16),
+            pltpu.VMEM((2, 2 * tok_rows, cols), BF16),
+            pltpu.VMEM((pairs, 2, tok_rows, 2 * tok_rows), BF16),
+            pltpu.SemaphoreType.DMA((5,)),
+            pltpu.SemaphoreType.DMA((2 * pairs,)),
+        ],
+        compiler_params=params(),
+        cost_estimate=pl.CostEstimate(flops=2**33, bytes_accessed=8 * MIB, transcendentals=0),
         name="attend_sides",
-    )(bias, own, a1, b1, a2, b2)
+    )(bias, a2_tokens, b2_tokens, gain, own, a1, b1, w_qkv)
     all_rows, side_weight, side_att = lax.optimization_barrier((all_rows, side_weight, side_att))
 
     batch = min(seq_count, 8)
@@ -558,7 +560,7 @@
     sources = (own, a1, b1, own_att, side_att, own_weight, side_weight, w_qkv, tokens)
     keep, send, stats, loss = pl.pallas_call(
         back_kernel,
-        in_specs=[SMEM_SPEC] + [vmem] * 6 + [pl.BlockSpec(memory_space=pl.ANY)] * len(sources),
+        in_specs=[SMEM_SPEC] + [vmem] * 6 + [hbm] * len(sources),
         out_specs=[vmem] * 4,
         out_shape=[
             jax.ShapeDtypeStruct((tok_rows, half_width), F32),
@@ -567,7 +569,7 @@
             jax.ShapeDtypeStruct((1, BLK), F32),
         ],
         scratch_shapes=[pltpu.VMEM(a.shape, a.dtype) for a in sources]
-        + [pltpu.SemaphoreType.DMA((len(sources),))],
+        + [pltpu.SemaphoreType.DMA((len(sources) + 2 * pairs,))],
         compiler_params=params(),
         name="back",
     )(core_index, resid_a, resid_b, counts, hot, mix, gain, *sources)

time: 63.5 us -> 60.9 us (0.959)
  Pallas kernels: 35.6 us -> 32.6 us
  local copies, waits for them, and re-layouts: 0.86 us -> 2.52 us
  waiting for transfers between devices: 8.9 us -> 7.91 us
    pallas_call x4 -> x3, Pallas kernels: 27.4 us -> 24.4 us  [the longest x1 8.77 us: local(): pl.pallas_call(back_kernel, in_specs=[SMEM_SPEC] + [vmem] * 6 + [hbm] * l...]
    ppermute x1, waiting for transfers between devices: 0.59 us -> 2.3 us  [local(): a1_tokens = lax.ppermute(tokens, ('seq', 'head'), shifted(1))]
    unnamed x18 -> x20, local copies, waits for them, and re-layouts: 0.82 us -> 2.52 us
    ppermute x1, starting transfers between devices: 4.96 us -> 3.49 us  [local(): a2_tokens = lax.ppermute(tokens, ('seq', 'head'), shifted(2))]
    ppermute x1, starting transfers between devices: 3.46 us -> 4.91 us  [local(): a1_tokens = lax.ppermute(tokens, ('seq', 'head'), shifted(1))]
    ppermute x2 -> x1, waiting for transfers between devices: 1.4 us -> 0.01 us  [local(): b2_tokens = lax.ppermute(a2_tokens, 'head', core_swap)]
    all_to_all x1, waiting for transfers between devices: 1.21 us -> 0.12 us  [local(): all_rows = lax.all_to_all(spread, 'seq', 0, 0)]
  transfers between devices with their start and end apart: 9 -> 8, of which waited for: 8 -> 6; matrix products, arithmetic and copies ran while one was open for 1% -> 1% of each run, Pallas kernels for 26% -> 36%
where the time goes in v4:
time: 60.9 us; the launch traced here: 60.5 us
  Pallas kernels  32.6 us (54%)
  starting transfers between devices  14.9 us (24%)
  waiting for transfers between devices  7.91 us (13%)
  local copies, waits for them, and re-layouts  2.52 us (4%)
  between operations  1.93 us (3%)
    pallas_call x1, Pallas kernels, local(): pl.pallas_call(back_kernel, in_specs=[SMEM_SPEC] + [vmem] * 6 + [hbm] * l...  8.77 us
    pallas_call x1, Pallas kernels, local(): pl.pallas_call(side_kernel, in_specs=[vmem] * 4 + [hbm] * 4, out_specs=[h...  8.47 us
    pallas_call x1, Pallas kernels, local(): pl.pallas_call(near_kernel, in_specs=[vmem] * 5 + [hbm] * 2, out_specs=[h...  7.21 us
    pallas_call x1, Pallas kernels, local(): pl.pallas_call(first_kernel, grid=(3,), in_specs=[SMEM_SPEC] * 3 + [whole...  5.98 us
    all_to_all x1, starting transfers between devices, local(): all_rows = lax.all_to_all(spread, 'seq', 0, 0)  5.68 us
    ppermute x1, starting transfers between devices, local(): a1_tokens = lax.ppermute(tokens, ('seq', 'head'), shifted(1))  4.91 us
    ppermute x1, starting transfers between devices, local(): a2_tokens = lax.ppermute(tokens, ('seq', 'head'), shifted(2))  3.49 us
    unnamed x20, local copies, waits for them, and re-layouts  2.52 us
  transfers between devices with their start and end apart: 8, of which 6 were waited for; matrix products, arithmetic and copies ran while one was open for 1% of the time, Pallas kernels for 36%

profile of v4, /device:TPU:0, one launch (start us, length us, event | category | flops | bytes accessed | tf_op | source)
XLA Modules:
  0.0 60.5 jit_solution(4886131325688370222)
XLA Ops:
  0.6 4.9 %collective-permute-start = (bf16[256,1024]{1,0:T(8,128)(2,1)}, bf16[256,1024]{1,0:T(8,128)(2,1)S(1)}, u32[]{:S(2)}, u32[]{:S(2)}) collective-permute-start(bf16[256,1024]{1,0:T(8,128)(2,1)} %tokens_ref.1), channel_id=1, source_target_pairs={{0,2},{2,4},{4,6},{6,8},{8,10},{10,12},{12,14},{3,1},{5,3},{7,5},{... | collective-permute-start | bytes 1572872 | tf_op jit(solution)/shard_map/ppermute | solution.py:429
  5.5 3.5 %collective-permute-start.1 = (bf16[256,1024]{1,0:T(8,128)(2,1)}, bf16[256,1024]{1,0:T(8,128)(2,1)S(1)}, u32[]{:S(2)}, u32[]{:S(2)}) collective-permute-start(bf16[256,1024]{1,0:T(8,128)(2,1)} %tokens_ref.1), channel_id=1, source_target_pairs={{0,4},{2,6},{4,8},{6,10},{8,12},{10,14},{5,1},{7,3},{9,5},{11,7},{... | collective-permute-start | bytes 1572872 | tf_op jit(solution)/shard_map/ppermute | solution.py:430
  9.0 0.6 pad_add_fusion.place_ref
  9.6 6.0 %first.1 = (f32[3,6,512]{2,1,0:T(8,128)}, bf16[256,768]{1,0:T(8,128)(2,1)}, bf16[128,512]{1,0:T(8,128)(2,1)}, f32[64,256]{1,0:T(8,128)}, bf16[3,256,512]{2,1,0:T(8,128)(2,1)}) custom-call(s32[3]{0:T(128)} %pad_add_fusion.place_ref, s32[4,16]{1,0:T(4,128)} %bitcast.15, s32[16]{0:T(128)} %lengths_ref.1, s32[1,2048]{1,0:T(1,128)} %bitcast.12, ...), custom_call_target="tpu_custom_call" | custom-call | flops 2147483648 | bytes 6291456 | tf_op jit(solution)/shard_map/first/pallas_call | solution.py:439
  15.6 2.3 %collective-permute-done.a1x_ref = bf16[256,1024]{1,0:T(8,128)(2,1)S(1)} collective-permute-done((bf16[256,1024]{1,0:T(8,128)(2,1)}, bf16[256,1024]{1,0:T(8,128)(2,1)S(1)}, u32[]{:S(2)}, u32[]{:S(2)}) %collective-permute-start) | collective-permute-done | bytes 524320 | tf_op jit(solution)/shard_map/ppermute | solution.py:429
  17.9 0.0 collective-permute-start.2
  17.9 0.0 collective-permute-done.1.a2x_ref
  17.9 1.9 %collective-permute-done.2.b1x_ref = bf16[256,1024]{1,0:T(8,128)(2,1)S(1)} collective-permute-done((bf16[256,1024]{1,0:T(8,128)(2,1)S(1)}, bf16[256,1024]{1,0:T(8,128)(2,1)S(1)}, u32[]{:S(2)}, u32[]{:S(2)}) %collective-permute-start.2) | collective-permute-done | bytes 524320 | tf_op jit(solution)/shard_map/ppermute | solution.py:477
  19.8 0.1 collective-permute-start.3
  19.9 0.0 copy-done.6
  19.9 0.9 %copy-done.3 = bf16[128,512]{1,0:T(8,128)(2,1)S(1)} copy-done((bf16[128,512]{1,0:T(8,128)(2,1)S(1)}, bf16[128,512]{1,0:T(8,128)(2,1)}, u32[]{:S(2)}) %copy-start.3) | copy-done | bytes 131096
  20.8 0.8 %copy-done.8 = f32[3,6,512]{2,1,0:T(8,128)S(1)} copy-done((f32[3,6,512]{2,1,0:T(8,128)S(1)}, f32[3,6,512]{2,1,0:T(8,128)}, u32[]{:S(2)}) %copy-start.8) | copy-done | bytes 36888
  21.6 7.2 %near.1 = (bf16[3,256,512]{2,1,0:T(8,128)(2,1)}, bf16[3,256,512]{2,1,0:T(8,128)(2,1)}, bf16[4,768,512]{2,1,0:T(8,128)(2,1)}, bf16[4,128,256]{2,1,0:T(8,128)(2,1)...) custom-call(f32[3,6,512]{2,1,0:T(8,128)S(1)} %copy-done.8, bf16[128,512]{1,0:T(8,128)(2,1)S(1)} %copy-done.3, ...), custom_call_target="tpu_custom_call" | custom-call | flops 8589934592 | bytes 8388608 | tf_op jit(solution)/shard_map/near/pallas_call | solution.py:481
  28.9 0.0 collective-permute-done.3.b2x_ref
  28.9 0.4 collective-permute-start.4
  29.3 0.9 %collective-permute-done.4.got_ref = f32[64,256]{1,0:T(8,128)S(1)} collective-permute-done((f32[64,256]{1,0:T(8,128)S(1)}, f32[64,256]{1,0:T(8,128)S(1)}, u32[]{:S(2)}, u32[]{:S(2)}) %collective-permute-start.4) | collective-permute-done | bytes 65568 | tf_op jit(solution)/shard_map/ppermute | solution.py:507
  30.2 0.7 %spread.1 = bf16[8,64,256]{2,1,0:T(8,128)(2,1)} custom-call(f32[64,256]{1,0:T(8,128)S(1)} %get-tuple-element.44.keep_ref, f32[64,256]{1,0:T(8,128)S(1)} %collective-permute-done.4.got_ref), custom_call_target="tpu_custom_call" | custom-call | tf_op jit(solution)/shard_map/spread/pallas_call | solution.py:508
  30.9 5.7 %all-to-all-start = ((bf16[8,64,256]{2,1,0:T(8,128)(2,1)}), bf16[8,64,256]{2,1,0:T(8,128)(2,1)S(1)}, u32[]{:S(2)}, u32[]{:S(2)}) async-start(bf16[8,64,256]{2,1,0:T(8,128)(2,1)} %spread.1), calls=%async_computation | async-start | bytes 524288 | tf_op jit(solution)/shard_map/all_to_all | solution.py:514
  36.6 0.0 copy-start.7
  36.7 0.0 copy-start.2
  36.7 0.0 copy-start.4
  36.7 8.5 %attend_sides.1 = (bf16[4,2,256,512]{3,2,1,0:T(8,128)(2,1)}, bf16[4,2,128,256]{3,2,1,0:T(8,128)(2,1)S(1)}) custom-call(f32[3,6,512]{2,1,0:T(8,128)S(1)} %copy-done.9, bf16[256,1024]{1,0:T(8,128)(2,1)S(1)} %collective-permute-done.1.a2x_ref, bf16[256,1024]{1,0:T(8,128)(2,1)S(1)} %collective-permute-done.3.b2x_ref, f32[1,1024]{1,0:T(1,128)S(1)} %bitcast.9, ...), custom_call_target="tpu_custom_call" | custom-call | flops 8589934592 | bytes 8388608 | tf_op jit(solution)/shard_map/attend_sides/pallas_call | solution.py:516
  45.2 0.0 copy-start.1
  45.2 0.8 %copy-done.1 = bf16[4,2,128,256]{3,2,1,0:T(8,128)(2,1)} copy-done((bf16[4,2,128,256]{3,2,1,0:T(8,128)(2,1)}, bf16[4,2,128,256]{3,2,1,0:T(8,128)(2,1)S(1)}, u32[]{:S(2)}) %copy-start.1) | copy-done | bytes 524312
  45.9 0.1 all-to-all-done.rows_ref
  46.1 0.5 pool.1
  46.5 0.1 collective-permute-start.5
  46.6 1.2 %collective-permute-done.5.resid_b_ref = f32[64,256]{1,0:T(8,128)S(1)} collective-permute-done((f32[64,256]{1,0:T(8,128)S(1)}, f32[64,256]{1,0:T(8,128)S(1)}, u32[]{:S(2)}, u32[]{:S(2)}) %collective-permute-start.5) | collective-permute-done | bytes 65568 | tf_op jit(solution)/shard_map/ppermute | solution.py:557
  47.9 8.8 %back.1 = (f32[256,512]{1,0:T(8,128)S(1)}, bf16[256,640]{1,0:T(8,128)(2,1)S(1)}, f32[256,128]{1,0:T(8,128)S(1)}, f32[1,128]{1,0:T(1,128)S(1)}) custom-call(s32[1]{0:T(128)} %bitcast.core_ref, f32[64,256]{1,0:T(8,128)S(1)} %get-tuple-element.55.resid_a_ref, f32[64,256]{1,0:T(8,128)S(1)} %collective-permute-done.5.resid_b_ref, ...), custom_call_target="tpu_custom_call" | custom-call | tf_op jit(solution)/shard_map/back/pallas_call | solution.py:561
  56.6 0.2 collective-permute-start.6
  56.9 1.4 %collective-permute-done.6.got_ref = bf16[256,640]{1,0:T(8,128)(2,1)S(1)} collective-permute-done((bf16[256,640]{1,0:T(8,128)(2,1)S(1)}, bf16[256,640]{1,0:T(8,128)(2,1)S(1)}, u32[]{:S(2)}, u32[]{:S(2)}) %collective-permute-start.6) | collective-permute-done | bytes 327712 | tf_op jit(solution)/shard_map/ppermute | solution.py:576
  58.3 1.0 %final.1 = f32[256,512]{1,0:T(8,128)} custom-call(s32[1]{0:T(128)} %bitcast.core_ref, f32[256,512]{1,0:T(8,128)S(1)} %get-tuple-element.62.keep_ref, bf16[256,640]{1,0:T(8,128)(2,1)S(1)} %collective-permute-done.6.got_ref, f32[256,128]{1,0:T(8,128)S(1)} %get-tuple-element.64.stat_ref, bf16[256,1024]{1,0:T(8,128)(2,1)S(1)} %copy-done, f32[1,1024]{1,0:T(1,128)S(1)} %bitcast.11), custom_call_target="tpu_custom_call" | custom-call | tf_op jit(solution)/shard_map/final/pallas_call | solution.py:578
  (12 shorter events, 0.0 us)
Async XLA Ops:
  0.6 17.3 %collective-permute-start = (bf16[256,1024]{1,0:T(8,128)(2,1)}, bf16[256,1024]{1,0:T(8,128)(2,1)S(1)}, u32[]{:S(2)}, u32[]{:S(2)}) collective-permute-start(bf16[256,1024]{1,0:T(8,128)(2,1)} %tokens_ref.1), channel_id=1, source_target_pairs={{0,2},{2,4},{4,6},{6,8},{8,10},{10,12},{12,14},{3,1},{5,3},{7,5},{... | collective-permute-start | bytes 1572872 | tf_op jit(solution)/shard_map/ppermute | solution.py:429
  5.5 12.4 %collective-permute-start.1 = (bf16[256,1024]{1,0:T(8,128)(2,1)}, bf16[256,1024]{1,0:T(8,128)(2,1)S(1)}, u32[]{:S(2)}, u32[]{:S(2)}) collective-permute-start(bf16[256,1024]{1,0:T(8,128)(2,1)} %tokens_ref.1), channel_id=1, source_target_pairs={{0,4},{2,6},{4,8},{6,10},{8,12},{10,14},{5,1},{7,3},{9,5},{11,7},{... | collective-permute-start | bytes 1572872 | tf_op jit(solution)/shard_map/ppermute | solution.py:430
  9.6 10.3 %copy-start.6 = (f32[1024]{0:T(1024)S(1)}, f32[1024]{0:T(1024)}, u32[]{:S(2)}) copy-start(f32[1024]{0:T(1024)} %param.10) | copy-start | bytes 12292
  17.9 1.9 %collective-permute-start.2 = (bf16[256,1024]{1,0:T(8,128)(2,1)S(1)}, bf16[256,1024]{1,0:T(8,128)(2,1)S(1)}, u32[]{:S(2)}, u32[]{:S(2)}) collective-permute-start(bf16[256,1024]{1,0:T(8,128)(2,1)S(1)} %collective-permute-done.a1x_ref), channel_id=1, source_target_pairs={{0,1},{1,0},{2,3},{3,2},{4,5},{5,4},{6,7},{7,6},{8,9},{9,8},{10,11... | collective-permute-start | bytes 1572872 | tf_op jit(solution)/shard_map/ppermute | solution.py:477
  19.8 9.1 %collective-permute-start.3 = (bf16[256,1024]{1,0:T(8,128)(2,1)S(1)}, bf16[256,1024]{1,0:T(8,128)(2,1)S(1)}, u32[]{:S(2)}, u32[]{:S(2)}) collective-permute-start(bf16[256,1024]{1,0:T(8,128)(2,1)S(1)} %collective-permute-done.1.a2x_ref), channel_id=1, source_target_pairs={{0,1},{1,0},{2,3},{3,2},{4,5},{5,4},{6,7},{7,6},{8,9},{9,8},{10,11... | collective-permute-start | bytes 1572872 | tf_op jit(solution)/shard_map/ppermute | solution.py:479
  19.9 0.9 %copy-start.3 = (bf16[128,512]{1,0:T(8,128)(2,1)S(1)}, bf16[128,512]{1,0:T(8,128)(2,1)}, u32[]{:S(2)}) copy-start(bf16[128,512]{1,0:T(8,128)(2,1)} %get-tuple-element.40.mix_ref) | copy-start | bytes 393220
  20.8 0.8 %copy-start.8 = (f32[3,6,512]{2,1,0:T(8,128)S(1)}, f32[3,6,512]{2,1,0:T(8,128)}, u32[]{:S(2)}) copy-start(f32[3,6,512]{2,1,0:T(8,128)} %get-tuple-element.39.bias_ref) | copy-start | bytes 110596
  21.6 15.0 %copy-start.9 = (f32[3,6,512]{2,1,0:T(8,128)S(1)}, f32[3,6,512]{2,1,0:T(8,128)}, u32[]{:S(2)}) copy-start(f32[3,6,512]{2,1,0:T(8,128)} %get-tuple-element.39.bias_ref) | copy-start | bytes 110596
  28.9 1.3 %collective-permute-start.4 = (f32[64,256]{1,0:T(8,128)S(1)}, f32[64,256]{1,0:T(8,128)S(1)}, u32[]{:S(2)}, u32[]{:S(2)}) collective-permute-start(f32[64,256]{1,0:T(8,128)S(1)} %get-tuple-element.47), channel_id=1, source_target_pairs={{0,1},{1,0},{2,3},{3,2},{4,5},{5,4},{6,7},{7,6},{8,9},{9,8},{10,11... | collective-permute-start | bytes 196616 | tf_op jit(solution)/shard_map/ppermute | solution.py:507
  30.9 15.1 %all-to-all-start = ((bf16[8,64,256]{2,1,0:T(8,128)(2,1)}), bf16[8,64,256]{2,1,0:T(8,128)(2,1)S(1)}, u32[]{:S(2)}, u32[]{:S(2)}) async-start(bf16[8,64,256]{2,1,0:T(8,128)(2,1)} %spread.1), calls=%async_computation | async-start | bytes 524288 | tf_op jit(solution)/shard_map/all_to_all | solution.py:514
  36.6 9.4 %copy-start.5 = (f32[64,256]{1,0:T(8,128)S(1)}, f32[64,256]{1,0:T(8,128)}, u32[]{:S(2)}) copy-start(f32[64,256]{1,0:T(8,128)} %get-tuple-element.54.targets_ref) | copy-start | bytes 196612
  36.6 9.4 %copy-start.7 = (s32[2048,1]{0,1:T(1,128)S(1)}, s32[2048,1]{0,1:T(1,128)}, u32[]{:S(2)}) copy-start(s32[2048,1]{0,1:T(1,128)} %param.17) | copy-start | bytes 24580
  36.7 11.2 %copy-start.2 = (bf16[256,768]{1,0:T(8,128)(2,1)S(1)}, bf16[256,768]{1,0:T(8,128)(2,1)}, u32[]{:S(2)}) copy-start(bf16[256,768]{1,0:T(8,128)(2,1)} %get-tuple-element.57.hot_ref) | copy-start | bytes 1179652
  36.7 11.2 %copy-start.4 = (bf16[128,512]{1,0:T(8,128)(2,1)S(1)}, bf16[128,512]{1,0:T(8,128)(2,1)}, u32[]{:S(2)}) copy-start(bf16[128,512]{1,0:T(8,128)(2,1)} %get-tuple-element.40.mix_ref) | copy-start | bytes 393220
  45.2 0.8 %copy-start.1 = (bf16[4,2,128,256]{3,2,1,0:T(8,128)(2,1)}, bf16[4,2,128,256]{3,2,1,0:T(8,128)(2,1)S(1)}, u32[]{:S(2)}) copy-start(bf16[4,2,128,256]{3,2,1,0:T(8,128)(2,1)S(1)} %get-tuple-element.59.refs_4_) | copy-start | bytes 1572868
  46.5 1.3 %collective-permute-start.5 = (f32[64,256]{1,0:T(8,128)S(1)}, f32[64,256]{1,0:T(8,128)S(1)}, u32[]{:S(2)}, u32[]{:S(2)}) collective-permute-start(f32[64,256]{1,0:T(8,128)S(1)} %get-tuple-element.55.resid_a_ref), channel_id=1, source_target_pairs={{0,1},{1,0},{2,3},{3,2},{4,5},{5,4},{6,7},{7,6},{8,9},{9,8},{10,11... | collective-permute-start | bytes 196616 | tf_op jit(solution)/shard_map/ppermute | solution.py:557
  47.9 10.5 %copy-start = (bf16[256,1024]{1,0:T(8,128)(2,1)S(1)}, bf16[256,1024]{1,0:T(8,128)(2,1)}, u32[]{:S(2)}) copy-start(bf16[256,1024]{1,0:T(8,128)(2,1)} %tokens_ref.1) | copy-start | bytes 1572868
  56.6 1.7 %collective-permute-start.6 = (bf16[256,640]{1,0:T(8,128)(2,1)S(1)}, bf16[256,640]{1,0:T(8,128)(2,1)S(1)}, u32[]{:S(2)}, u32[]{:S(2)}) collective-permute-start(bf16[256,640]{1,0:T(8,128)(2,1)S(1)} %get-tuple-element.63), channel_id=1, source_target_pairs={{0,1},{1,0},{2,3},{3,2},{4,5},{5,4},{6,7},{7,6},{8,9},{9,8},{10,11... | collective-permute-start | bytes 983048 | tf_op jit(solution)/shard_map/ppermute | solution.py:576

commit v5 on v4

--- a/solution.py
+++ b/solution.py
@@ -50,27 +50,30 @@
 
 def first_kernel(
     place_ref, lists_ref, lengths_ref, ids_ref, w_out_ref, read_ref, targets_ref, x_ref, gain_ref, w_ref,
-    bias_ref, hot_ref, mix_ref, own_targets_ref, own_ref, flipped, normed,
+    hot_ref, mix_ref, own_targets_ref, own_ref, inverse_ref, flipped, normed,
 ):
     part = pl.program_id(0)
 
     @pl.when(part == 0)
     def _():
         normed[...] = normalise(x_ref, gain_ref)
-
-    own_ref[0] = project_rows(normed[...], w_ref[0], part)
+        inverse_ref[...] = jnp.broadcast_to(
+            inverse_root(x_ref[...].astype(F32)), inverse_ref.shape
+        )
+
+    own_ref[part] = project_rows(normed[...], w_ref[0], part)
 
     @pl.when(part == 0)
     def _():
         prepare(
             place_ref, lists_ref, lengths_ref, ids_ref, w_out_ref, read_ref, targets_ref,
-            bias_ref, hot_ref, mix_ref, own_targets_ref, flipped,
+            hot_ref, mix_ref, own_targets_ref, own_ref, flipped,
         )
 
 
 def prepare(
     place_ref, lists_ref, lengths_ref, ids_ref, w_out_ref, read_ref, targets_ref,
-    bias_ref, hot_ref, mix_ref, own_targets_ref, flipped,
+    hot_ref, mix_ref, own_targets_ref, own_ref, flipped,
 ):
     seq_index, core, seq_count = place_ref[0], place_ref[1], place_ref[2]
     side = 2 * core - 1
@@ -79,7 +82,11 @@
     per = tok_rows // BLK
     mix = dot(w_out_ref[...], read_ref[...], NN).T
     flip = jnp.concatenate([mix[half_read:], mix[:half_read]], axis=0)
-    mix_ref[...] = jnp.where(core == 0, mix, flip).astype(BF16)
+    mix = jnp.where(core == 0, mix, flip).astype(BF16)
+    mix_ref[...] = mix
+    readout = mix.shape[0]
+    own_ref[3, :readout] = mix
+    own_ref[3, readout:] = jnp.zeros((tok_rows - readout, mix.shape[1]), BF16)
     flipped[...] = targets_ref[...].T
     own_targets_ref[...] = flipped[pl.ds(pl.multiple_of(core * half_read, half_read), half_read), :]
     panel = lax.broadcasted_iota(jnp.int32, (panels, tok_rows), 0)
@@ -91,6 +98,7 @@
         ids = ids_ref[:, pl.ds(pl.multiple_of(stretch * tok_rows, tok_rows), tok_rows)]
         hits = (panel == ids) & inside
         hot_ref[:, t * tok_rows : (t + 1) * tok_rows] = jnp.where(hits, 1.0, 0.0).astype(BF16)
+        biases = []
         for k in range(3 * per):
             key_block = (seq_index + side * int(KEY_STEP[t, k // per])) * per + k % per
             row = jnp.zeros((1, 2 * tok_rows), F32)
@@ -103,7 +111,11 @@
                     )
                 off = jnp.where(live, 0.0, DEAD)
                 row = jnp.where((column // BLK) % per == b, off, row)
-            bias_ref[t, k : k + 1, :] = row
+            biases.append(row)
+        biases.append(jnp.zeros((16 - 3 * per, 2 * tok_rows), F32))
+        own_ref[3, readout + 16 * t : readout + 16 * (t + 1)] = jnp.concatenate(
+            biases, axis=0
+        ).astype(BF16)
 
 
 def pair_cols(p):
@@ -118,15 +130,21 @@
     )
 
 
+def head_halves(pair_t):
+    half = pair_t.shape[1] // 2
+    return pair_t[:HD, :half], pair_t[HD:, half:]
+
+
 def fold_heads(pair_t):
-    half = pair_t.shape[1] // 2
-    return jnp.concatenate([pair_t[:HD, :half], pair_t[HD:, half:]], axis=0)
-
-
-def soften(bias_ref, stretch, scores):
+    return jnp.concatenate(head_halves(pair_t), axis=0)
+
+
+def soften(own_ref, stretch, scores):
     count = scores.shape[0] // BLK
     blocks = [scores[k * BLK : (k + 1) * BLK] for k in range(count)]
-    biases = [bias_ref[stretch, k : k + 1, :] for k in range(count)]
+    base = own_ref.shape[1] // 2 + 16 * stretch
+    bias = own_ref[3, base : base + 16, :].astype(F32)
+    biases = [bias[k : k + 1] for k in range(count)]
     tops = [jnp.max(b, axis=0, keepdims=True) - d for b, d in zip(blocks, biases)]
     top = functools.reduce(jnp.maximum, tops)
     expo = [jnp.exp(b - (top + d)) for b, d in zip(blocks, biases)]
@@ -147,8 +165,8 @@
 
 
 def near_kernel(
-    bias_ref, mix_ref, a1x_ref, b1x_ref, gain_ref, own_hbm, w_hbm,
-    a1_hbm, b1_hbm, weight_hbm, att_ref, keep_ref, send_ref,
+    a1x_ref, b1x_ref, gain_ref, own_hbm, w_hbm,
+    a1_hbm, b1_hbm, weight_hbm, keep_ref, send_ref,
     own_ref, w_ref, near_ref, weight_ref, arrived, sent,
 ):
     rows = own_ref.shape[1]
@@ -182,23 +200,31 @@
     for p in range(pairs):
         if p + 1 < pairs:
             scores[p + 1] = score(p + 1)
-        weight = soften(bias_ref, 0, scores[p])
-        weight_ref[p] = weight
-        out.append(pltpu.make_async_copy(weight_ref.at[p], weight_hbm.at[p], sent.at[6 + p]))
+        weight = soften(own_ref, 0, scores[p])
+        weight_ref[p, : 3 * rows] = weight
+        part = (p, pl.ds(0, 3 * rows))
+        out.append(pltpu.make_async_copy(weight_ref.at[part], weight_hbm.at[part], sent.at[6 + p]))
         out[-1].start()
         if p == pairs - 1:
             project(0)
-        attended.append(fold_heads(dot(stack(2, p), weight, TN)).astype(BF16))
-        att_ref[p] = attended[p]
-    read = dot(mix_ref[...], jnp.concatenate(attended, axis=0), NN)
+        halves = head_halves(dot(stack(2, p), weight, TN).astype(BF16))
+        weight_ref[p, 3 * rows :] = jnp.concatenate(halves, axis=1)
+        if p == pairs - 1:
+            part = (slice(None), pl.ds(3 * rows, HD))
+            out.append(
+                pltpu.make_async_copy(weight_ref.at[part], weight_hbm.at[part], sent.at[6 + pairs])
+            )
+            out[-1].start()
+        attended.extend(halves)
     half = keep_ref.shape[0]
+    read = dot(own_ref[3, : 2 * half, :], jnp.concatenate(attended, axis=0), NN)
     keep_ref[...] = read[:half]
     send_ref[...] = read[half:]
     wait_all(out)
 
 
 def side_kernel(
-    bias_ref, a2x_ref, b2x_ref, gain_ref, own_hbm, a1_hbm, b1_hbm, w_hbm, weight_hbm, att_ref,
+    a2x_ref, b2x_ref, gain_ref, own_hbm, a1_hbm, b1_hbm, w_hbm, weight_hbm,
     own_ref, a1_ref, b1_ref, w_ref, far_ref, weight_ref, arrived, sent,
 ):
     rows = own_ref.shape[1]
@@ -237,13 +263,14 @@
     for n, (p, side) in enumerate(jobs):
         if n + 1 < len(jobs):
             scores[jobs[n + 1]] = score(*jobs[n + 1])
-        weight = soften(bias_ref, 1 + side, scores[p, side])
-        weight_ref[p, side] = weight[:rows]
+        weight = soften(own_ref, 1 + side, scores[p, side])
+        weight_ref[p, side, :rows] = weight[:rows]
+        halves = head_halves(dot(stack(2, p, side), weight, TN).astype(BF16))
+        weight_ref[p, side, rows:] = jnp.concatenate(halves, axis=1)
         out.append(
             pltpu.make_async_copy(weight_ref.at[p, side], weight_hbm.at[p, side], sent.at[n])
         )
         out[-1].start()
-        att_ref[p, side] = fold_heads(dot(stack(2, p, side), weight, TN)).astype(BF16)
     wait_all(out)
 
 
@@ -278,23 +305,23 @@
 def back_kernel(
     core_ref, resid_a_ref, resid_b_ref, counts_ref, hot_ref, mix_ref, gain_ref, *refs
 ):
-    sources, (keep_ref, send_ref, stat_ref, loss_ref) = refs[:9], refs[9:13]
-    buffers, arrived = refs[13:22], refs[22]
-    own_ref, a1_ref, b1_ref, own_att_ref, side_att_ref, own_w_ref, side_w_ref, w_ref, tokens_ref = buffers
+    sources, (keep_ref, send_ref, stat_ref, loss_ref) = refs[:7], refs[7:11]
+    buffers, arrived = refs[11:18], refs[18]
+    own_ref, a1_ref, b1_ref, own_w_ref, side_w_ref, w_ref, tokens_ref = buffers
     pairs = own_ref.shape[2] // PAIR
-    copies = [
-        pltpu.make_async_copy(sources[n], buffers[n], arrived.at[n]) for n in (0, 1, 2, 3, 4, 7, 8)
-    ]
-    weight_in = [
-        [
-            pltpu.make_async_copy(
-                sources[n].at[p], buffers[n].at[p], arrived.at[9 + 2 * p + n - 5]
-            )
-            for n in (5, 6)
-        ]
-        for p in range(pairs)
-    ]
-    start_all(copies[:5] + [copy for pair in weight_in for copy in pair] + copies[5:])
+    slots = iter(range(arrived.shape[0]))
+
+    def fetch(n, index):
+        return pltpu.make_async_copy(
+            sources[n].at[index], buffers[n].at[index], arrived.at[next(slots)]
+        )
+
+    values_in = [fetch(n, pl.ds(2, 1)) for n in range(3)]
+    weight_in = [[fetch(n, pl.ds(p, 1)) for n in (3, 4)] for p in range(pairs)]
+    rest_in = [fetch(n, pl.ds(0, 2)) for n in range(3)]
+    last_in = [fetch(5, pl.ds(0, 3)), fetch(6, pl.ds(0, tokens_ref.shape[0]))]
+    start_all(values_in + weight_in[0] + rest_in)
+    start_all([copy for pair in weight_in[1:] for copy in pair] + last_in)
     own_rows = own_ref.shape[1]
     residual = jnp.concatenate([resid_a_ref[...], resid_b_ref[...]], axis=0)
     loss_ref[...] = jnp.broadcast_to(
@@ -307,89 +334,88 @@
     def tile_of(p, t):
         return out_grad[pair_cols(p), t * own_rows : (t + 1) * own_rows]
 
-    def open_pair(p):
-        values = jnp.concatenate([r[2, :, pair_cols(p)] for r in stretches], axis=0)
-        grads, changes = [], []
-        for t in range(3):
-            tile = tile_of(p, t)
-            none = jnp.zeros((HD, own_rows), BF16)
-            grads.append(
-                jnp.concatenate(
-                    [
-                        jnp.concatenate([tile[:HD], none], axis=0),
-                        jnp.concatenate([none, tile[HD:]], axis=0),
-                    ],
-                    axis=1,
-                )
-            )
-            changes.append(dot(values if t == 0 else values[:own_rows], grads[t], NN))
-        return grads, changes
-
-    def score_pair(p, changes):
-        scores = []
-        for t in range(3):
-            attended = own_att_ref[p] if t == 0 else side_att_ref[p, t - 1]
-            product = tile_of(p, t).astype(F32) * attended.astype(F32)
-            delta = jnp.concatenate(
-                [
-                    jnp.sum(product[:HD], axis=0, keepdims=True),
-                    jnp.sum(product[HD:], axis=0, keepdims=True),
-                ],
-                axis=1,
-            )
-            weight = own_w_ref[p] if t == 0 else side_w_ref[p, t - 1]
-            scores.append((weight.astype(F32) * (changes[t] - delta)).astype(BF16))
-        return scores
-
-    def close_pair(p, grads, scores):
+    def open_job(p, t):
+        values = jnp.concatenate(
+            [r[2, :, pair_cols(p)] for r in (stretches if t == 0 else stretches[:1])], axis=0
+        )
+        tile = tile_of(p, t)
+        none = jnp.zeros((HD, own_rows), BF16)
+        grad = jnp.concatenate(
+            [
+                jnp.concatenate([tile[:HD], none], axis=0),
+                jnp.concatenate([none, tile[HD:]], axis=0),
+            ],
+            axis=1,
+        )
+        return grad, dot(values, grad, NN)
+
+    def score_job(p, t, change):
+        pack = own_w_ref[p] if t == 0 else side_w_ref[p, t - 1]
+        weight, attended = pack[:-HD], pack[-HD:]
+        tile = tile_of(p, t)
+        flat_tile = jnp.concatenate([tile[:HD], tile[HD:]], axis=1)
+        delta = jnp.sum(flat_tile.astype(F32) * attended.astype(F32), axis=0, keepdims=True)
+        return (weight.astype(F32) * (change - delta)).astype(BF16)
+
+    def query_of(p, score):
         keys = jnp.concatenate([r[1, :, pair_cols(p)] for r in stretches], axis=0)
-        grad_query = fold_heads(dot(keys, scores[0], TN)) * SCALE
-        queries = jnp.concatenate([two_heads(r[0, :, pair_cols(p)]) for r in stretches], axis=0)
-        own_scores = jnp.concatenate([s[:own_rows] for s in scores], axis=1)
-        grad_key = dot(own_scores, queries, NN)
-        own_weights = jnp.concatenate(
-            [own_w_ref[p, :own_rows], side_w_ref[p, 0], side_w_ref[p, 1]], axis=1
-        )
-        grad_value = dot(own_weights, jnp.concatenate(grads, axis=1), NT)
-        return grad_query.T.astype(BF16), grad_key.astype(BF16), grad_value.astype(BF16)
-
-    wait_all(copies[:3])
-    opened = open_pair(0)
-    wait_all(copies[3:5])
+        grad_query = fold_heads(dot(keys, score, TN)) * SCALE
+        return grad_query.T.astype(BF16)
+
+    def close_job(p, t, grad, score):
+        weight = own_w_ref[p, :own_rows] if t == 0 else side_w_ref[p, t - 1, :own_rows]
+        queries = two_heads(stretches[t][0, :, pair_cols(p)])
+        return dot(score[:own_rows], queries, NN), dot(weight, grad, NT)
+
+    wait_all(values_in)
+    jobs = [(p, t) for p in range(pairs) for t in range(3)]
+    opened = open_job(*jobs[0])
     grad_proj = []
-    for p in range(pairs):
-        grads, changes = opened
-        if p + 1 < pairs:
-            opened = open_pair(p + 1)
-        wait_all(weight_in[p])
-        grad_proj.append(close_pair(p, grads, score_pair(p, changes)))
+    for n, (p, t) in enumerate(jobs):
+        grad, change = opened
+        if n + 1 < len(jobs):
+            opened = open_job(*jobs[n + 1])
+        if t == 0:
+            wait_all(weight_in[p])
+        score = score_job(p, t, change)
+        if n == 0:
+            wait_all(rest_in)
+        if t == 0:
+            grad_query = query_of(p, score)
+            grad_key, grad_value = close_job(p, t, grad, score)
+        else:
+            more_key, more_value = close_job(p, t, grad, score)
+            grad_key, grad_value = grad_key + more_key, grad_value + more_value
+        if t == 2:
+            grad_proj.append((grad_query, grad_key.astype(BF16), grad_value.astype(BF16)))
     flat = jnp.concatenate([grad_proj[p][c] for c in range(3) for p in range(pairs)], axis=1)
-    wait_all(copies[5:])
+    wait_all(last_in)
     half = keep_ref.shape[1]
-    inputs = tokens_ref[...].astype(F32)
-    scaled = inputs * gain_ref[...]
     row_sum = jnp.zeros((own_rows, 1), F32)
+    core = core_ref[0]
     parts = []
-    for h in range(2):
-        rows = slice(h * half, (h + 1) * half)
+    for h in (core, 1 - core):
+        rows = pl.ds(pl.multiple_of(h * half, half), half)
         w_part = jnp.concatenate([w_ref[c, rows, :] for c in range(3)], axis=1)
         parts.append(dot(flat, w_part, NT))
-        row_sum += jnp.sum(scaled[:, rows] * parts[h], axis=-1, keepdims=True)
-    first = core_ref[0] == 0
-    keep_ref[...] = jnp.where(first, parts[0], parts[1])
-    send_ref[:, :half] = jnp.where(first, parts[1], parts[0]).astype(BF16)
+        scaled = tokens_ref[:, rows].astype(F32) * gain_ref[:, rows]
+        row_sum += jnp.sum(scaled * parts[-1], axis=-1, keepdims=True)
+    keep_ref[...] = parts[0]
+    send_ref[:, :half] = parts[1].astype(BF16)
     high = row_sum.astype(BF16).astype(F32)
     lane = lax.broadcasted_iota(jnp.int32, (own_rows, BLK), 1)
     send_ref[:, half:] = jnp.where(lane < HD, high, row_sum - high).astype(BF16)
-    stat_ref[...] = jnp.where(lane < HD, row_sum, inverse_root(inputs))
-
-
-def final_kernel(core_ref, keep_ref, got_ref, stat_ref, tokens_ref, gain_ref, out_ref):
+    stat_ref[...] = jnp.broadcast_to(row_sum, stat_ref.shape)
+
+
+def final_kernel(
+    core_ref, keep_ref, got_ref, stat_ref, inverse_ref, tokens_ref, gain_ref, out_ref
+):
     half = keep_ref.shape[1]
     cols = pl.ds(pl.multiple_of(core_ref[0] * half, half), half)
     got_sum = got_ref[:, half : half + 1].astype(F32) + got_ref[:, half + HD : half + HD + 1].astype(F32)
     row_sum = stat_ref[:, :1] + got_sum
-    inverse = stat_ref[:, HD : HD + 1]
+    inverse = inverse_ref[:, :1]
     grad_normed = keep_ref[...] + got_ref[:, :half].astype(F32)
     shrink = row_sum * (inverse * inverse * inverse) * (0.5 / half)
     out_ref[...] = (
@@ -435,8 +461,7 @@
     vmem = pl.BlockSpec(memory_space=pltpu.VMEM)
     whole_tokens = whole_spec((tok_rows, width))
     whole_gain = whole_spec((1, width))
-    bias_spec = whole_spec((3, 3 * per, 2 * tok_rows))
-    bias, hot, mix, own_targets, own = pl.pallas_call(
+    hot, mix, own_targets, own, inverse = pl.pallas_call(
         first_kernel,
         grid=(3,),
         in_specs=[SMEM_SPEC] * 3
@@ -450,18 +475,18 @@
             pl.BlockSpec((1, width, cols), lambda c: (c, 0, 0)),
         ],
         out_specs=[
-            bias_spec,
             whole_spec((panels, 3 * tok_rows)),
             whole_spec((readout, cols)),
             whole_spec((half_read, panels)),
-            pl.BlockSpec((1, tok_rows, cols), lambda c: (c, 0, 0)),
+            whole_spec((4, tok_rows, cols)),
+            whole_spec((tok_rows, BLK)),
         ],
         out_shape=[
-            jax.ShapeDtypeStruct((3, 3 * per, 2 * tok_rows), F32),
             jax.ShapeDtypeStruct((panels, 3 * tok_rows), BF16),
             jax.ShapeDtypeStruct((readout, cols), BF16),
             jax.ShapeDtypeStruct((half_read, panels), F32),
-            jax.ShapeDtypeStruct((3, tok_rows, cols), BF16),
+            jax.ShapeDtypeStruct((4, tok_rows, cols), BF16),
+            jax.ShapeDtypeStruct((tok_rows, BLK), F32),
         ],
         scratch_shapes=[pltpu.VMEM((readout, panels), F32), pltpu.VMEM((tok_rows, width), BF16)],
         compiler_params=params("arbitrary", mib=60),
@@ -471,37 +496,36 @@
         place, key_blocks.T, list_len, flat_ids, w_out, readout_weight, targets, tokens, gain, w_qkv
     )
 
-    a1_tokens, own, mix, own_targets, hot, bias = lax.optimization_barrier(
-        (a1_tokens, own, mix, own_targets, hot, bias)
+    a1_tokens, own, mix, own_targets, hot = lax.optimization_barrier(
+        (a1_tokens, own, mix, own_targets, hot)
     )
     b1_tokens = lax.ppermute(a1_tokens, "head", core_swap)
     a2_tokens, b1_tokens = lax.optimization_barrier((a2_tokens, b1_tokens))
     b2_tokens = lax.ppermute(a2_tokens, "head", core_swap)
     hbm = pl.BlockSpec(memory_space=pl.ANY)
-    a1, b1, own_weight, own_att, read_keep, read_send = pl.pallas_call(
+    a1, b1, own_weight, read_keep, read_send = pl.pallas_call(
         near_kernel,
-        in_specs=[vmem] * 5 + [hbm] * 2,
-        out_specs=[hbm] * 3 + [vmem] * 3,
+        in_specs=[vmem] * 3 + [hbm] * 2,
+        out_specs=[hbm] * 3 + [vmem] * 2,
         out_shape=[
             jax.ShapeDtypeStruct((3, tok_rows, cols), BF16),
             jax.ShapeDtypeStruct((3, tok_rows, cols), BF16),
-            jax.ShapeDtypeStruct((pairs, 3 * tok_rows, 2 * tok_rows), BF16),
-            jax.ShapeDtypeStruct((pairs, PAIR, tok_rows), BF16),
+            jax.ShapeDtypeStruct((pairs, 3 * tok_rows + HD, 2 * tok_rows), BF16),
             jax.ShapeDtypeStruct((half_read, tok_rows), F32),
             jax.ShapeDtypeStruct((half_read, tok_rows), F32),
         ],
         scratch_shapes=[
-            pltpu.VMEM((3, tok_rows, cols), BF16),
+            pltpu.VMEM((4, tok_rows, cols), BF16),
             pltpu.VMEM((3, width, cols), BF16),
             pltpu.VMEM((3, 2 * tok_rows, cols), BF16),
-            pltpu.VMEM((pairs, 3 * tok_rows, 2 * tok_rows), BF16),
+            pltpu.VMEM((pairs, 3 * tok_rows + HD, 2 * tok_rows), BF16),
             pltpu.SemaphoreType.DMA((4,)),
-            pltpu.SemaphoreType.DMA((6 + pairs,)),
+            pltpu.SemaphoreType.DMA((7 + pairs,)),
         ],
         compiler_params=params(),
         cost_estimate=pl.CostEstimate(flops=2**33, bytes_accessed=8 * MIB, transcendentals=0),
         name="near",
-    )(bias, mix, a1_tokens, b1_tokens, gain, own, w_qkv)
+    )(a1_tokens, b1_tokens, gain, own, w_qkv)
 
     read_send, b2_tokens = lax.optimization_barrier((read_send, b2_tokens))
     read_got = lax.ppermute(read_send, "head", core_swap)
@@ -513,27 +537,25 @@
     )(read_keep, read_got)
     all_rows = lax.all_to_all(spread, "seq", 0, 0)
 
-    side_weight, side_att = pl.pallas_call(
+    side_weight = pl.pallas_call(
         side_kernel,
-        in_specs=[vmem] * 4 + [hbm] * 4,
-        out_specs=[hbm, vmem],
-        out_shape=[
-            jax.ShapeDtypeStruct((pairs, 2, tok_rows, 2 * tok_rows), BF16),
-            jax.ShapeDtypeStruct((pairs, 2, PAIR, tok_rows), BF16),
-        ],
-        scratch_shapes=[pltpu.VMEM((3, tok_rows, cols), BF16)] * 3
+        in_specs=[vmem] * 3 + [hbm] * 4,
+        out_specs=hbm,
+        out_shape=jax.ShapeDtypeStruct((pairs, 2, tok_rows + HD, 2 * tok_rows), BF16),
+        scratch_shapes=[pltpu.VMEM((4, tok_rows, cols), BF16)]
+        + [pltpu.VMEM((3, tok_rows, cols), BF16)] * 2
         + [
             pltpu.VMEM((2, width, cols), BF16),
             pltpu.VMEM((2, 2 * tok_rows, cols), BF16),
-            pltpu.VMEM((pairs, 2, tok_rows, 2 * tok_rows), BF16),
+            pltpu.VMEM((pairs, 2, tok_rows + HD, 2 * tok_rows), BF16),
             pltpu.SemaphoreType.DMA((5,)),
             pltpu.SemaphoreType.DMA((2 * pairs,)),
         ],
         compiler_params=params(),
         cost_estimate=pl.CostEstimate(flops=2**33, bytes_accessed=8 * MIB, transcendentals=0),
         name="attend_sides",
-    )(bias, a2_tokens, b2_tokens, gain, own, a1, b1, w_qkv)
-    all_rows, side_weight, side_att = lax.optimization_barrier((all_rows, side_weight, side_att))
+    )(a2_tokens, b2_tokens, gain, own, a1, b1, w_qkv)
+    all_rows, side_weight = lax.optimization_barrier((all_rows, side_weight))
 
     batch = min(seq_count, 8)
     pool_steps = seq_count // batch
@@ -557,7 +579,7 @@
     resid_b = lax.ppermute(resid_a, "head", core_swap)
 
     core_index = place[1:2]
-    sources = (own, a1, b1, own_att, side_att, own_weight, side_weight, w_qkv, tokens)
+    sources = (own, a1, b1, own_weight, side_weight, w_qkv, tokens)
     keep, send, stats, loss = pl.pallas_call(
         back_kernel,
         in_specs=[SMEM_SPEC] + [vmem] * 6 + [hbm] * len(sources),
@@ -569,7 +591,7 @@
             jax.ShapeDtypeStruct((1, BLK), F32),
         ],
         scratch_shapes=[pltpu.VMEM(a.shape, a.dtype) for a in sources]
-        + [pltpu.SemaphoreType.DMA((len(sources) + 2 * pairs,))],
+        + [pltpu.SemaphoreType.DMA((8 + 2 * pairs,))],
         compiler_params=params(),
         name="back",
     )(core_index, resid_a, resid_b, counts, hot, mix, gain, *sources)
@@ -577,11 +599,11 @@
     loss_mean = 0.5 * loss[0, :1] / (all_tokens * readout)
     gradient = pl.pallas_call(
         final_kernel,
-        in_specs=[SMEM_SPEC] + [pl.BlockSpec(memory_space=pltpu.VMEM)] * 5,
+        in_specs=[SMEM_SPEC] + [vmem] * 6,
         out_shape=jax.ShapeDtypeStruct((tok_rows, half_width), F32),
         compiler_params=params(),
         name="final",
-    )(core_index, keep, got, stats, tokens, gain)
+    )(core_index, keep, got, stats, inverse, tokens, gain)
     return (gradient, loss_mean)
 
 

time: 60.9 us -> 59.6 us (0.979)
  local copies, waits for them, and re-layouts: 2.52 us -> 0.04 us
  Pallas kernels: 32.6 us -> 33.7 us
    unnamed x20 -> x16, local copies, waits for them, and re-layouts: 2.52 us -> 0.04 us
    pallas_call x3, Pallas kernels: 16.7 us -> 17.4 us  [the longest x1 8.74 us: local(): pl.pallas_call(side_kernel, in_specs=[vmem] * 3 + [hbm] * 4, out_specs=hb...]
  transfers between devices with their start and end apart: 8 -> 8, of which waited for: 6 -> 6; matrix products, arithmetic and copies ran while one was open for 1% -> 1% of each run, Pallas kernels for 36% -> 38%
where the time goes in v5:
time: 59.6 us; the launch traced here: 59.3 us
  Pallas kernels  33.7 us (57%)
  starting transfers between devices  14.9 us (25%)
  waiting for transfers between devices  8.08 us (14%)
  between operations  1.93 us (3%)
  other arithmetic  0.61 us (1%)
    pallas_call x1, Pallas kernels, local(): pl.pallas_call(back_kernel, in_specs=[SMEM_SPEC] + [vmem] * 6 + [hbm] * l...  8.86 us
    pallas_call x1, Pallas kernels, local(): pl.pallas_call(side_kernel, in_specs=[vmem] * 3 + [hbm] * 4, out_specs=hb...  8.74 us
    pallas_call x1, Pallas kernels, local(): pl.pallas_call(near_kernel, in_specs=[vmem] * 3 + [hbm] * 2, out_specs=[h...  7.62 us
    pallas_call x1, Pallas kernels, local(): pl.pallas_call(first_kernel, grid=(3,), in_specs=[SMEM_SPEC] * 3 + [whole...  6.28 us
    all_to_all x1, starting transfers between devices, local(): all_rows = lax.all_to_all(spread, 'seq', 0, 0)  5.69 us
    ppermute x1, starting transfers between devices, local(): a1_tokens = lax.ppermute(tokens, ('seq', 'head'), shifted(1))  4.91 us
    ppermute x1, starting transfers between devices, local(): a2_tokens = lax.ppermute(tokens, ('seq', 'head'), shifted(2))  3.49 us
    ppermute x1, waiting for transfers between devices, local(): a1_tokens = lax.ppermute(tokens, ('seq', 'head'), shifted(1))  1.95 us
  transfers between devices with their start and end apart: 8, of which 6 were waited for; matrix products, arithmetic and copies ran while one was open for 1% of the time, Pallas kernels for 38%

profile of v5, /device:TPU:0, one launch (start us, length us, event | category | flops | bytes accessed | tf_op | source)
XLA Modules:
  0.0 59.3 jit_solution(13821586932282439159)
XLA Ops:
  0.6 4.9 %collective-permute-start = (bf16[256,1024]{1,0:T(8,128)(2,1)}, bf16[256,1024]{1,0:T(8,128)(2,1)S(1)}, u32[]{:S(2)}, u32[]{:S(2)}) collective-permute-start(bf16[256,1024]{1,0:T(8,128)(2,1)} %tokens_ref.1), channel_id=1, source_target_pairs={{0,2},{2,4},{4,6},{6,8},{8,10},{10,12},{12,14},{3,1},{5,3},{7,5},{... | collective-permute-start | bytes 1572872 | tf_op jit(solution)/shard_map/ppermute | solution.py:455
  5.5 3.5 %collective-permute-start.1 = (bf16[256,1024]{1,0:T(8,128)(2,1)}, bf16[256,1024]{1,0:T(8,128)(2,1)S(1)}, u32[]{:S(2)}, u32[]{:S(2)}) collective-permute-start(bf16[256,1024]{1,0:T(8,128)(2,1)} %tokens_ref.1), channel_id=1, source_target_pairs={{0,4},{2,6},{4,8},{6,10},{8,12},{10,14},{5,1},{7,3},{9,5},{11,7},{... | collective-permute-start | bytes 1572872 | tf_op jit(solution)/shard_map/ppermute | solution.py:456
  9.0 0.6 %pad_add_fusion.place_ref = s32[3]{0:T(128)} fusion(s32[1]{0:T(128)} %constant.14.clone.1, s32[1]{0:T(128)} %bitcast.core_ref, s32[1]{0:T(128)} %bitcast.1), kind=kLoop, calls=%fused_computation | loop fusion | flops 6 | bytes 24 | tf_op jit(solution)/shard_map/stack | solution.py:460
  9.7 6.3 %first.1 = (bf16[256,768]{1,0:T(8,128)(2,1)}, bf16[128,512]{1,0:T(8,128)(2,1)}, f32[64,256]{1,0:T(8,128)}, bf16[4,256,512]{2,1,0:T(8,128)(2,1)}, f32[256,128]{1,0:T(8,128)}) custom-call(s32[3]{0:T(128)} %pad_add_fusion.place_ref, s32[4,16]{1,0:T(4,128)} %bitcast.15, s32[16]{0:T(128)} %lengths_ref.1, s32[1,2048]{1,0:T(1,128)} %bitcast.12, ...), custom_call_target="tpu_custom_call" | custom-call | flops 2147483648 | bytes 6291456 | tf_op jit(solution)/shard_map/first/pallas_call | solution.py:464
  15.9 2.0 %collective-permute-done.a1x_ref = bf16[256,1024]{1,0:T(8,128)(2,1)S(1)} collective-permute-done((bf16[256,1024]{1,0:T(8,128)(2,1)}, bf16[256,1024]{1,0:T(8,128)(2,1)S(1)}, u32[]{:S(2)}, u32[]{:S(2)}) %collective-permute-start) | collective-permute-done | bytes 524320 | tf_op jit(solution)/shard_map/ppermute | solution.py:455
  17.9 0.0 collective-permute-start.2
  17.9 0.0 collective-permute-done.1.a2x_ref
  17.9 1.9 %collective-permute-done.2.b1x_ref = bf16[256,1024]{1,0:T(8,128)(2,1)S(1)} collective-permute-done((bf16[256,1024]{1,0:T(8,128)(2,1)S(1)}, bf16[256,1024]{1,0:T(8,128)(2,1)S(1)}, u32[]{:S(2)}, u32[]{:S(2)}) %collective-permute-start.2) | collective-permute-done | bytes 524320 | tf_op jit(solution)/shard_map/ppermute | solution.py:502
  19.8 0.1 collective-permute-start.3
  19.9 0.0 copy-done.6
  19.9 7.6 %near.1 = (bf16[3,256,512]{2,1,0:T(8,128)(2,1)S(1)}, bf16[3,256,512]{2,1,0:T(8,128)(2,1)}, bf16[4,832,512]{2,1,0:T(8,128)(2,1)}, f32[64,256]{1,0:T(8,128)S(1)}, f32[64,256]{1,0:T(8,128)S(1)}) custom-call(bf16[256,1024]{1,0:T(8,128)(2,1)S(1)} %collective-permute-done.a1x_ref, bf16[256,1024]{1,0:T(8,128)(2,1)S(1)} %collective-permute-done.2.b1x_ref, ...), custom_call_target="tpu_custom_call" | custom-call | flops 8589934592 | bytes 8388608 | tf_op jit(solution)/shard_map/near/pallas_call | solution.py:506
  27.6 0.0 copy-start.1
  27.6 0.0 collective-permute-done.3.b2x_ref
  27.6 0.4 collective-permute-start.4
  28.0 0.9 %collective-permute-done.4.got_ref = f32[64,256]{1,0:T(8,128)S(1)} collective-permute-done((f32[64,256]{1,0:T(8,128)S(1)}, f32[64,256]{1,0:T(8,128)S(1)}, u32[]{:S(2)}, u32[]{:S(2)}) %collective-permute-start.4) | collective-permute-done | bytes 65568 | tf_op jit(solution)/shard_map/ppermute | solution.py:531
  28.9 0.7 %spread.1 = bf16[8,64,256]{2,1,0:T(8,128)(2,1)} custom-call(f32[64,256]{1,0:T(8,128)S(1)} %get-tuple-element.36.keep_ref, f32[64,256]{1,0:T(8,128)S(1)} %collective-permute-done.4.got_ref), custom_call_target="tpu_custom_call" | custom-call | tf_op jit(solution)/shard_map/spread/pallas_call | solution.py:532
  29.7 5.7 %all-to-all-start = ((bf16[8,64,256]{2,1,0:T(8,128)(2,1)}), bf16[8,64,256]{2,1,0:T(8,128)(2,1)S(1)}, u32[]{:S(2)}, u32[]{:S(2)}) async-start(bf16[8,64,256]{2,1,0:T(8,128)(2,1)} %spread.1), calls=%async_computation | async-start | bytes 524288 | tf_op jit(solution)/shard_map/all_to_all | solution.py:538
  35.4 0.0 copy-start.7
  35.4 0.0 copy-start.2
  35.4 8.7 %attend_sides.1.refs_4_ = bf16[4,2,320,512]{3,2,1,0:T(8,128)(2,1)} custom-call(bf16[256,1024]{1,0:T(8,128)(2,1)S(1)} %collective-permute-done.1.a2x_ref, bf16[256,1024]{1,0:T(8,128)(2,1)S(1)} %collective-permute-done.3.b2x_ref, f32[1,1024]{1,0:T(1,128)S(1)} %bitcast.9, bf16[4,256,512]{2,1,0:T(8,128)(2,1)} %get-tuple-element.35.own_hbm.refs_0_, ...), custom_call_target="tpu_custom_call" | custom-call | flops 8589934592 | bytes 8388608 | tf_op jit(solution)/shard_map/attend_sides/pallas_call | solution.py:540
  44.1 0.0 copy-done.1
  44.2 0.6 %all-to-all-done.rows_ref = bf16[8,64,256]{2,1,0:T(8,128)(2,1)S(1)} async-done(((bf16[8,64,256]{2,1,0:T(8,128)(2,1)}), bf16[8,64,256]{2,1,0:T(8,128)(2,1)S(1)}, u32[]{:S(2)}, u32[]{:S(2)}) %all-to-all-start) | async-done | bytes 262176 | tf_op jit(solution)/shard_map/all_to_all | solution.py:538
  44.8 0.0 copy-done.5
  44.8 0.5 pool.1
  45.3 0.1 collective-permute-start.5
  45.3 1.2 %collective-permute-done.5.resid_b_ref = f32[64,256]{1,0:T(8,128)S(1)} collective-permute-done((f32[64,256]{1,0:T(8,128)S(1)}, f32[64,256]{1,0:T(8,128)S(1)}, u32[]{:S(2)}, u32[]{:S(2)}) %collective-permute-start.5) | collective-permute-done | bytes 65568 | tf_op jit(solution)/shard_map/ppermute | solution.py:579
  46.6 0.0 copy-done.2
  46.6 8.9 %back.1 = (f32[256,512]{1,0:T(8,128)S(1)}, bf16[256,640]{1,0:T(8,128)(2,1)S(1)}, f32[256,128]{1,0:T(8,128)S(1)}, f32[1,128]{1,0:T(1,128)S(1)}) custom-call(s32[1]{0:T(128)} %bitcast.core_ref, f32[64,256]{1,0:T(8,128)S(1)} %get-tuple-element.45.resid_a_ref, f32[64,256]{1,0:T(8,128)S(1)} %collective-permute-done.5.resid_b_ref, ...), custom_call_target="tpu_custom_call" | custom-call | tf_op jit(solution)/shard_map/back/pallas_call | solution.py:583
  55.5 0.2 collective-permute-start.6
  55.7 1.4 %collective-permute-done.6.got_ref = bf16[256,640]{1,0:T(8,128)(2,1)S(1)} collective-permute-done((bf16[256,640]{1,0:T(8,128)(2,1)S(1)}, bf16[256,640]{1,0:T(8,128)(2,1)S(1)}, u32[]{:S(2)}, u32[]{:S(2)}) %collective-permute-start.6) | collective-permute-done | bytes 327712 | tf_op jit(solution)/shard_map/ppermute | solution.py:598
  57.2 0.0 copy-done
  57.2 1.0 %final.1 = f32[256,512]{1,0:T(8,128)} custom-call(s32[1]{0:T(128)} %bitcast.core_ref, f32[256,512]{1,0:T(8,128)S(1)} %get-tuple-element.51.keep_ref, bf16[256,640]{1,0:T(8,128)(2,1)S(1)} %collective-permute-done.6.got_ref, f32[256,128]{1,0:T(8,128)S(1)} %get-tuple-element.53.stat_ref, f32[256,128]{1,0:T(8,128)S(1)} %copy-done.4, ...), custom_call_target="tpu_custom_call" | custom-call | tf_op jit(solution)/shard_map/final/pallas_call | solution.py:600
  (8 shorter events, 0.0 us)
Async XLA Ops:
  0.6 17.3 %collective-permute-start = (bf16[256,1024]{1,0:T(8,128)(2,1)}, bf16[256,1024]{1,0:T(8,128)(2,1)S(1)}, u32[]{:S(2)}, u32[]{:S(2)}) collective-permute-start(bf16[256,1024]{1,0:T(8,128)(2,1)} %tokens_ref.1), channel_id=1, source_target_pairs={{0,2},{2,4},{4,6},{6,8},{8,10},{10,12},{12,14},{3,1},{5,3},{7,5},{... | collective-permute-start | bytes 1572872 | tf_op jit(solution)/shard_map/ppermute | solution.py:455
  5.5 12.4 %collective-permute-start.1 = (bf16[256,1024]{1,0:T(8,128)(2,1)}, bf16[256,1024]{1,0:T(8,128)(2,1)S(1)}, u32[]{:S(2)}, u32[]{:S(2)}) collective-permute-start(bf16[256,1024]{1,0:T(8,128)(2,1)} %tokens_ref.1), channel_id=1, source_target_pairs={{0,4},{2,6},{4,8},{6,10},{8,12},{10,14},{5,1},{7,3},{9,5},{11,7},{... | collective-permute-start | bytes 1572872 | tf_op jit(solution)/shard_map/ppermute | solution.py:456
  9.7 10.3 %copy-start.6 = (f32[1024]{0:T(1024)S(1)}, f32[1024]{0:T(1024)}, u32[]{:S(2)}) copy-start(f32[1024]{0:T(1024)} %param.10) | copy-start | bytes 12292
  17.9 1.9 %collective-permute-start.2 = (bf16[256,1024]{1,0:T(8,128)(2,1)S(1)}, bf16[256,1024]{1,0:T(8,128)(2,1)S(1)}, u32[]{:S(2)}, u32[]{:S(2)}) collective-permute-start(bf16[256,1024]{1,0:T(8,128)(2,1)S(1)} %collective-permute-done.a1x_ref), channel_id=1, source_target_pairs={{0,1},{1,0},{2,3},{3,2},{4,5},{5,4},{6,7},{7,6},{8,9},{9,8},{10,11... | collective-permute-start | bytes 1572872 | tf_op jit(solution)/shard_map/ppermute | solution.py:502
  19.8 7.8 %collective-permute-start.3 = (bf16[256,1024]{1,0:T(8,128)(2,1)S(1)}, bf16[256,1024]{1,0:T(8,128)(2,1)S(1)}, u32[]{:S(2)}, u32[]{:S(2)}) collective-permute-start(bf16[256,1024]{1,0:T(8,128)(2,1)S(1)} %collective-permute-done.1.a2x_ref), channel_id=1, source_target_pairs={{0,1},{1,0},{2,3},{3,2},{4,5},{5,4},{6,7},{7,6},{8,9},{9,8},{10,11... | collective-permute-start | bytes 1572872 | tf_op jit(solution)/shard_map/ppermute | solution.py:504
  27.6 16.6 %copy-start.1 = (bf16[3,256,512]{2,1,0:T(8,128)(2,1)}, bf16[3,256,512]{2,1,0:T(8,128)(2,1)S(1)}, u32[]{:S(2)}) copy-start(bf16[3,256,512]{2,1,0:T(8,128)(2,1)S(1)} %get-tuple-element.41.a1_hbm.refs_1_) | copy-start | bytes 2359300
  27.6 1.3 %collective-permute-start.4 = (f32[64,256]{1,0:T(8,128)S(1)}, f32[64,256]{1,0:T(8,128)S(1)}, u32[]{:S(2)}, u32[]{:S(2)}) collective-permute-start(f32[64,256]{1,0:T(8,128)S(1)} %get-tuple-element.39), channel_id=1, source_target_pairs={{0,1},{1,0},{2,3},{3,2},{4,5},{5,4},{6,7},{7,6},{8,9},{9,8},{10,11... | collective-permute-start | bytes 196616 | tf_op jit(solution)/shard_map/ppermute | solution.py:531
  29.7 15.1 %all-to-all-start = ((bf16[8,64,256]{2,1,0:T(8,128)(2,1)}), bf16[8,64,256]{2,1,0:T(8,128)(2,1)S(1)}, u32[]{:S(2)}, u32[]{:S(2)}) async-start(bf16[8,64,256]{2,1,0:T(8,128)(2,1)} %spread.1), calls=%async_computation | async-start | bytes 524288 | tf_op jit(solution)/shard_map/all_to_all | solution.py:538
  35.4 9.4 %copy-start.5 = (f32[64,256]{1,0:T(8,128)S(1)}, f32[64,256]{1,0:T(8,128)}, u32[]{:S(2)}) copy-start(f32[64,256]{1,0:T(8,128)} %get-tuple-element.44.targets_ref) | copy-start | bytes 196612
  35.4 9.4 %copy-start.7 = (s32[2048,1]{0,1:T(1,128)S(1)}, s32[2048,1]{0,1:T(1,128)}, u32[]{:S(2)}) copy-start(s32[2048,1]{0,1:T(1,128)} %param.17) | copy-start | bytes 24580
  35.4 11.2 %copy-start.2 = (bf16[256,768]{1,0:T(8,128)(2,1)S(1)}, bf16[256,768]{1,0:T(8,128)(2,1)}, u32[]{:S(2)}) copy-start(bf16[256,768]{1,0:T(8,128)(2,1)} %get-tuple-element.47.hot_ref) | copy-start | bytes 1179652
  35.4 11.2 %copy-start.3 = (bf16[128,512]{1,0:T(8,128)(2,1)S(1)}, bf16[128,512]{1,0:T(8,128)(2,1)}, u32[]{:S(2)}) copy-start(bf16[128,512]{1,0:T(8,128)(2,1)} %get-tuple-element.48.mix_ref) | copy-start | bytes 393220
  45.3 1.3 %collective-permute-start.5 = (f32[64,256]{1,0:T(8,128)S(1)}, f32[64,256]{1,0:T(8,128)S(1)}, u32[]{:S(2)}, u32[]{:S(2)}) collective-permute-start(f32[64,256]{1,0:T(8,128)S(1)} %get-tuple-element.45.resid_a_ref), channel_id=1, source_target_pairs={{0,1},{1,0},{2,3},{3,2},{4,5},{5,4},{6,7},{7,6},{8,9},{9,8},{10,11... | collective-permute-start | bytes 196616 | tf_op jit(solution)/shard_map/ppermute | solution.py:579
  46.6 10.6 %copy-start = (bf16[256,1024]{1,0:T(8,128)(2,1)S(1)}, bf16[256,1024]{1,0:T(8,128)(2,1)}, u32[]{:S(2)}) copy-start(bf16[256,1024]{1,0:T(8,128)(2,1)} %tokens_ref.1) | copy-start | bytes 1572868
  46.6 10.6 %copy-start.4 = (f32[256,128]{1,0:T(8,128)S(1)}, f32[256,128]{1,0:T(8,128)}, u32[]{:S(2)}) copy-start(f32[256,128]{1,0:T(8,128)} %get-tuple-element.54.inverse_ref) | copy-start | bytes 393220
  55.5 1.7 %collective-permute-start.6 = (bf16[256,640]{1,0:T(8,128)(2,1)S(1)}, bf16[256,640]{1,0:T(8,128)(2,1)S(1)}, u32[]{:S(2)}, u32[]{:S(2)}) collective-permute-start(bf16[256,640]{1,0:T(8,128)(2,1)S(1)} %get-tuple-element.52), channel_id=1, source_target_pairs={{0,1},{1,0},{2,3},{3,2},{4,5},{5,4},{6,7},{7,6},{8,9},{9,8},{10,11... | collective-permute-start | bytes 983048 | tf_op jit(solution)/shard_map/ppermute | solution.py:598

commit v6 on v5

--- a/solution.py
+++ b/solution.py
@@ -141,16 +141,20 @@
 
 def soften(own_ref, stretch, scores):
     count = scores.shape[0] // BLK
-    blocks = [scores[k * BLK : (k + 1) * BLK] for k in range(count)]
     base = own_ref.shape[1] // 2 + 16 * stretch
     bias = own_ref[3, base : base + 16, :].astype(F32)
-    biases = [bias[k : k + 1] for k in range(count)]
-    tops = [jnp.max(b, axis=0, keepdims=True) - d for b, d in zip(blocks, biases)]
-    top = functools.reduce(jnp.maximum, tops)
-    expo = [jnp.exp(b - (top + d)) for b, d in zip(blocks, biases)]
-    total = functools.reduce(jnp.add, [jnp.sum(e, axis=0, keepdims=True) for e in expo])
-    inverse = 1.0 / total
-    return jnp.concatenate([(e * inverse).astype(BF16) for e in expo], axis=0)
+    weights = []
+    for first in range(0, scores.shape[1], BLK):
+        cols = slice(first, first + BLK)
+        blocks = [scores[k * BLK : (k + 1) * BLK, cols] for k in range(count)]
+        biases = [bias[k : k + 1, cols] for k in range(count)]
+        tops = [jnp.max(b, axis=0, keepdims=True) - d for b, d in zip(blocks, biases)]
+        top = functools.reduce(jnp.maximum, tops)
+        expo = [jnp.exp(b - (top + d)) for b, d in zip(blocks, biases)]
+        total = functools.reduce(jnp.add, [jnp.sum(e, axis=0, keepdims=True) for e in expo])
+        inverse = 1.0 / total
+        weights.append(jnp.concatenate([(e * inverse).astype(BF16) for e in expo], axis=0))
+    return jnp.concatenate(weights, axis=1)
 
 
 def start_all(copies):

time: 59.6 us -> 59.5 us (level)
  no operation moved by 1% of the time
where the time goes in v6:
time: 59.5 us; the launch traced here: 59.2 us
  Pallas kernels  33.5 us (56%)
  starting transfers between devices  14.9 us (25%)
  waiting for transfers between devices  8.22 us (14%)
  between operations  1.93 us (3%)
  other arithmetic  0.61 us (1%)
    pallas_call x1, Pallas kernels, local(): pl.pallas_call(back_kernel, in_specs=[SMEM_SPEC] + [vmem] * 6 + [hbm] * l...  8.85 us
    pallas_call x1, Pallas kernels, local(): pl.pallas_call(side_kernel, in_specs=[vmem] * 3 + [hbm] * 4, out_specs=hb...  8.59 us
    pallas_call x1, Pallas kernels, local(): pl.pallas_call(near_kernel, in_specs=[vmem] * 3 + [hbm] * 2, out_specs=[h...  7.57 us
    pallas_call x1, Pallas kernels, local(): pl.pallas_call(first_kernel, grid=(3,), in_specs=[SMEM_SPEC] * 3 + [whole...  6.28 us
    all_to_all x1, starting transfers between devices, local(): all_rows = lax.all_to_all(spread, 'seq', 0, 0)  5.69 us
    ppermute x1, starting transfers between devices, local(): a1_tokens = lax.ppermute(tokens, ('seq', 'head'), shifted(1))  4.91 us
    ppermute x1, starting transfers between devices, local(): a2_tokens = lax.ppermute(tokens, ('seq', 'head'), shifted(2))  3.49 us
    ppermute x1, waiting for transfers between devices, local(): a1_tokens = lax.ppermute(tokens, ('seq', 'head'), shifted(1))  1.95 us
  transfers between devices with their start and end apart: 8, of which 6 were waited for; matrix products, arithmetic and copies ran while one was open for 1% of the time, Pallas kernels for 38%

profile of v6, /device:TPU:0, one launch (start us, length us, event | category | flops | bytes accessed | tf_op | source)
XLA Modules:
  0.0 59.2 jit_solution(1221603967436860157)
XLA Ops:
  0.6 4.9 %collective-permute-start = (bf16[256,1024]{1,0:T(8,128)(2,1)}, bf16[256,1024]{1,0:T(8,128)(2,1)S(1)}, u32[]{:S(2)}, u32[]{:S(2)}) collective-permute-start(bf16[256,1024]{1,0:T(8,128)(2,1)} %tokens_ref.1), channel_id=1, source_target_pairs={{0,2},{2,4},{4,6},{6,8},{8,10},{10,12},{12,14},{3,1},{5,3},{7,5},{... | collective-permute-start | bytes 1572872 | tf_op jit(solution)/shard_map/ppermute | solution.py:459
  5.5 3.5 %collective-permute-start.1 = (bf16[256,1024]{1,0:T(8,128)(2,1)}, bf16[256,1024]{1,0:T(8,128)(2,1)S(1)}, u32[]{:S(2)}, u32[]{:S(2)}) collective-permute-start(bf16[256,1024]{1,0:T(8,128)(2,1)} %tokens_ref.1), channel_id=1, source_target_pairs={{0,4},{2,6},{4,8},{6,10},{8,12},{10,14},{5,1},{7,3},{9,5},{11,7},{... | collective-permute-start | bytes 1572872 | tf_op jit(solution)/shard_map/ppermute | solution.py:460
  9.0 0.6 %pad_add_fusion.place_ref = s32[3]{0:T(128)} fusion(s32[1]{0:T(128)} %constant.14.clone.1, s32[1]{0:T(128)} %bitcast.core_ref, s32[1]{0:T(128)} %bitcast.1), kind=kLoop, calls=%fused_computation | loop fusion | flops 6 | bytes 24 | tf_op jit(solution)/shard_map/stack | solution.py:464
  9.7 6.3 %first.1 = (bf16[256,768]{1,0:T(8,128)(2,1)}, bf16[128,512]{1,0:T(8,128)(2,1)}, f32[64,256]{1,0:T(8,128)}, bf16[4,256,512]{2,1,0:T(8,128)(2,1)}, f32[256,128]{1,0:T(8,128)}) custom-call(s32[3]{0:T(128)} %pad_add_fusion.place_ref, s32[4,16]{1,0:T(4,128)} %bitcast.15, s32[16]{0:T(128)} %lengths_ref.1, s32[1,2048]{1,0:T(1,128)} %bitcast.12, ...), custom_call_target="tpu_custom_call" | custom-call | flops 2147483648 | bytes 6291456 | tf_op jit(solution)/shard_map/first/pallas_call | solution.py:468
  15.9 2.0 %collective-permute-done.a1x_ref = bf16[256,1024]{1,0:T(8,128)(2,1)S(1)} collective-permute-done((bf16[256,1024]{1,0:T(8,128)(2,1)}, bf16[256,1024]{1,0:T(8,128)(2,1)S(1)}, u32[]{:S(2)}, u32[]{:S(2)}) %collective-permute-start) | collective-permute-done | bytes 524320 | tf_op jit(solution)/shard_map/ppermute | solution.py:459
  17.9 0.0 collective-permute-start.2
  17.9 0.0 collective-permute-done.1.a2x_ref
  17.9 1.9 %collective-permute-done.2.b1x_ref = bf16[256,1024]{1,0:T(8,128)(2,1)S(1)} collective-permute-done((bf16[256,1024]{1,0:T(8,128)(2,1)S(1)}, bf16[256,1024]{1,0:T(8,128)(2,1)S(1)}, u32[]{:S(2)}, u32[]{:S(2)}) %collective-permute-start.2) | collective-permute-done | bytes 524320 | tf_op jit(solution)/shard_map/ppermute | solution.py:506
  19.8 0.1 collective-permute-start.3
  19.9 0.0 copy-done.6
  19.9 7.6 %near.1 = (bf16[3,256,512]{2,1,0:T(8,128)(2,1)S(1)}, bf16[3,256,512]{2,1,0:T(8,128)(2,1)}, bf16[4,832,512]{2,1,0:T(8,128)(2,1)}, f32[64,256]{1,0:T(8,128)S(1)}, f32[64,256]{1,0:T(8,128)S(1)}) custom-call(bf16[256,1024]{1,0:T(8,128)(2,1)S(1)} %collective-permute-done.a1x_ref, bf16[256,1024]{1,0:T(8,128)(2,1)S(1)} %collective-permute-done.2.b1x_ref, ...), custom_call_target="tpu_custom_call" | custom-call | flops 8589934592 | bytes 8388608 | tf_op jit(solution)/shard_map/near/pallas_call | solution.py:510
  27.5 0.0 copy-start.1
  27.5 0.0 collective-permute-done.3.b2x_ref
  27.5 0.4 collective-permute-start.4
  28.0 0.9 %collective-permute-done.4.got_ref = f32[64,256]{1,0:T(8,128)S(1)} collective-permute-done((f32[64,256]{1,0:T(8,128)S(1)}, f32[64,256]{1,0:T(8,128)S(1)}, u32[]{:S(2)}, u32[]{:S(2)}) %collective-permute-start.4) | collective-permute-done | bytes 65568 | tf_op jit(solution)/shard_map/ppermute | solution.py:535
  28.9 0.7 %spread.1 = bf16[8,64,256]{2,1,0:T(8,128)(2,1)} custom-call(f32[64,256]{1,0:T(8,128)S(1)} %get-tuple-element.36.keep_ref, f32[64,256]{1,0:T(8,128)S(1)} %collective-permute-done.4.got_ref), custom_call_target="tpu_custom_call" | custom-call | tf_op jit(solution)/shard_map/spread/pallas_call | solution.py:536
  29.6 5.7 %all-to-all-start = ((bf16[8,64,256]{2,1,0:T(8,128)(2,1)}), bf16[8,64,256]{2,1,0:T(8,128)(2,1)S(1)}, u32[]{:S(2)}, u32[]{:S(2)}) async-start(bf16[8,64,256]{2,1,0:T(8,128)(2,1)} %spread.1), calls=%async_computation | async-start | bytes 524288 | tf_op jit(solution)/shard_map/all_to_all | solution.py:542
  35.3 0.0 copy-start.7
  35.3 0.0 copy-start.2
  35.3 0.0 copy-start.3
  35.3 8.6 %attend_sides.1.refs_4_ = bf16[4,2,320,512]{3,2,1,0:T(8,128)(2,1)} custom-call(bf16[256,1024]{1,0:T(8,128)(2,1)S(1)} %collective-permute-done.1.a2x_ref, bf16[256,1024]{1,0:T(8,128)(2,1)S(1)} %collective-permute-done.3.b2x_ref, f32[1,1024]{1,0:T(1,128)S(1)} %bitcast.9, bf16[4,256,512]{2,1,0:T(8,128)(2,1)} %get-tuple-element.35.own_hbm.refs_0_, ...), custom_call_target="tpu_custom_call" | custom-call | flops 8589934592 | bytes 8388608 | tf_op jit(solution)/shard_map/attend_sides/pallas_call | solution.py:544
  43.9 0.0 copy-done.1
  44.0 0.8 %all-to-all-done.rows_ref = bf16[8,64,256]{2,1,0:T(8,128)(2,1)S(1)} async-done(((bf16[8,64,256]{2,1,0:T(8,128)(2,1)}), bf16[8,64,256]{2,1,0:T(8,128)(2,1)S(1)}, u32[]{:S(2)}, u32[]{:S(2)}) %all-to-all-start) | async-done | bytes 262176 | tf_op jit(solution)/shard_map/all_to_all | solution.py:542
  44.7 0.0 copy-done.5
  44.7 0.0 copy-done.7
  44.7 0.5 pool.1
  45.2 0.1 collective-permute-start.5
  45.3 1.2 %collective-permute-done.5.resid_b_ref = f32[64,256]{1,0:T(8,128)S(1)} collective-permute-done((f32[64,256]{1,0:T(8,128)S(1)}, f32[64,256]{1,0:T(8,128)S(1)}, u32[]{:S(2)}, u32[]{:S(2)}) %collective-permute-start.5) | collective-permute-done | bytes 65568 | tf_op jit(solution)/shard_map/ppermute | solution.py:583
  46.5 8.9 %back.1 = (f32[256,512]{1,0:T(8,128)S(1)}, bf16[256,640]{1,0:T(8,128)(2,1)S(1)}, f32[256,128]{1,0:T(8,128)S(1)}, f32[1,128]{1,0:T(1,128)S(1)}) custom-call(s32[1]{0:T(128)} %bitcast.core_ref, f32[64,256]{1,0:T(8,128)S(1)} %get-tuple-element.45.resid_a_ref, f32[64,256]{1,0:T(8,128)S(1)} %collective-permute-done.5.resid_b_ref, ...), custom_call_target="tpu_custom_call" | custom-call | tf_op jit(solution)/shard_map/back/pallas_call | solution.py:587
  55.4 0.2 collective-permute-start.6
  55.7 1.4 %collective-permute-done.6.got_ref = bf16[256,640]{1,0:T(8,128)(2,1)S(1)} collective-permute-done((bf16[256,640]{1,0:T(8,128)(2,1)S(1)}, bf16[256,640]{1,0:T(8,128)(2,1)S(1)}, u32[]{:S(2)}, u32[]{:S(2)}) %collective-permute-start.6) | collective-permute-done | bytes 327712 | tf_op jit(solution)/shard_map/ppermute | solution.py:602
  57.1 1.0 %final.1 = f32[256,512]{1,0:T(8,128)} custom-call(s32[1]{0:T(128)} %bitcast.core_ref, f32[256,512]{1,0:T(8,128)S(1)} %get-tuple-element.51.keep_ref, bf16[256,640]{1,0:T(8,128)(2,1)S(1)} %collective-permute-done.6.got_ref, f32[256,128]{1,0:T(8,128)S(1)} %get-tuple-element.53.stat_ref, f32[256,128]{1,0:T(8,128)S(1)} %copy-done.4, ...), custom_call_target="tpu_custom_call" | custom-call | tf_op jit(solution)/shard_map/final/pallas_call | solution.py:604
  (8 shorter events, 0.0 us)
Async XLA Ops:
  0.6 17.3 %collective-permute-start = (bf16[256,1024]{1,0:T(8,128)(2,1)}, bf16[256,1024]{1,0:T(8,128)(2,1)S(1)}, u32[]{:S(2)}, u32[]{:S(2)}) collective-permute-start(bf16[256,1024]{1,0:T(8,128)(2,1)} %tokens_ref.1), channel_id=1, source_target_pairs={{0,2},{2,4},{4,6},{6,8},{8,10},{10,12},{12,14},{3,1},{5,3},{7,5},{... | collective-permute-start | bytes 1572872 | tf_op jit(solution)/shard_map/ppermute | solution.py:459
  5.5 12.4 %collective-permute-start.1 = (bf16[256,1024]{1,0:T(8,128)(2,1)}, bf16[256,1024]{1,0:T(8,128)(2,1)S(1)}, u32[]{:S(2)}, u32[]{:S(2)}) collective-permute-start(bf16[256,1024]{1,0:T(8,128)(2,1)} %tokens_ref.1), channel_id=1, source_target_pairs={{0,4},{2,6},{4,8},{6,10},{8,12},{10,14},{5,1},{7,3},{9,5},{11,7},{... | collective-permute-start | bytes 1572872 | tf_op jit(solution)/shard_map/ppermute | solution.py:460
  9.7 10.3 %copy-start.6 = (f32[1024]{0:T(1024)S(1)}, f32[1024]{0:T(1024)}, u32[]{:S(2)}) copy-start(f32[1024]{0:T(1024)} %param.10) | copy-start | bytes 12292
  17.9 1.9 %collective-permute-start.2 = (bf16[256,1024]{1,0:T(8,128)(2,1)S(1)}, bf16[256,1024]{1,0:T(8,128)(2,1)S(1)}, u32[]{:S(2)}, u32[]{:S(2)}) collective-permute-start(bf16[256,1024]{1,0:T(8,128)(2,1)S(1)} %collective-permute-done.a1x_ref), channel_id=1, source_target_pairs={{0,1},{1,0},{2,3},{3,2},{4,5},{5,4},{6,7},{7,6},{8,9},{9,8},{10,11... | collective-permute-start | bytes 1572872 | tf_op jit(solution)/shard_map/ppermute | solution.py:506
  19.8 7.7 %collective-permute-start.3 = (bf16[256,1024]{1,0:T(8,128)(2,1)S(1)}, bf16[256,1024]{1,0:T(8,128)(2,1)S(1)}, u32[]{:S(2)}, u32[]{:S(2)}) collective-permute-start(bf16[256,1024]{1,0:T(8,128)(2,1)S(1)} %collective-permute-done.1.a2x_ref), channel_id=1, source_target_pairs={{0,1},{1,0},{2,3},{3,2},{4,5},{5,4},{6,7},{7,6},{8,9},{9,8},{10,11... | collective-permute-start | bytes 1572872 | tf_op jit(solution)/shard_map/ppermute | solution.py:508
  27.5 16.4 %copy-start.1 = (bf16[3,256,512]{2,1,0:T(8,128)(2,1)}, bf16[3,256,512]{2,1,0:T(8,128)(2,1)S(1)}, u32[]{:S(2)}) copy-start(bf16[3,256,512]{2,1,0:T(8,128)(2,1)S(1)} %get-tuple-element.41.a1_hbm.refs_1_) | copy-start | bytes 2359300
  27.5 1.3 %collective-permute-start.4 = (f32[64,256]{1,0:T(8,128)S(1)}, f32[64,256]{1,0:T(8,128)S(1)}, u32[]{:S(2)}, u32[]{:S(2)}) collective-permute-start(f32[64,256]{1,0:T(8,128)S(1)} %get-tuple-element.39), channel_id=1, source_target_pairs={{0,1},{1,0},{2,3},{3,2},{4,5},{5,4},{6,7},{7,6},{8,9},{9,8},{10,11... | collective-permute-start | bytes 196616 | tf_op jit(solution)/shard_map/ppermute | solution.py:535
  29.6 15.1 %all-to-all-start = ((bf16[8,64,256]{2,1,0:T(8,128)(2,1)}), bf16[8,64,256]{2,1,0:T(8,128)(2,1)S(1)}, u32[]{:S(2)}, u32[]{:S(2)}) async-start(bf16[8,64,256]{2,1,0:T(8,128)(2,1)} %spread.1), calls=%async_computation | async-start | bytes 524288 | tf_op jit(solution)/shard_map/all_to_all | solution.py:542
  35.3 9.4 %copy-start.5 = (f32[64,256]{1,0:T(8,128)S(1)}, f32[64,256]{1,0:T(8,128)}, u32[]{:S(2)}) copy-start(f32[64,256]{1,0:T(8,128)} %get-tuple-element.44.targets_ref) | copy-start | bytes 196612
  35.3 9.4 %copy-start.7 = (s32[2048,1]{0,1:T(1,128)S(1)}, s32[2048,1]{0,1:T(1,128)}, u32[]{:S(2)}) copy-start(s32[2048,1]{0,1:T(1,128)} %param.17) | copy-start | bytes 24580
  35.3 11.2 %copy-start.2 = (bf16[256,768]{1,0:T(8,128)(2,1)S(1)}, bf16[256,768]{1,0:T(8,128)(2,1)}, u32[]{:S(2)}) copy-start(bf16[256,768]{1,0:T(8,128)(2,1)} %get-tuple-element.47.hot_ref) | copy-start | bytes 1179652
  35.3 11.2 %copy-start.3 = (bf16[128,512]{1,0:T(8,128)(2,1)S(1)}, bf16[128,512]{1,0:T(8,128)(2,1)}, u32[]{:S(2)}) copy-start(bf16[128,512]{1,0:T(8,128)(2,1)} %get-tuple-element.48.mix_ref) | copy-start | bytes 393220
  45.2 1.3 %collective-permute-start.5 = (f32[64,256]{1,0:T(8,128)S(1)}, f32[64,256]{1,0:T(8,128)S(1)}, u32[]{:S(2)}, u32[]{:S(2)}) collective-permute-start(f32[64,256]{1,0:T(8,128)S(1)} %get-tuple-element.45.resid_a_ref), channel_id=1, source_target_pairs={{0,1},{1,0},{2,3},{3,2},{4,5},{5,4},{6,7},{7,6},{8,9},{9,8},{10,11... | collective-permute-start | bytes 196616 | tf_op jit(solution)/shard_map/ppermute | solution.py:583
  46.5 10.6 %copy-start = (bf16[256,1024]{1,0:T(8,128)(2,1)S(1)}, bf16[256,1024]{1,0:T(8,128)(2,1)}, u32[]{:S(2)}) copy-start(bf16[256,1024]{1,0:T(8,128)(2,1)} %tokens_ref.1) | copy-start | bytes 1572868
  46.5 10.6 %copy-start.4 = (f32[256,128]{1,0:T(8,128)S(1)}, f32[256,128]{1,0:T(8,128)}, u32[]{:S(2)}) copy-start(f32[256,128]{1,0:T(8,128)} %get-tuple-element.54.inverse_ref) | copy-start | bytes 393220
  55.4 1.7 %collective-permute-start.6 = (bf16[256,640]{1,0:T(8,128)(2,1)S(1)}, bf16[256,640]{1,0:T(8,128)(2,1)S(1)}, u32[]{:S(2)}, u32[]{:S(2)}) collective-permute-start(bf16[256,640]{1,0:T(8,128)(2,1)S(1)} %get-tuple-element.52), channel_id=1, source_target_pairs={{0,1},{1,0},{2,3},{3,2},{4,5},{5,4},{6,7},{7,6},{8,9},{9,8},{10,11... | collective-permute-start | bytes 983048 | tf_op jit(solution)/shard_map/ppermute | solution.py:602

commit v7 on v5

--- a/solution.py
+++ b/solution.py
@@ -174,7 +174,7 @@
     order = (1, 2, 0)
     w_in = {c: pltpu.make_async_copy(w_hbm.at[c], w_ref.at[c], arrived.at[c]) for c in order}
     own_in = pltpu.make_async_copy(own_hbm, own_ref, arrived.at[3])
-    start_all([w_in[1], own_in, w_in[2], w_in[0]])
+    start_all([w_in[1], own_in])
     normed = jnp.concatenate([normalise(a1x_ref, gain_ref), normalise(b1x_ref, gain_ref)], axis=0)
     out = []
 
@@ -192,8 +192,10 @@
     def score(p):
         return dot(stack(1, p), two_heads(own_ref[0, :, pair_cols(p)]), NT)
 
+    w_in[2].start()
     project(1)
     own_in.wait()
+    w_in[0].start()
     scores = {0: score(0)}
     project(2)
     attended = []
@@ -321,7 +323,6 @@
     rest_in = [fetch(n, pl.ds(0, 2)) for n in range(3)]
     last_in = [fetch(5, pl.ds(0, 3)), fetch(6, pl.ds(0, tokens_ref.shape[0]))]
     start_all(values_in + weight_in[0] + rest_in)
-    start_all([copy for pair in weight_in[1:] for copy in pair] + last_in)
     own_rows = own_ref.shape[1]
     residual = jnp.concatenate([resid_a_ref[...], resid_b_ref[...]], axis=0)
     loss_ref[...] = jnp.broadcast_to(
@@ -368,6 +369,7 @@
         return dot(score[:own_rows], queries, NN), dot(weight, grad, NT)
 
     wait_all(values_in)
+    start_all([copy for pair in weight_in[1:] for copy in pair] + last_in)
     jobs = [(p, t) for p in range(pairs) for t in range(3)]
     opened = open_job(*jobs[0])
     grad_proj = []

time: 59.6 us -> 59.6 us (level)
  no operation moved by 1% of the time
where the time goes in v7:
time: 59.6 us; the launch traced here: 59.3 us
  Pallas kernels  33.7 us (57%)
  starting transfers between devices  15 us (25%)
  waiting for transfers between devices  8.05 us (14%)
  between operations  1.93 us (3%)
  other arithmetic  0.61 us (1%)
    pallas_call x1, Pallas kernels, local(): pl.pallas_call(back_kernel, in_specs=[SMEM_SPEC] + [vmem] * 6 + [hbm] * l...  8.87 us
    pallas_call x1, Pallas kernels, local(): pl.pallas_call(side_kernel, in_specs=[vmem] * 3 + [hbm] * 4, out_specs=hb...  8.74 us
    pallas_call x1, Pallas kernels, local(): pl.pallas_call(near_kernel, in_specs=[vmem] * 3 + [hbm] * 2, out_specs=[h...  7.62 us
    pallas_call x1, Pallas kernels, local(): pl.pallas_call(first_kernel, grid=(3,), in_specs=[SMEM_SPEC] * 3 + [whole...  6.28 us
    all_to_all x1, starting transfers between devices, local(): all_rows = lax.all_to_all(spread, 'seq', 0, 0)  5.69 us
    ppermute x1, starting transfers between devices, local(): a1_tokens = lax.ppermute(tokens, ('seq', 'head'), shifted(1))  4.91 us
    ppermute x1, starting transfers between devices, local(): a2_tokens = lax.ppermute(tokens, ('seq', 'head'), shifted(2))  3.49 us
    ppermute x1, waiting for transfers between devices, local(): a1_tokens = lax.ppermute(tokens, ('seq', 'head'), shifted(1))  1.95 us
  transfers between devices with their start and end apart: 8, of which 6 were waited for; matrix products, arithmetic and copies ran while one was open for 1% of the time, Pallas kernels for 38%

profile of v7, /device:TPU:0, one launch (start us, length us, event | category | flops | bytes accessed | tf_op | source)
XLA Modules:
  0.0 59.3 jit_solution(13277805131311107822)
XLA Ops:
  0.6 4.9 %collective-permute-start = (bf16[256,1024]{1,0:T(8,128)(2,1)}, bf16[256,1024]{1,0:T(8,128)(2,1)S(1)}, u32[]{:S(2)}, u32[]{:S(2)}) collective-permute-start(bf16[256,1024]{1,0:T(8,128)(2,1)} %tokens_ref.1), channel_id=1, source_target_pairs={{0,2},{2,4},{4,6},{6,8},{8,10},{10,12},{12,14},{3,1},{5,3},{7,5},{... | collective-permute-start | bytes 1572872 | tf_op jit(solution)/shard_map/ppermute | solution.py:457
  5.5 3.5 %collective-permute-start.1 = (bf16[256,1024]{1,0:T(8,128)(2,1)}, bf16[256,1024]{1,0:T(8,128)(2,1)S(1)}, u32[]{:S(2)}, u32[]{:S(2)}) collective-permute-start(bf16[256,1024]{1,0:T(8,128)(2,1)} %tokens_ref.1), channel_id=1, source_target_pairs={{0,4},{2,6},{4,8},{6,10},{8,12},{10,14},{5,1},{7,3},{9,5},{11,7},{... | collective-permute-start | bytes 1572872 | tf_op jit(solution)/shard_map/ppermute | solution.py:458
  9.0 0.6 %pad_add_fusion.place_ref = s32[3]{0:T(128)} fusion(s32[1]{0:T(128)} %constant.14.clone.1, s32[1]{0:T(128)} %bitcast.core_ref, s32[1]{0:T(128)} %bitcast.1), kind=kLoop, calls=%fused_computation | loop fusion | flops 6 | bytes 24 | tf_op jit(solution)/shard_map/stack | solution.py:462
  9.7 6.3 %first.1 = (bf16[256,768]{1,0:T(8,128)(2,1)}, bf16[128,512]{1,0:T(8,128)(2,1)}, f32[64,256]{1,0:T(8,128)}, bf16[4,256,512]{2,1,0:T(8,128)(2,1)}, f32[256,128]{1,0:T(8,128)}) custom-call(s32[3]{0:T(128)} %pad_add_fusion.place_ref, s32[4,16]{1,0:T(4,128)} %bitcast.15, s32[16]{0:T(128)} %lengths_ref.1, s32[1,2048]{1,0:T(1,128)} %bitcast.12, ...), custom_call_target="tpu_custom_call" | custom-call | flops 2147483648 | bytes 6291456 | tf_op jit(solution)/shard_map/first/pallas_call | solution.py:466
  15.9 2.0 %collective-permute-done.a1x_ref = bf16[256,1024]{1,0:T(8,128)(2,1)S(1)} collective-permute-done((bf16[256,1024]{1,0:T(8,128)(2,1)}, bf16[256,1024]{1,0:T(8,128)(2,1)S(1)}, u32[]{:S(2)}, u32[]{:S(2)}) %collective-permute-start) | collective-permute-done | bytes 524320 | tf_op jit(solution)/shard_map/ppermute | solution.py:457
  17.9 0.0 collective-permute-start.2
  17.9 0.0 collective-permute-done.1.a2x_ref
  17.9 1.9 %collective-permute-done.2.b1x_ref = bf16[256,1024]{1,0:T(8,128)(2,1)S(1)} collective-permute-done((bf16[256,1024]{1,0:T(8,128)(2,1)S(1)}, bf16[256,1024]{1,0:T(8,128)(2,1)S(1)}, u32[]{:S(2)}, u32[]{:S(2)}) %collective-permute-start.2) | collective-permute-done | bytes 524320 | tf_op jit(solution)/shard_map/ppermute | solution.py:504
  19.8 0.1 collective-permute-start.3
  19.9 0.0 copy-done.6
  19.9 7.6 %near.1 = (bf16[3,256,512]{2,1,0:T(8,128)(2,1)S(1)}, bf16[3,256,512]{2,1,0:T(8,128)(2,1)}, bf16[4,832,512]{2,1,0:T(8,128)(2,1)}, f32[64,256]{1,0:T(8,128)S(1)}, f32[64,256]{1,0:T(8,128)S(1)}) custom-call(bf16[256,1024]{1,0:T(8,128)(2,1)S(1)} %collective-permute-done.a1x_ref, bf16[256,1024]{1,0:T(8,128)(2,1)S(1)} %collective-permute-done.2.b1x_ref, ...), custom_call_target="tpu_custom_call" | custom-call | flops 8589934592 | bytes 8388608 | tf_op jit(solution)/shard_map/near/pallas_call | solution.py:508
  27.6 0.0 copy-start.1
  27.6 0.0 collective-permute-done.3.b2x_ref
  27.6 0.4 collective-permute-start.4
  28.0 0.9 %collective-permute-done.4.got_ref = f32[64,256]{1,0:T(8,128)S(1)} collective-permute-done((f32[64,256]{1,0:T(8,128)S(1)}, f32[64,256]{1,0:T(8,128)S(1)}, u32[]{:S(2)}, u32[]{:S(2)}) %collective-permute-start.4) | collective-permute-done | bytes 65568 | tf_op jit(solution)/shard_map/ppermute | solution.py:533
  28.9 0.7 %spread.1 = bf16[8,64,256]{2,1,0:T(8,128)(2,1)} custom-call(f32[64,256]{1,0:T(8,128)S(1)} %get-tuple-element.36.keep_ref, f32[64,256]{1,0:T(8,128)S(1)} %collective-permute-done.4.got_ref), custom_call_target="tpu_custom_call" | custom-call | tf_op jit(solution)/shard_map/spread/pallas_call | solution.py:534
  29.7 5.7 %all-to-all-start = ((bf16[8,64,256]{2,1,0:T(8,128)(2,1)}), bf16[8,64,256]{2,1,0:T(8,128)(2,1)S(1)}, u32[]{:S(2)}, u32[]{:S(2)}) async-start(bf16[8,64,256]{2,1,0:T(8,128)(2,1)} %spread.1), calls=%async_computation | async-start | bytes 524288 | tf_op jit(solution)/shard_map/all_to_all | solution.py:540
  35.4 0.0 copy-start.7
  35.4 0.0 copy-start.2
  35.4 0.0 copy-start.3
  35.4 8.7 %attend_sides.1.refs_4_ = bf16[4,2,320,512]{3,2,1,0:T(8,128)(2,1)} custom-call(bf16[256,1024]{1,0:T(8,128)(2,1)S(1)} %collective-permute-done.1.a2x_ref, bf16[256,1024]{1,0:T(8,128)(2,1)S(1)} %collective-permute-done.3.b2x_ref, f32[1,1024]{1,0:T(1,128)S(1)} %bitcast.9, bf16[4,256,512]{2,1,0:T(8,128)(2,1)} %get-tuple-element.35.own_hbm.refs_0_, ...), custom_call_target="tpu_custom_call" | custom-call | flops 8589934592 | bytes 8388608 | tf_op jit(solution)/shard_map/attend_sides/pallas_call | solution.py:542
  44.1 0.0 copy-done.1
  44.2 0.6 %all-to-all-done.rows_ref = bf16[8,64,256]{2,1,0:T(8,128)(2,1)S(1)} async-done(((bf16[8,64,256]{2,1,0:T(8,128)(2,1)}), bf16[8,64,256]{2,1,0:T(8,128)(2,1)S(1)}, u32[]{:S(2)}, u32[]{:S(2)}) %all-to-all-start) | async-done | bytes 262176 | tf_op jit(solution)/shard_map/all_to_all | solution.py:540
  44.8 0.0 copy-done.5
  44.8 0.0 copy-done.7
  44.8 0.5 pool.1
  45.3 0.1 collective-permute-start.5
  45.3 1.2 %collective-permute-done.5.resid_b_ref = f32[64,256]{1,0:T(8,128)S(1)} collective-permute-done((f32[64,256]{1,0:T(8,128)S(1)}, f32[64,256]{1,0:T(8,128)S(1)}, u32[]{:S(2)}, u32[]{:S(2)}) %collective-permute-start.5) | collective-permute-done | bytes 65568 | tf_op jit(solution)/shard_map/ppermute | solution.py:581
  46.6 8.9 %back.1 = (f32[256,512]{1,0:T(8,128)S(1)}, bf16[256,640]{1,0:T(8,128)(2,1)S(1)}, f32[256,128]{1,0:T(8,128)S(1)}, f32[1,128]{1,0:T(1,128)S(1)}) custom-call(s32[1]{0:T(128)} %bitcast.core_ref, f32[64,256]{1,0:T(8,128)S(1)} %get-tuple-element.45.resid_a_ref, f32[64,256]{1,0:T(8,128)S(1)} %collective-permute-done.5.resid_b_ref, ...), custom_call_target="tpu_custom_call" | custom-call | tf_op jit(solution)/shard_map/back/pallas_call | solution.py:585
  55.5 0.2 collective-permute-start.6
  55.8 1.4 %collective-permute-done.6.got_ref = bf16[256,640]{1,0:T(8,128)(2,1)S(1)} collective-permute-done((bf16[256,640]{1,0:T(8,128)(2,1)S(1)}, bf16[256,640]{1,0:T(8,128)(2,1)S(1)}, u32[]{:S(2)}, u32[]{:S(2)}) %collective-permute-start.6) | collective-permute-done | bytes 327712 | tf_op jit(solution)/shard_map/ppermute | solution.py:600
  57.2 1.0 %final.1 = f32[256,512]{1,0:T(8,128)} custom-call(s32[1]{0:T(128)} %bitcast.core_ref, f32[256,512]{1,0:T(8,128)S(1)} %get-tuple-element.51.keep_ref, bf16[256,640]{1,0:T(8,128)(2,1)S(1)} %collective-permute-done.6.got_ref, f32[256,128]{1,0:T(8,128)S(1)} %get-tuple-element.53.stat_ref, f32[256,128]{1,0:T(8,128)S(1)} %copy-done.4, ...), custom_call_target="tpu_custom_call" | custom-call | tf_op jit(solution)/shard_map/final/pallas_call | solution.py:602
  (8 shorter events, 0.0 us)
Async XLA Ops:
  0.6 17.3 %collective-permute-start = (bf16[256,1024]{1,0:T(8,128)(2,1)}, bf16[256,1024]{1,0:T(8,128)(2,1)S(1)}, u32[]{:S(2)}, u32[]{:S(2)}) collective-permute-start(bf16[256,1024]{1,0:T(8,128)(2,1)} %tokens_ref.1), channel_id=1, source_target_pairs={{0,2},{2,4},{4,6},{6,8},{8,10},{10,12},{12,14},{3,1},{5,3},{7,5},{... | collective-permute-start | bytes 1572872 | tf_op jit(solution)/shard_map/ppermute | solution.py:457
  5.5 12.4 %collective-permute-start.1 = (bf16[256,1024]{1,0:T(8,128)(2,1)}, bf16[256,1024]{1,0:T(8,128)(2,1)S(1)}, u32[]{:S(2)}, u32[]{:S(2)}) collective-permute-start(bf16[256,1024]{1,0:T(8,128)(2,1)} %tokens_ref.1), channel_id=1, source_target_pairs={{0,4},{2,6},{4,8},{6,10},{8,12},{10,14},{5,1},{7,3},{9,5},{11,7},{... | collective-permute-start | bytes 1572872 | tf_op jit(solution)/shard_map/ppermute | solution.py:458
  9.7 10.3 %copy-start.6 = (f32[1024]{0:T(1024)S(1)}, f32[1024]{0:T(1024)}, u32[]{:S(2)}) copy-start(f32[1024]{0:T(1024)} %param.10) | copy-start | bytes 12292
  17.9 1.9 %collective-permute-start.2 = (bf16[256,1024]{1,0:T(8,128)(2,1)S(1)}, bf16[256,1024]{1,0:T(8,128)(2,1)S(1)}, u32[]{:S(2)}, u32[]{:S(2)}) collective-permute-start(bf16[256,1024]{1,0:T(8,128)(2,1)S(1)} %collective-permute-done.a1x_ref), channel_id=1, source_target_pairs={{0,1},{1,0},{2,3},{3,2},{4,5},{5,4},{6,7},{7,6},{8,9},{9,8},{10,11... | collective-permute-start | bytes 1572872 | tf_op jit(solution)/shard_map/ppermute | solution.py:504
  19.8 7.8 %collective-permute-start.3 = (bf16[256,1024]{1,0:T(8,128)(2,1)S(1)}, bf16[256,1024]{1,0:T(8,128)(2,1)S(1)}, u32[]{:S(2)}, u32[]{:S(2)}) collective-permute-start(bf16[256,1024]{1,0:T(8,128)(2,1)S(1)} %collective-permute-done.1.a2x_ref), channel_id=1, source_target_pairs={{0,1},{1,0},{2,3},{3,2},{4,5},{5,4},{6,7},{7,6},{8,9},{9,8},{10,11... | collective-permute-start | bytes 1572872 | tf_op jit(solution)/shard_map/ppermute | solution.py:506
  27.6 16.6 %copy-start.1 = (bf16[3,256,512]{2,1,0:T(8,128)(2,1)}, bf16[3,256,512]{2,1,0:T(8,128)(2,1)S(1)}, u32[]{:S(2)}) copy-start(bf16[3,256,512]{2,1,0:T(8,128)(2,1)S(1)} %get-tuple-element.41.a1_hbm.refs_1_) | copy-start | bytes 2359300
  27.6 1.3 %collective-permute-start.4 = (f32[64,256]{1,0:T(8,128)S(1)}, f32[64,256]{1,0:T(8,128)S(1)}, u32[]{:S(2)}, u32[]{:S(2)}) collective-permute-start(f32[64,256]{1,0:T(8,128)S(1)} %get-tuple-element.39), channel_id=1, source_target_pairs={{0,1},{1,0},{2,3},{3,2},{4,5},{5,4},{6,7},{7,6},{8,9},{9,8},{10,11... | collective-permute-start | bytes 196616 | tf_op jit(solution)/shard_map/ppermute | solution.py:533
  29.7 15.1 %all-to-all-start = ((bf16[8,64,256]{2,1,0:T(8,128)(2,1)}), bf16[8,64,256]{2,1,0:T(8,128)(2,1)S(1)}, u32[]{:S(2)}, u32[]{:S(2)}) async-start(bf16[8,64,256]{2,1,0:T(8,128)(2,1)} %spread.1), calls=%async_computation | async-start | bytes 524288 | tf_op jit(solution)/shard_map/all_to_all | solution.py:540
  35.4 9.4 %copy-start.5 = (f32[64,256]{1,0:T(8,128)S(1)}, f32[64,256]{1,0:T(8,128)}, u32[]{:S(2)}) copy-start(f32[64,256]{1,0:T(8,128)} %get-tuple-element.44.targets_ref) | copy-start | bytes 196612
  35.4 9.4 %copy-start.7 = (s32[2048,1]{0,1:T(1,128)S(1)}, s32[2048,1]{0,1:T(1,128)}, u32[]{:S(2)}) copy-start(s32[2048,1]{0,1:T(1,128)} %param.17) | copy-start | bytes 24580
  35.4 11.2 %copy-start.2 = (bf16[256,768]{1,0:T(8,128)(2,1)S(1)}, bf16[256,768]{1,0:T(8,128)(2,1)}, u32[]{:S(2)}) copy-start(bf16[256,768]{1,0:T(8,128)(2,1)} %get-tuple-element.47.hot_ref) | copy-start | bytes 1179652
  35.4 11.2 %copy-start.3 = (bf16[128,512]{1,0:T(8,128)(2,1)S(1)}, bf16[128,512]{1,0:T(8,128)(2,1)}, u32[]{:S(2)}) copy-start(bf16[128,512]{1,0:T(8,128)(2,1)} %get-tuple-element.48.mix_ref) | copy-start | bytes 393220
  45.3 1.3 %collective-permute-start.5 = (f32[64,256]{1,0:T(8,128)S(1)}, f32[64,256]{1,0:T(8,128)S(1)}, u32[]{:S(2)}, u32[]{:S(2)}) collective-permute-start(f32[64,256]{1,0:T(8,128)S(1)} %get-tuple-element.45.resid_a_ref), channel_id=1, source_target_pairs={{0,1},{1,0},{2,3},{3,2},{4,5},{5,4},{6,7},{7,6},{8,9},{9,8},{10,11... | collective-permute-start | bytes 196616 | tf_op jit(solution)/shard_map/ppermute | solution.py:581
  46.6 10.6 %copy-start = (bf16[256,1024]{1,0:T(8,128)(2,1)S(1)}, bf16[256,1024]{1,0:T(8,128)(2,1)}, u32[]{:S(2)}) copy-start(bf16[256,1024]{1,0:T(8,128)(2,1)} %tokens_ref.1) | copy-start | bytes 1572868
  46.6 10.6 %copy-start.4 = (f32[256,128]{1,0:T(8,128)S(1)}, f32[256,128]{1,0:T(8,128)}, u32[]{:S(2)}) copy-start(f32[256,128]{1,0:T(8,128)} %get-tuple-element.54.inverse_ref) | copy-start | bytes 393220
  55.5 1.7 %collective-permute-start.6 = (bf16[256,640]{1,0:T(8,128)(2,1)S(1)}, bf16[256,640]{1,0:T(8,128)(2,1)S(1)}, u32[]{:S(2)}, u32[]{:S(2)}) collective-permute-start(bf16[256,640]{1,0:T(8,128)(2,1)S(1)} %get-tuple-element.52), channel_id=1, source_target_pairs={{0,1},{1,0},{2,3},{3,2},{4,5},{5,4},{6,7},{7,6},{8,9},{9,8},{10,11... | collective-permute-start | bytes 983048 | tf_op jit(solution)/shard_map/ppermute | solution.py:600

commit v8 on v6

--- a/solution.py
+++ b/solution.py
@@ -331,7 +331,12 @@
     loss_ref[...] = jnp.broadcast_to(
         jnp.sum(counts_ref[...] * residual * residual, keepdims=True), loss_ref.shape
     )
-    panel_grad = dot(mix_ref[...].astype(F32), residual, TN, lax.Precision.HIGHEST).astype(BF16)
+    high = residual.astype(BF16)
+    left = residual - high.astype(F32)
+    middle = left.astype(BF16)
+    low = (left - middle.astype(F32)).astype(BF16)
+    terms = jnp.concatenate([low, middle, high], axis=0)
+    panel_grad = dot(jnp.concatenate([mix_ref[...]] * 3, axis=0), terms, TN).astype(BF16)
     out_grad = dot(panel_grad, hot_ref[...], NN).astype(BF16)
     stretches = (own_ref, a1_ref, b1_ref)
 
@@ -406,9 +411,9 @@
         row_sum += jnp.sum(scaled * parts[-1], axis=-1, keepdims=True)
     keep_ref[...] = parts[0]
     send_ref[:, :half] = parts[1].astype(BF16)
-    high = row_sum.astype(BF16).astype(F32)
+    top = row_sum.astype(BF16).astype(F32)
     lane = lax.broadcasted_iota(jnp.int32, (own_rows, BLK), 1)
-    send_ref[:, half:] = jnp.where(lane < HD, high, row_sum - high).astype(BF16)
+    send_ref[:, half:] = jnp.where(lane < HD, top, row_sum - top).astype(BF16)
     stat_ref[...] = jnp.broadcast_to(row_sum, stat_ref.shape)
 
 

time: 59.5 us -> 58.9 us (0.990)
  Pallas kernels: 33.5 us -> 32.9 us
    pallas_call x1, Pallas kernels: 8.85 us -> 8.24 us  [local(): pl.pallas_call(back_kernel, in_specs=[SMEM_SPEC] + [vmem] * 6 + [hbm] * l...]
where the time goes in v8:
time: 58.9 us; the launch traced here: 58.6 us
  Pallas kernels  32.9 us (56%)
  starting transfers between devices  14.9 us (25%)
  waiting for transfers between devices  8.22 us (14%)
  between operations  1.93 us (3%)
  other arithmetic  0.61 us (1%)
    pallas_call x1, Pallas kernels, local(): pl.pallas_call(side_kernel, in_specs=[vmem] * 3 + [hbm] * 4, out_specs=hb...  8.59 us
    pallas_call x1, Pallas kernels, local(): pl.pallas_call(back_kernel, in_specs=[SMEM_SPEC] + [vmem] * 6 + [hbm] * l...  8.24 us
    pallas_call x1, Pallas kernels, local(): pl.pallas_call(near_kernel, in_specs=[vmem] * 3 + [hbm] * 2, out_specs=[h...  7.57 us
    pallas_call x1, Pallas kernels, local(): pl.pallas_call(first_kernel, grid=(3,), in_specs=[SMEM_SPEC] * 3 + [whole...  6.28 us
    all_to_all x1, starting transfers between devices, local(): all_rows = lax.all_to_all(spread, 'seq', 0, 0)  5.69 us
    ppermute x1, starting transfers between devices, local(): a1_tokens = lax.ppermute(tokens, ('seq', 'head'), shifted(1))  4.91 us
    ppermute x1, starting transfers between devices, local(): a2_tokens = lax.ppermute(tokens, ('seq', 'head'), shifted(2))  3.49 us
    ppermute x1, waiting for transfers between devices, local(): a1_tokens = lax.ppermute(tokens, ('seq', 'head'), shifted(1))  1.95 us
  transfers between devices with their start and end apart: 8, of which 6 were waited for; matrix products, arithmetic and copies ran while one was open for 1% of the time, Pallas kernels for 38%

profile of v8, /device:TPU:0, one launch (start us, length us, event | category | flops | bytes accessed | tf_op | source)
XLA Modules:
  0.0 58.6 jit_solution(11896959901468658963)
XLA Ops:
  0.6 4.9 %collective-permute-start = (bf16[256,1024]{1,0:T(8,128)(2,1)}, bf16[256,1024]{1,0:T(8,128)(2,1)S(1)}, u32[]{:S(2)}, u32[]{:S(2)}) collective-permute-start(bf16[256,1024]{1,0:T(8,128)(2,1)} %tokens_ref.1), channel_id=1, source_target_pairs={{0,2},{2,4},{4,6},{6,8},{8,10},{10,12},{12,14},{3,1},{5,3},{7,5},{... | collective-permute-start | bytes 1572872 | tf_op jit(solution)/shard_map/ppermute | solution.py:464
  5.5 3.5 %collective-permute-start.1 = (bf16[256,1024]{1,0:T(8,128)(2,1)}, bf16[256,1024]{1,0:T(8,128)(2,1)S(1)}, u32[]{:S(2)}, u32[]{:S(2)}) collective-permute-start(bf16[256,1024]{1,0:T(8,128)(2,1)} %tokens_ref.1), channel_id=1, source_target_pairs={{0,4},{2,6},{4,8},{6,10},{8,12},{10,14},{5,1},{7,3},{9,5},{11,7},{... | collective-permute-start | bytes 1572872 | tf_op jit(solution)/shard_map/ppermute | solution.py:465
  9.0 0.6 %pad_add_fusion.place_ref = s32[3]{0:T(128)} fusion(s32[1]{0:T(128)} %constant.14.clone.1, s32[1]{0:T(128)} %bitcast.core_ref, s32[1]{0:T(128)} %bitcast.1), kind=kLoop, calls=%fused_computation | loop fusion | flops 6 | bytes 24 | tf_op jit(solution)/shard_map/stack | solution.py:469
  9.7 6.3 %first.1 = (bf16[256,768]{1,0:T(8,128)(2,1)}, bf16[128,512]{1,0:T(8,128)(2,1)}, f32[64,256]{1,0:T(8,128)}, bf16[4,256,512]{2,1,0:T(8,128)(2,1)}, f32[256,128]{1,0:T(8,128)}) custom-call(s32[3]{0:T(128)} %pad_add_fusion.place_ref, s32[4,16]{1,0:T(4,128)} %bitcast.15, s32[16]{0:T(128)} %lengths_ref.1, s32[1,2048]{1,0:T(1,128)} %bitcast.12, ...), custom_call_target="tpu_custom_call" | custom-call | flops 2147483648 | bytes 6291456 | tf_op jit(solution)/shard_map/first/pallas_call | solution.py:473
  15.9 2.0 %collective-permute-done.a1x_ref = bf16[256,1024]{1,0:T(8,128)(2,1)S(1)} collective-permute-done((bf16[256,1024]{1,0:T(8,128)(2,1)}, bf16[256,1024]{1,0:T(8,128)(2,1)S(1)}, u32[]{:S(2)}, u32[]{:S(2)}) %collective-permute-start) | collective-permute-done | bytes 524320 | tf_op jit(solution)/shard_map/ppermute | solution.py:464
  17.9 0.0 collective-permute-start.2
  17.9 0.0 collective-permute-done.1.a2x_ref
  17.9 1.9 %collective-permute-done.2.b1x_ref = bf16[256,1024]{1,0:T(8,128)(2,1)S(1)} collective-permute-done((bf16[256,1024]{1,0:T(8,128)(2,1)S(1)}, bf16[256,1024]{1,0:T(8,128)(2,1)S(1)}, u32[]{:S(2)}, u32[]{:S(2)}) %collective-permute-start.2) | collective-permute-done | bytes 524320 | tf_op jit(solution)/shard_map/ppermute | solution.py:511
  19.8 0.1 collective-permute-start.3
  19.9 0.0 copy-done.6
  19.9 7.6 %near.1 = (bf16[3,256,512]{2,1,0:T(8,128)(2,1)S(1)}, bf16[3,256,512]{2,1,0:T(8,128)(2,1)}, bf16[4,832,512]{2,1,0:T(8,128)(2,1)}, f32[64,256]{1,0:T(8,128)S(1)}, f32[64,256]{1,0:T(8,128)S(1)}) custom-call(bf16[256,1024]{1,0:T(8,128)(2,1)S(1)} %collective-permute-done.a1x_ref, bf16[256,1024]{1,0:T(8,128)(2,1)S(1)} %collective-permute-done.2.b1x_ref, ...), custom_call_target="tpu_custom_call" | custom-call | flops 8589934592 | bytes 8388608 | tf_op jit(solution)/shard_map/near/pallas_call | solution.py:515
  27.5 0.0 copy-start.1
  27.5 0.0 collective-permute-done.3.b2x_ref
  27.5 0.4 collective-permute-start.4
  28.0 0.9 %collective-permute-done.4.got_ref = f32[64,256]{1,0:T(8,128)S(1)} collective-permute-done((f32[64,256]{1,0:T(8,128)S(1)}, f32[64,256]{1,0:T(8,128)S(1)}, u32[]{:S(2)}, u32[]{:S(2)}) %collective-permute-start.4) | collective-permute-done | bytes 65568 | tf_op jit(solution)/shard_map/ppermute | solution.py:540
  28.9 0.7 %spread.1 = bf16[8,64,256]{2,1,0:T(8,128)(2,1)} custom-call(f32[64,256]{1,0:T(8,128)S(1)} %get-tuple-element.36.keep_ref, f32[64,256]{1,0:T(8,128)S(1)} %collective-permute-done.4.got_ref), custom_call_target="tpu_custom_call" | custom-call | tf_op jit(solution)/shard_map/spread/pallas_call | solution.py:541
  29.6 5.7 %all-to-all-start = ((bf16[8,64,256]{2,1,0:T(8,128)(2,1)}), bf16[8,64,256]{2,1,0:T(8,128)(2,1)S(1)}, u32[]{:S(2)}, u32[]{:S(2)}) async-start(bf16[8,64,256]{2,1,0:T(8,128)(2,1)} %spread.1), calls=%async_computation | async-start | bytes 524288 | tf_op jit(solution)/shard_map/all_to_all | solution.py:547
  35.3 0.0 copy-start.7
  35.3 0.0 copy-start.2
  35.3 0.0 copy-start.3
  35.3 8.6 %attend_sides.1.refs_4_ = bf16[4,2,320,512]{3,2,1,0:T(8,128)(2,1)} custom-call(bf16[256,1024]{1,0:T(8,128)(2,1)S(1)} %collective-permute-done.1.a2x_ref, bf16[256,1024]{1,0:T(8,128)(2,1)S(1)} %collective-permute-done.3.b2x_ref, f32[1,1024]{1,0:T(1,128)S(1)} %bitcast.9, bf16[4,256,512]{2,1,0:T(8,128)(2,1)} %get-tuple-element.35.own_hbm.refs_0_, ...), custom_call_target="tpu_custom_call" | custom-call | flops 8589934592 | bytes 8388608 | tf_op jit(solution)/shard_map/attend_sides/pallas_call | solution.py:549
  43.9 0.0 copy-done.1
  44.0 0.8 %all-to-all-done.rows_ref = bf16[8,64,256]{2,1,0:T(8,128)(2,1)S(1)} async-done(((bf16[8,64,256]{2,1,0:T(8,128)(2,1)}), bf16[8,64,256]{2,1,0:T(8,128)(2,1)S(1)}, u32[]{:S(2)}, u32[]{:S(2)}) %all-to-all-start) | async-done | bytes 262176 | tf_op jit(solution)/shard_map/all_to_all | solution.py:547
  44.7 0.5 pool.1
  45.2 0.1 collective-permute-start.5
  45.3 1.2 %collective-permute-done.5.resid_b_ref = f32[64,256]{1,0:T(8,128)S(1)} collective-permute-done((f32[64,256]{1,0:T(8,128)S(1)}, f32[64,256]{1,0:T(8,128)S(1)}, u32[]{:S(2)}, u32[]{:S(2)}) %collective-permute-start.5) | collective-permute-done | bytes 65568 | tf_op jit(solution)/shard_map/ppermute | solution.py:588
  46.5 0.0 copy-done.2
  46.5 8.2 %back.1 = (f32[256,512]{1,0:T(8,128)S(1)}, bf16[256,640]{1,0:T(8,128)(2,1)S(1)}, f32[256,128]{1,0:T(8,128)S(1)}, f32[1,128]{1,0:T(1,128)S(1)}) custom-call(s32[1]{0:T(128)} %bitcast.core_ref, f32[64,256]{1,0:T(8,128)S(1)} %get-tuple-element.45.resid_a_ref, f32[64,256]{1,0:T(8,128)S(1)} %collective-permute-done.5.resid_b_ref, ...), custom_call_target="tpu_custom_call" | custom-call | tf_op jit(solution)/shard_map/back/pallas_call | solution.py:592
  54.8 0.2 collective-permute-start.6
  55.1 1.4 %collective-permute-done.6.got_ref = bf16[256,640]{1,0:T(8,128)(2,1)S(1)} collective-permute-done((bf16[256,640]{1,0:T(8,128)(2,1)S(1)}, bf16[256,640]{1,0:T(8,128)(2,1)S(1)}, u32[]{:S(2)}, u32[]{:S(2)}) %collective-permute-start.6) | collective-permute-done | bytes 327712 | tf_op jit(solution)/shard_map/ppermute | solution.py:607
  56.5 0.0 copy-done
  56.5 1.0 %final.1 = f32[256,512]{1,0:T(8,128)} custom-call(s32[1]{0:T(128)} %bitcast.core_ref, f32[256,512]{1,0:T(8,128)S(1)} %get-tuple-element.51.keep_ref, bf16[256,640]{1,0:T(8,128)(2,1)S(1)} %collective-permute-done.6.got_ref, f32[256,128]{1,0:T(8,128)S(1)} %get-tuple-element.53.stat_ref, f32[256,128]{1,0:T(8,128)S(1)} %copy-done.4, ...), custom_call_target="tpu_custom_call" | custom-call | tf_op jit(solution)/shard_map/final/pallas_call | solution.py:609
  (8 shorter events, 0.0 us)
Async XLA Ops:
  0.6 17.3 %collective-permute-start = (bf16[256,1024]{1,0:T(8,128)(2,1)}, bf16[256,1024]{1,0:T(8,128)(2,1)S(1)}, u32[]{:S(2)}, u32[]{:S(2)}) collective-permute-start(bf16[256,1024]{1,0:T(8,128)(2,1)} %tokens_ref.1), channel_id=1, source_target_pairs={{0,2},{2,4},{4,6},{6,8},{8,10},{10,12},{12,14},{3,1},{5,3},{7,5},{... | collective-permute-start | bytes 1572872 | tf_op jit(solution)/shard_map/ppermute | solution.py:464
  5.5 12.4 %collective-permute-start.1 = (bf16[256,1024]{1,0:T(8,128)(2,1)}, bf16[256,1024]{1,0:T(8,128)(2,1)S(1)}, u32[]{:S(2)}, u32[]{:S(2)}) collective-permute-start(bf16[256,1024]{1,0:T(8,128)(2,1)} %tokens_ref.1), channel_id=1, source_target_pairs={{0,4},{2,6},{4,8},{6,10},{8,12},{10,14},{5,1},{7,3},{9,5},{11,7},{... | collective-permute-start | bytes 1572872 | tf_op jit(solution)/shard_map/ppermute | solution.py:465
  9.7 10.3 %copy-start.6 = (f32[1024]{0:T(1024)S(1)}, f32[1024]{0:T(1024)}, u32[]{:S(2)}) copy-start(f32[1024]{0:T(1024)} %param.10) | copy-start | bytes 12292
  17.9 1.9 %collective-permute-start.2 = (bf16[256,1024]{1,0:T(8,128)(2,1)S(1)}, bf16[256,1024]{1,0:T(8,128)(2,1)S(1)}, u32[]{:S(2)}, u32[]{:S(2)}) collective-permute-start(bf16[256,1024]{1,0:T(8,128)(2,1)S(1)} %collective-permute-done.a1x_ref), channel_id=1, source_target_pairs={{0,1},{1,0},{2,3},{3,2},{4,5},{5,4},{6,7},{7,6},{8,9},{9,8},{10,11... | collective-permute-start | bytes 1572872 | tf_op jit(solution)/shard_map/ppermute | solution.py:511
  19.8 7.7 %collective-permute-start.3 = (bf16[256,1024]{1,0:T(8,128)(2,1)S(1)}, bf16[256,1024]{1,0:T(8,128)(2,1)S(1)}, u32[]{:S(2)}, u32[]{:S(2)}) collective-permute-start(bf16[256,1024]{1,0:T(8,128)(2,1)S(1)} %collective-permute-done.1.a2x_ref), channel_id=1, source_target_pairs={{0,1},{1,0},{2,3},{3,2},{4,5},{5,4},{6,7},{7,6},{8,9},{9,8},{10,11... | collective-permute-start | bytes 1572872 | tf_op jit(solution)/shard_map/ppermute | solution.py:513
  27.5 16.4 %copy-start.1 = (bf16[3,256,512]{2,1,0:T(8,128)(2,1)}, bf16[3,256,512]{2,1,0:T(8,128)(2,1)S(1)}, u32[]{:S(2)}) copy-start(bf16[3,256,512]{2,1,0:T(8,128)(2,1)S(1)} %get-tuple-element.41.a1_hbm.refs_1_) | copy-start | bytes 2359300
  27.5 1.3 %collective-permute-start.4 = (f32[64,256]{1,0:T(8,128)S(1)}, f32[64,256]{1,0:T(8,128)S(1)}, u32[]{:S(2)}, u32[]{:S(2)}) collective-permute-start(f32[64,256]{1,0:T(8,128)S(1)} %get-tuple-element.39), channel_id=1, source_target_pairs={{0,1},{1,0},{2,3},{3,2},{4,5},{5,4},{6,7},{7,6},{8,9},{9,8},{10,11... | collective-permute-start | bytes 196616 | tf_op jit(solution)/shard_map/ppermute | solution.py:540
  29.6 15.1 %all-to-all-start = ((bf16[8,64,256]{2,1,0:T(8,128)(2,1)}), bf16[8,64,256]{2,1,0:T(8,128)(2,1)S(1)}, u32[]{:S(2)}, u32[]{:S(2)}) async-start(bf16[8,64,256]{2,1,0:T(8,128)(2,1)} %spread.1), calls=%async_computation | async-start | bytes 524288 | tf_op jit(solution)/shard_map/all_to_all | solution.py:547
  35.3 9.4 %copy-start.5 = (f32[64,256]{1,0:T(8,128)S(1)}, f32[64,256]{1,0:T(8,128)}, u32[]{:S(2)}) copy-start(f32[64,256]{1,0:T(8,128)} %get-tuple-element.44.targets_ref) | copy-start | bytes 196612
  35.3 9.4 %copy-start.7 = (s32[2048,1]{0,1:T(1,128)S(1)}, s32[2048,1]{0,1:T(1,128)}, u32[]{:S(2)}) copy-start(s32[2048,1]{0,1:T(1,128)} %param.17) | copy-start | bytes 24580
  35.3 11.2 %copy-start.2 = (bf16[256,768]{1,0:T(8,128)(2,1)S(1)}, bf16[256,768]{1,0:T(8,128)(2,1)}, u32[]{:S(2)}) copy-start(bf16[256,768]{1,0:T(8,128)(2,1)} %get-tuple-element.47.hot_ref) | copy-start | bytes 1179652
  35.3 11.2 %copy-start.3 = (bf16[128,512]{1,0:T(8,128)(2,1)S(1)}, bf16[128,512]{1,0:T(8,128)(2,1)}, u32[]{:S(2)}) copy-start(bf16[128,512]{1,0:T(8,128)(2,1)} %get-tuple-element.48.mix_ref) | copy-start | bytes 393220
  45.2 1.3 %collective-permute-start.5 = (f32[64,256]{1,0:T(8,128)S(1)}, f32[64,256]{1,0:T(8,128)S(1)}, u32[]{:S(2)}, u32[]{:S(2)}) collective-permute-start(f32[64,256]{1,0:T(8,128)S(1)} %get-tuple-element.45.resid_a_ref), channel_id=1, source_target_pairs={{0,1},{1,0},{2,3},{3,2},{4,5},{5,4},{6,7},{7,6},{8,9},{9,8},{10,11... | collective-permute-start | bytes 196616 | tf_op jit(solution)/shard_map/ppermute | solution.py:588
  46.5 10.0 %copy-start = (bf16[256,1024]{1,0:T(8,128)(2,1)S(1)}, bf16[256,1024]{1,0:T(8,128)(2,1)}, u32[]{:S(2)}) copy-start(bf16[256,1024]{1,0:T(8,128)(2,1)} %tokens_ref.1) | copy-start | bytes 1572868
  46.5 10.0 %copy-start.4 = (f32[256,128]{1,0:T(8,128)S(1)}, f32[256,128]{1,0:T(8,128)}, u32[]{:S(2)}) copy-start(f32[256,128]{1,0:T(8,128)} %get-tuple-element.54.inverse_ref) | copy-start | bytes 393220
  54.8 1.7 %collective-permute-start.6 = (bf16[256,640]{1,0:T(8,128)(2,1)S(1)}, bf16[256,640]{1,0:T(8,128)(2,1)S(1)}, u32[]{:S(2)}, u32[]{:S(2)}) collective-permute-start(bf16[256,640]{1,0:T(8,128)(2,1)S(1)} %get-tuple-element.52), channel_id=1, source_target_pairs={{0,1},{1,0},{2,3},{3,2},{4,5},{5,4},{6,7},{7,6},{8,9},{9,8},{10,11... | collective-permute-start | bytes 983048 | tf_op jit(solution)/shard_map/ppermute | solution.py:607
